TPU v7x, 32 devices: a whole 2x2x4 slice. The times are simulated.
32 devices in a mesh: seq: 8 (over z, y), tensor: 4 (over x, core).
Axes of the slice: x: 2, y: 2, z: 4, core: 2. Of those that a mesh axis runs over, the one named last changes fastest.
Arguments:
- tokens: bfloat16 [8192, 1280], P('seq'), may hold values from -6 to 6
- cotangent: bfloat16 [8192, 1280], P(('seq', 'tensor')), may hold values from -6 to 6
- lengths: int32 [1, 14], replicated, may hold values from 1 to 2048, as said below
- qkv: float32 [3, 1280, 1280], P(None, 'seq', 'tensor'), may hold values from -0.15625 to 0.15625
- out_proj: float32 [1280, 1280], P('seq', 'tensor'), may hold values from -1 to 1
- mlp: float32 [2, 1280, 1280], P(None, 'seq', 'tensor'), may hold values from -0.15625 to 0.15625
- gains: float32 [2, 1280], replicated, may hold values from 0.5 to 1.5
- query_scale: float32 [80], replicated, may hold values from -1 to 1.5
- row_second: float32 [6, 1280], P(None, 'seq'), as said below
- col_second: float32 [6, 1280], P(None, 'tensor'), as said below
- gain_second: float32 [2, 1280], P(None, 'seq'), may hold values from 819.2 to 16384
- scale_second: float32 [80], replicated, may hold values from 6553.6 to 131072
Outputs:
- result: float32 [8192, 1280], P(('seq', 'tensor'))
- tokens_grad: float32 [8192, 1280], P(('seq', 'tensor'))
- qkv_grad: float32 [3, 1280, 1280], P(None, 'seq', 'tensor')
- out_proj_grad: float32 [1280, 1280], P('seq', 'tensor')
- mlp_grad: float32 [2, 1280, 1280], P(None, 'seq', 'tensor')
- gains_grad: float32 [2, 1280], P(None, 'seq')
- scale_grad: float32 [80], replicated
- qkv_new: float32 [3, 1280, 1280], P(None, 'seq', 'tensor')
- out_proj_new: float32 [1280, 1280], P('seq', 'tensor')
- mlp_new: float32 [2, 1280, 1280], P(None, 'seq', 'tensor')
- gains_new: float32 [2, 1280], P(None, 'seq')
- scale_new: float32 [80], replicated
- row_new: float32 [6, 1280], P(None, 'seq')
- col_new: float32 [6, 1280], P(None, 'tensor')
- update_rms: float32 [6], replicated
- gain_second_new: float32 [2, 1280], P(None, 'seq')
- scale_second_new: float32 [80], replicated
Inputs may be any that keep to these rules, and one draw needn't show every extreme that they name: The row lists the 14 document lengths of the packed sequence in order; they sum to 7680, and the last 512 positions are padding. The first document has exactly 2048 tokens; after it, each block of 1024 tokens holds at least two document ends, none at a multiple of 1024. `row_second`: positive statistics. `col_second`: positive statistics.
All inputs are finite; a program needn't handle non-finite values.
Results may differ from a plain program's by a relative error of at most 0.012.
The roundings to bfloat16 on the way count: a program that leaves them out, or rounds other values in their place, can miss the bound.
Values may be sent and summed in bfloat16 or wider, within the bound.
No kernel may reach another device: no remote copies, remote signals or barrier semaphores. Data moves between devices by JAX's collectives and lax.ppermute only.
A program may use at most 128 MiB of HBM per device.

v0:
```python
import math

import jax
import jax.numpy as jnp
from jax import lax
from jax.sharding import PartitionSpec as P

HD = 80
WINDOW = 1024
QB = 512


EPSILON = 1e-06
LOG_BASE = 1.442695
BETA_TWO = 0.5
STEP_RATE = 0.3
CLIP_LEVEL = 0.1
VECTOR_RATE = 0.3
NEGATIVE = -1e30


def passed_along(shard, axis, by):
    peers = lax.axis_size(axis)
    pairs = [(i, i + by) for i in range(peers) if 0 <= i + by < peers]
    return lax.ppermute(shard, axis, pairs)


def rms_scale(values):
    return values * lax.rsqrt(jnp.mean(values * values, axis=-1, keepdims=True) + EPSILON)


def rms_back(values, normed, grad_h, gain):
    factor = lax.rsqrt(jnp.mean(values * values, axis=-1, keepdims=True) + EPSILON)
    scaled = grad_h * gain
    return factor * (scaled - normed * jnp.mean(scaled * normed, axis=-1, keepdims=True))


def times_trans(left, right):
    return lax.dot_general(
        left, right, (((1,), (1,)), ((), ())), preferred_element_type=jnp.float32
    )


def contract_rows(left, right):
    return lax.dot_general(
        left, right, (((0,), (0,)), ((), ())), preferred_element_type=jnp.float32
    )


def silu_back(pre_act, grad_hidden):
    gate_sig = jax.nn.sigmoid(pre_act)
    return (grad_hidden * gate_sig * (1.0 + pre_act * (1.0 - gate_sig))).astype(jnp.bfloat16)


def label_table(lengths, places, seq_len, doc_count):
    ends = jnp.cumsum(lengths, axis=1)
    sequence = jnp.floor_divide(places, seq_len)
    offset = places - sequence * seq_len
    clipped = jnp.clip(sequence, 0, lengths.shape[0] - 1)
    onehot = (clipped[:, None] == jnp.arange(lengths.shape[0], dtype=jnp.int32)[None, :]).astype(
        jnp.int32
    )
    picked = jnp.sum(onehot[:, :, None] * ends[None, :, :], axis=1)
    docnum = jnp.sum((picked <= offset[:, None]).astype(jnp.int32), axis=1)
    return (sequence * (doc_count + 1) + docnum, (docnum == doc_count).astype(jnp.int32))


def block_scores(queries, key_table, labels, padded, begin, heads_here):
    q_block = lax.dynamic_slice_in_dim(queries, begin, QB, 0).reshape(QB, heads_here, HD)
    k_block = lax.dynamic_slice_in_dim(key_table, begin, QB + WINDOW, 0).reshape(
        QB + WINDOW, heads_here, HD
    )
    q_place = begin + WINDOW + jnp.arange(QB, dtype=jnp.int32)
    k_place = begin + jnp.arange(QB + WINDOW, dtype=jnp.int32)
    q_label = lax.dynamic_slice_in_dim(labels, begin + WINDOW, QB, 0)
    k_label = lax.dynamic_slice_in_dim(labels, begin, QB + WINDOW, 0)
    k_pad = lax.dynamic_slice_in_dim(padded, begin, QB + WINDOW, 0)
    before = k_place[None, :] <= q_place[:, None]
    inside = q_place[:, None] - k_place[None, :] < WINDOW
    same_doc = (q_label[:, None] == k_label[None, :]) & (k_pad[None, :] == 0)
    allowed = before & inside & (same_doc | (q_place[:, None] == k_place[None, :]))
    scores = jnp.einsum("qhd,khd->hqk", q_block, k_block, preferred_element_type=jnp.float32)
    return (jnp.where(allowed[None], scores, NEGATIVE), q_block, k_block)


def shards(
    tokens,
    cotangent,
    lengths,
    qkv,
    out_proj,
    mlp,
    gains,
    query_scale,
    row_second,
    col_second,
    gain_second,
    scale_second,
):
    n_tensor = lax.axis_size("tensor")
    n_seq = lax.axis_size("seq")
    seq_index = lax.axis_index("seq")
    ten_index = lax.axis_index("tensor")
    tok_dev = tokens.shape[0]
    share = cotangent.shape[0]
    width = tokens.shape[1]
    rows_own = qkv.shape[1]
    cols_own = qkv.shape[2]
    heads_here = cols_own // HD
    blocks = tok_dev // QB
    row_first = ten_index * share
    seq_len = tok_dev * n_seq
    doc_count = lengths.shape[1]
    w_qkv, w_out, w_mlp = (
        lax.all_gather(qkv.astype(jnp.bfloat16), "seq", axis=1, tiled=True),
        lax.all_gather(out_proj.astype(jnp.bfloat16), "seq", axis=0, tiled=True),
        lax.all_gather(mlp.astype(jnp.bfloat16), "seq", axis=1, tiled=True),
    )
    x_full = tokens.astype(jnp.float32)
    norm_one = rms_scale(x_full)
    h_one = (norm_one * gains[0]).astype(jnp.bfloat16)
    projected = jnp.einsum("td,kdh->kth", h_one, w_qkv, preferred_element_type=jnp.float32)
    factor = jax.nn.softplus(query_scale) * (LOG_BASE / math.sqrt(HD))
    scale_cols = jnp.tile(factor, heads_here)
    queries = (projected[0] * scale_cols).astype(jnp.bfloat16)
    key_rows = projected[1].astype(jnp.bfloat16)
    value_rows = projected[2].astype(jnp.bfloat16)
    rim_keys, rim_values = passed_along((key_rows, value_rows), "seq", 1)
    key_table = jnp.concatenate([rim_keys, key_rows], axis=0)
    value_table = jnp.concatenate([rim_values, value_rows], axis=0)
    places = seq_index * tok_dev - WINDOW + jnp.arange(WINDOW + tok_dev, dtype=jnp.int32)
    labels, padded = label_table(lengths, places, seq_len, doc_count)
    begins = jnp.arange(blocks, dtype=jnp.int32) * QB

    def forward_block(begin):
        scores, q_block, k_block = block_scores(
            queries, key_table, labels, padded, begin, heads_here
        )
        v_block = lax.dynamic_slice_in_dim(value_table, begin, QB + WINDOW, 0).reshape(
            QB + WINDOW, heads_here, HD
        )
        top_score = jnp.max(scores, axis=-1, keepdims=True)
        weights = jnp.exp(scores - top_score)
        totals = jnp.sum(weights, axis=-1, keepdims=True)
        probs = (weights / totals).astype(jnp.bfloat16)
        mixed = jnp.einsum("hqk,khd->qhd", probs, v_block, preferred_element_type=jnp.float32)
        return (mixed.reshape(QB, cols_own), top_score[..., 0] + jnp.log(totals[..., 0]))

    mixed_blocks, log_totals = lax.map(forward_block, begins)
    context = mixed_blocks.reshape(tok_dev, cols_own).astype(jnp.bfloat16)
    attn = lax.psum_scatter(times_trans(context, w_out), "tensor", scatter_dimension=0, tiled=True)
    x_share = lax.dynamic_slice_in_dim(x_full, row_first, share, 0)
    norm_share = lax.dynamic_slice_in_dim(norm_one, row_first, share, 0)
    mid = x_share + attn
    norm_two = rms_scale(mid)
    h_two = (norm_two * gains[1]).astype(jnp.bfloat16)
    grad_out = cotangent.astype(jnp.float32)
    h_all, grad_all = (
        lax.all_gather(h_two, "tensor", axis=0, tiled=True),
        lax.all_gather(cotangent, "tensor", axis=0, tiled=True),
    )
    pre_act = jnp.dot(h_all, w_mlp[0], preferred_element_type=jnp.float32)
    hidden = jax.nn.silu(pre_act).astype(jnp.bfloat16)
    result = mid + lax.psum_scatter(
        times_trans(hidden, w_mlp[1]).astype(jnp.bfloat16),
        "tensor",
        scatter_dimension=0,
        tiled=True,
    ).astype(jnp.float32)
    grad_pre = silu_back(pre_act, jnp.dot(grad_all, w_mlp[1], preferred_element_type=jnp.float32))
    grad_mlp = jnp.stack([contract_rows(h_all, grad_pre), contract_rows(grad_all, hidden)])
    grad_two = lax.psum_scatter(
        times_trans(grad_pre, w_mlp[0]), "tensor", scatter_dimension=0, tiled=True
    )
    gain_two_grad = jnp.sum(grad_two * norm_two, axis=0)
    grad_mid = grad_out + rms_back(mid, norm_two, grad_two, gains[1])
    grad_all_mid = lax.all_gather(grad_mid.astype(jnp.bfloat16), "tensor", axis=0, tiled=True)
    grad_context = jnp.dot(grad_all_mid, w_out, preferred_element_type=jnp.float32).astype(
        jnp.bfloat16
    )
    grad_w_out = contract_rows(grad_all_mid, context)

    def backward_block(index, carry):
        grad_q, grad_k, grad_v = carry
        begin = index * QB
        scores, q_block, k_block = block_scores(
            queries, key_table, labels, padded, begin, heads_here
        )
        v_block = lax.dynamic_slice_in_dim(value_table, begin, QB + WINDOW, 0).reshape(
            QB + WINDOW, heads_here, HD
        )
        probs = jnp.exp(scores - log_totals[index][..., None])
        g_block = lax.dynamic_slice_in_dim(grad_context, begin, QB, 0).reshape(QB, heads_here, HD)
        grad_probs = jnp.einsum(
            "qhd,khd->hqk", g_block, v_block, preferred_element_type=jnp.float32
        )
        inner = jnp.sum(probs * grad_probs, axis=-1, keepdims=True)
        grad_scores = (probs * (grad_probs - inner)).astype(jnp.bfloat16)
        q_part = jnp.einsum(
            "hqk,khd->qhd", grad_scores, k_block, preferred_element_type=jnp.float32
        ).reshape(QB, cols_own)
        k_part = jnp.einsum(
            "hqk,qhd->khd", grad_scores, q_block, preferred_element_type=jnp.float32
        ).reshape(QB + WINDOW, cols_own)
        v_part = jnp.einsum(
            "hqk,qhd->khd", probs.astype(jnp.bfloat16), g_block, preferred_element_type=jnp.float32
        ).reshape(QB + WINDOW, cols_own)
        grad_q = lax.dynamic_update_slice_in_dim(grad_q, q_part, begin, 0)
        grad_k = lax.dynamic_update_slice_in_dim(
            grad_k, lax.dynamic_slice_in_dim(grad_k, begin, QB + WINDOW, 0) + k_part, begin, 0
        )
        grad_v = lax.dynamic_update_slice_in_dim(
            grad_v, lax.dynamic_slice_in_dim(grad_v, begin, QB + WINDOW, 0) + v_part, begin, 0
        )
        return (grad_q, grad_k, grad_v)

    initial = (
        jnp.zeros((tok_dev, cols_own), jnp.float32),
        jnp.zeros((WINDOW + tok_dev, cols_own), jnp.float32),
        jnp.zeros((WINDOW + tok_dev, cols_own), jnp.float32),
    )
    grad_q, grad_k, grad_v = lax.fori_loop(0, blocks, backward_block, initial)
    back_keys, back_values = passed_along((grad_k[:WINDOW], grad_v[:WINDOW]), "seq", -1)
    own_keys = grad_k[WINDOW:].at[tok_dev - WINDOW :].add(back_keys)
    own_values = grad_v[WINDOW:].at[tok_dev - WINDOW :].add(back_values)
    scale_part = (
        jnp.sum((grad_q * projected[0]).reshape(tok_dev, heads_here, HD), axis=(0, 1))
        * (LOG_BASE / math.sqrt(HD))
        * jax.nn.sigmoid(query_scale)
    )
    grad_proj = jnp.stack(
        [
            (grad_q * scale_cols).astype(jnp.bfloat16),
            own_keys.astype(jnp.bfloat16),
            own_values.astype(jnp.bfloat16),
        ]
    )
    grad_w_qkv = jnp.einsum("td,kth->kdh", h_one, grad_proj, preferred_element_type=jnp.float32)
    grad_one = lax.psum_scatter(
        jnp.einsum("kth,kdh->td", grad_proj, w_qkv, preferred_element_type=jnp.float32),
        "tensor",
        scatter_dimension=0,
        tiled=True,
    )
    gain_one_grad = jnp.sum(grad_one * norm_share, axis=0)
    tokens_grad = grad_mid + rms_back(x_share, norm_share, grad_one, gains[0])
    own_qkv, own_out, own_mlp = (
        lax.psum_scatter(grad_w_qkv, "seq", scatter_dimension=1, tiled=True),
        lax.psum_scatter(grad_w_out, "seq", scatter_dimension=0, tiled=True),
        lax.psum_scatter(grad_mlp, "seq", scatter_dimension=1, tiled=True),
    )
    stacked = jnp.concatenate([own_qkv, own_out[None], own_mlp], axis=0)
    squares = stacked * stacked
    row_begin = seq_index * rows_own
    col_begin = ten_index * cols_own
    total_cols = cols_own * n_tensor
    row_part = lax.dynamic_update_slice_in_dim(
        jnp.zeros((6, width), jnp.float32), jnp.sum(squares, axis=2), row_begin, 1
    )
    col_part = lax.dynamic_update_slice_in_dim(
        jnp.zeros((6, total_cols), jnp.float32), jnp.sum(squares, axis=1), col_begin, 1
    )
    old_total = jnp.where(ten_index == 0, jnp.sum(row_second, axis=1), 0.0)
    gain_part = jnp.stack([gain_one_grad, gain_two_grad])
    row_sums, col_sums, old_sums, gain_grad_full, scale_grad = lax.psum(
        (row_part, col_part, old_total, gain_part, scale_part), ("seq", "tensor")
    )
    row_square = lax.dynamic_slice_in_dim(row_sums, row_begin, rows_own, 1)
    col_square = lax.dynamic_slice_in_dim(col_sums, col_begin, cols_own, 1)
    row_new = BETA_TWO * row_second + (1.0 - BETA_TWO) * row_square / total_cols
    col_new = BETA_TWO * col_second + (1.0 - BETA_TWO) * col_square / width
    row_mean = (
        BETA_TWO * old_sums + (1.0 - BETA_TWO) * jnp.sum(row_sums, axis=1) / total_cols
    ) / width
    update = stacked * lax.rsqrt(
        row_new[:, :, None] * col_new[:, None, :] / row_mean[:, None, None]
    )
    update_square = lax.psum(jnp.sum(update * update, axis=(1, 2)), ("seq", "tensor"))
    update_rms = jnp.sqrt(update_square / (width * total_cols))
    weights_old = jnp.concatenate([qkv, out_proj[None], mlp], axis=0)
    fresh = (
        weights_old - STEP_RATE * update / jnp.maximum(1.0, update_rms / CLIP_LEVEL)[:, None, None]
    )
    gains_grad = lax.dynamic_slice_in_dim(gain_grad_full, row_begin, rows_own, 1)
    gains_own = lax.dynamic_slice_in_dim(gains, row_begin, rows_own, 1)
    gain_second_new = BETA_TWO * gain_second + (1.0 - BETA_TWO) * gains_grad * gains_grad
    gains_new = gains_own - VECTOR_RATE * gains_grad * lax.rsqrt(gain_second_new)
    scale_second_new = BETA_TWO * scale_second + (1.0 - BETA_TWO) * scale_grad * scale_grad
    scale_new = query_scale - VECTOR_RATE * scale_grad * lax.rsqrt(scale_second_new)
    return (
        result,
        tokens_grad,
        own_qkv,
        own_out,
        own_mlp,
        gains_grad,
        scale_grad,
        fresh[:3],
        fresh[3],
        fresh[4:],
        gains_new,
        scale_new,
        row_new,
        col_new,
        update_rms,
        gain_second_new,
        scale_second_new,
    )


def solution(mesh):
    return jax.shard_map(
        shards,
        mesh=mesh,
        in_specs=(
            P("seq", None),
            P(("seq", "tensor"), None),
            P(),
            P(None, "seq", "tensor"),
            P("seq", "tensor"),
            P(None, "seq", "tensor"),
            P(),
            P(),
            P(None, "seq"),
            P(None, "tensor"),
            P(None, "seq"),
            P(),
        ),
        out_specs=(
            P(("seq", "tensor"), None),
            P(("seq", "tensor"), None),
            P(None, "seq", "tensor"),
            P("seq", "tensor"),
            P(None, "seq", "tensor"),
            P(None, "seq"),
            P(),
            P(None, "seq", "tensor"),
            P("seq", "tensor"),
            P(None, "seq", "tensor"),
            P(None, "seq"),
            P(),
            P(None, "seq"),
            P(None, "tensor"),
            P(),
            P(None, "seq"),
            P(),
        ),
        check_vma=False,
    )
```

profile of v0, /device:TPU:0, one launch (start us, length us, event | category | flops | bytes accessed | tf_op | source)
XLA Modules:
  0.0 928.2 jit_solution(11815533637862494307)
XLA Ops:
  14.4 38.2 %all_gather.19 = bf16[1280,320]{1,0:T(8,128)(2,1)} all-gather(bf16[160,320]{1,0:T(8,128)(2,1)S(1)} %convert_element_type.117), channel_id=1, replica_groups=mesh['seq'=8,'tensor'=4] {'seq'}, dimensions={0}, use_global_device_ids=true | all-gather | bytes 921600 | tf_op jit(solution)/shard_map/all_gather | solution.py:116
  52.6 25.2 %all-gather.6.cloned.1.call-done = bf16[3,1280,320]{2,1,0:T(8,128)(2,1)} async-done(((bf16[3,160,320]{2,1,0:T(8,128)(2,1)}), bf16[3,1280,320]{2,1,0:T(8,128)(2,1)}) %all-gather.6.cloned.1.call-update) | async-done | bytes 2457616 | tf_op jit(solution)/shard_map/all_gather | solution.py:115
  77.8 7.4 fusion.36
  88.3 5.1 collective-permute-start.1
  95.9 7.6 collective-permute-done
  103.6 11.6 %collective-permute-done.1 = bf16[1024,320]{0,1:T(8,128)(2,1)} collective-permute-done((bf16[1024,320]{0,1:T(8,128)(2,1)S(1)}, bf16[1024,320]{0,1:T(8,128)(2,1)}, u32[]{:S(2)}, u32[]{:S(2)}) %collective-permute-start.1) | collective-permute-done | bytes 655392 | tf_op jit(solution)/shard_map/ppermute | solution.py:25
  117.4 65.8 %while.37 = (s32[]{:T(128)}, bf16[2,512,320]{1,2,0:T(8,128)(2,1)}, f32[2,4,512]{2,1,0:T(4,128)S(1)}, s32[2]{0:T(128)S(1)}, bf16[2048,320]{0,1:T(8,128)(2,1)S(1)}...) while((s32[]{:T(128)}, bf16[2,512,320]{1,2,0:T(8,128)(2,1)}, ...), condition=%wide.region_6.7_spmd, body=%wide.region_3.6_spmd.sunk | while | flops 1042023936 | bytes 58049892 | solution.py:149
  128.7 6.6 select_reduce_fusion.2
  135.2 7.8 fusion.93
  143.1 6.4 fusion.94
  161.5 6.6 select_reduce_fusion.2
  168.1 7.8 fusion.93
  176.0 6.4 fusion.94
  185.3 3.9 fusion.40
  191.2 4.5 convert_element_type.106
  195.7 47.5 %reduce-scatter.11.cloned.1.call-done = f32[256,1280]{1,0:T(8,128)} async-done(((f32[1024,1280]{1,0:T(8,128)}), f32[256,1280]{1,0:T(8,128)}) %reduce-scatter.11.cloned.1.call-update) | async-done | bytes 1310736 | tf_op jit(solution)/shard_map/reduce_scatter | solution.py:151
  247.6 46.1 %all-gather.10.cloned.1.call-done = bf16[2,1280,320]{2,1,0:T(8,128)(2,1)} async-done(((bf16[2,160,320]{2,1,0:T(8,128)(2,1)}), bf16[2,1280,320]{2,1,0:T(8,128)(2,1)}) %all-gather.10.cloned.1.call-update) | async-done | bytes 1638416 | tf_op jit(solution)/shard_map/all_gather | solution.py:117
  293.7 26.7 %all-gather.8.cloned.1.call-done = bf16[1024,1280]{1,0:T(8,128)(2,1)} async-done(((bf16[256,1280]{1,0:T(8,128)(2,1)}), bf16[1024,1280]{1,0:T(8,128)(2,1)}) %all-gather.8.cloned.1.call-update) | async-done | bytes 2621456 | tf_op jit(solution)/shard_map/all_gather | solution.py:159
  320.5 4.1 fusion.18
  324.6 23.0 %all-gather.12.cloned.1.call-done = bf16[1024,1280]{1,0:T(8,128)(2,1)} async-done(((bf16[256,1280]{1,0:T(8,128)(2,1)}), bf16[1024,1280]{1,0:T(8,128)(2,1)}) %all-gather.12.cloned.1.call-update) | async-done | bytes 2621456 | tf_op jit(solution)/shard_map/all_gather | solution.py:160
  347.6 3.8 fusion.16
  351.4 3.9 fusion.17
  355.4 51.5 %reduce-scatter.15.cloned.1.call-done = f32[256,1280]{1,0:T(8,128)} async-done(((f32[1024,1280]{1,0:T(8,128)}), f32[256,1280]{1,0:T(8,128)}) %reduce-scatter.15.cloned.1.call-update) | async-done | bytes 1310736 | tf_op jit(solution)/shard_map/reduce_scatter | solution.py:172
  417.5 7.6 copy.65
  425.2 11.8 %all-gather.14.cloned.1.call-done = bf16[1024,1280]{1,0:T(8,128)(2,1)} async-done(((bf16[256,1280]{1,0:T(8,128)(2,1)}), bf16[1024,1280]{1,0:T(8,128)(2,1)}) %all-gather.14.cloned.1.call-update) | async-done | bytes 2621456 | tf_op jit(solution)/shard_map/all_gather | solution.py:177
  436.9 4.6 fusion.41
  442.7 3.6 convolution_convert_fusion.1
  451.2 81.9 %while.38 = (s32[]{:T(128)}, f32[1024,320]{0,1:T(8,128)}, f32[2048,320]{0,1:T(8,128)}, f32[2048,320]{0,1:T(8,128)}, bf16[2048,320]{0,1:T(8,128)(2,1)}, /*index=5...) while((s32[]{:T(128)}, f32[1024,320]{0,1:T(8,128)}, ...), condition=%wide.region_15.16_spmd, body=%wide.region_13.15_spmd.sunk | while | flops 2562393600 | bytes 183543216 | solution.py:222
  452.7 6.3 fusion.105
  461.9 11.3 %multiply_reduce_fusion.13 = (f32[4,512]{1,0:T(4,128)S(1)}, f32[4,512,1536]{2,1,0:T(8,128)}) fusion(f32[4,512,1536]{2,1,0:T(8,128)} %fusion.105, f32[4,512]{1,0:T(4,128)S(1)} %dynamic-slice_bitcast_fusion.2, pred[512,1536]{1,0:T(8,128)(4,1)S(1)} %fusion.106, bf16[512,4,80]{0,2,1:T(8,128)(2,1)S(1)} %bitcast.165, bf16[1536,4,80]{0,2,1:T(8,128)(2,1)S(1)} %bitcast.163), kind=kOutput, calls=%fused_computation.18.clone.1 | convolution fusion | flops 515897344 | bytes 27279360 | tf_op jit(solution)/shard_map/while/body/eval_jaxpr/qhd,khd->hqk/dot_general | solution.py:194
  474.7 6.7 multiply_convert_fusion.9
  485.6 3.6 constant_dynamic-update-slice_fusion.9
  493.4 6.3 fusion.105
  502.7 11.3 %multiply_reduce_fusion.13 = (f32[4,512]{1,0:T(4,128)S(1)}, f32[4,512,1536]{2,1,0:T(8,128)}) fusion(f32[4,512,1536]{2,1,0:T(8,128)} %fusion.105, f32[4,512]{1,0:T(4,128)S(1)} %dynamic-slice_bitcast_fusion.2, pred[512,1536]{1,0:T(8,128)(4,1)S(1)} %fusion.106, bf16[512,4,80]{0,2,1:T(8,128)(2,1)S(1)} %bitcast.165, bf16[1536,4,80]{0,2,1:T(8,128)(2,1)S(1)} %bitcast.163), kind=kOutput, calls=%fused_computation.18.clone.1 | convolution fusion | flops 515897344 | bytes 27279360 | tf_op jit(solution)/shard_map/while/body/eval_jaxpr/qhd,khd->hqk/dot_general | solution.py:194
  515.4 6.7 multiply_convert_fusion.9
  539.7 42.6 %collective-permute-done.2 = f32[1024,320]{0,1:T(8,128)S(1)} collective-permute-done((f32[1024,320]{0,1:T(8,128)S(1)}, f32[1024,320]{0,1:T(8,128)S(1)}, u32[]{:S(2)}, u32[]{:S(2)}) %collective-permute-start.2) | collective-permute-done | bytes 1310752 | tf_op jit(solution)/shard_map/ppermute | solution.py:25
  582.6 26.9 %collective-permute-done.3 = f32[1024,320]{0,1:T(8,128)S(1)} collective-permute-done((f32[1024,320]{0,1:T(8,128)S(1)}, f32[1024,320]{0,1:T(8,128)S(1)}, u32[]{:S(2)}, u32[]{:S(2)}) %collective-permute-start.3) | collective-permute-done | bytes 1310752 | tf_op jit(solution)/shard_map/ppermute | solution.py:25
  609.8 4.7 convolution_bitcast_fusion.1
  614.5 9.1 copy.77
  623.6 10.4 %reshape.631 = f32[1280,960]{1,0:T(8,128)} reshape(f32[1280,3,320]{2,1,0:T(4,128)} %bitcast.169) | data formatting | bytes 9830400
  634.1 7.3 convolution_bitcast_fusion
  651.6 4.5 broadcast_multiply_fusion
  658.5 42.2 %reduce-scatter.21.cloned.1.call-done = f32[160,320]{1,0:T(8,128)} async-done(((f32[1280,320]{1,0:T(8,128)}), f32[160,320]{1,0:T(8,128)}) %reduce-scatter.21.cloned.1.call-update) | async-done | bytes 204816
  701.9 104.2 %reduce-scatter.19.cloned.1.call-done = f32[160,960]{1,0:T(8,128)} async-done(((f32[1280,960]{1,0:T(8,128)}), f32[160,960]{1,0:T(8,128)}) %reduce-scatter.19.cloned.1.call-update) | async-done | bytes 614416
  810.0 41.8 %all-reduce.2 = (f32[6,1280]{1,0:T(8,128)S(1)}, f32[6]{0:T(128)S(1)}, f32[6,1280]{1,0:T(8,128)S(1)}) all-reduce(f32[6,1280]{1,0:T(8,128)S(1)} %dynamic_update_slice.50, f32[6]{0:T(128)S(1)} %broadcast_select_fusion, f32[6,1280]{1,0:T(8,128)S(1)} %dynamic_update_slice.51), channel_id=1, replica_groups=mesh['seq'=8,'tensor'=4] {'seq','tensor'}, use_global_device_ids=true, to_apply=%region_28.29 | all-reduce | flops 15366 | bytes 122928 | tf_op jit(solution)/shard_map/psum | solution.py:265
  852.8 7.9 reduce-scatter.17.cloned.1.call-done
  862.7 39.5 %all-reduce.1 = (f32[2,1280]{1,0:T(2,128)S(1)}, f32[80]{0:T(128)S(1)}, f32[6]{0:T(128)S(1)}) all-reduce(f32[2,1280]{1,0:T(2,128)S(1)} %pad_maximum_fusion.7, f32[80]{0:T(128)S(1)} %divide_multiply_fusion, f32[6]{0:T(128)S(1)} %multiply_reduce_fusion.2), channel_id=1, replica_groups=mesh['seq'=8,'tensor'=4] {'seq','tensor'}, use_global_device_ids=true, to_apply=%region_23.24 | all-reduce | flops 2646 | bytes 21168 | tf_op jit(solution)/shard_map/psum | solution.py:265
  917.2 3.9 multiply_add_fusion
  (299 shorter events, 127.0 us)
Async XLA Ops:
  7.2 70.6 %all-gather.6.cloned.1.call-start = ((), (), s32[]{:S(2)}) async-start(), calls=%async_computation.6 | async-start | bytes 3317760 | tf_op jit(solution)/shard_map/all_gather | solution.py:115
  9.2 234.0 %reduce-scatter.11.cloned.1.call-start = ((), (), s32[]{:S(2)}) async-start(), calls=%async_computation.7 | async-start | bytes 6553600 | tf_op jit(solution)/shard_map/reduce_scatter | solution.py:151
  11.9 73.3 %copy-start.32 = (f32[1280]{0:T(1024)}, f32[1280]{0:T(1024)S(1)}, u32[]{:S(2)}) copy-start(f32[1280]{0:T(1024)S(1)} %get-tuple-element.517) | copy-start | bytes 15364
  11.9 397.5 %copy-start.28 = (f32[1280]{0:T(1024)}, f32[1280]{0:T(1024)S(1)}, u32[]{:S(2)}) copy-start(f32[1280]{0:T(1024)S(1)} %get-tuple-element.516) | copy-start | bytes 15364
  14.3 70.9 %copy-start.40 = (f32[1024]{0:T(1024)}, f32[1024]{0:T(1024)S(1)}, u32[]{:S(2)}) copy-start(f32[1024]{0:T(1024)S(1)} %add_rsqrt_fusion) | copy-start | bytes 12292
  85.2 8.2 copy-start.47
  85.3 18.1 %collective-permute-start = (bf16[1024,320]{0,1:T(8,128)(2,1)S(1)}, bf16[1024,320]{0,1:T(8,128)(2,1)S(1)}, u32[]{:S(2)}, u32[]{:S(2)}) collective-permute-start(bf16[1024,320]{0,1:T(8,128)(2,1)S(1)} %get-tuple-element.583), channel_id=1, source_target_pairs={{0,4},{4,8},{8,12},{12,16},{16,20},{20,24},{24,28},{1,5},{5,9},{9,... | collective-permute-start | bytes 1966088 | tf_op jit(solution)/shard_map/ppermute | solution.py:25
  88.3 26.9 %collective-permute-start.1 = (bf16[1024,320]{0,1:T(8,128)(2,1)S(1)}, bf16[1024,320]{0,1:T(8,128)(2,1)}, u32[]{:S(2)}, u32[]{:S(2)}) collective-permute-start(bf16[1024,320]{0,1:T(8,128)(2,1)S(1)} %get-tuple-element.582), channel_id=1, source_target_pairs={{0,4},{4,8},{8,12},{12,16},{16,20},{20,24},{24,28},{1,5},{5,9},{9,... | collective-permute-start | bytes 1966088 | tf_op jit(solution)/shard_map/ppermute | solution.py:25
  135.2 7.8 copy-start.6
  189.2 104.5 %all-gather.10.cloned.1.call-start = ((), (), s32[]{:S(2)}) async-start(), calls=%async_computation.9 | async-start | bytes 2211840 | tf_op jit(solution)/shard_map/all_gather | solution.py:117
  191.0 129.5 %all-gather.8.cloned.1.call-start = ((), (), s32[]{:S(2)}) async-start(), calls=%async_computation.8 | async-start | bytes 3276800 | tf_op jit(solution)/shard_map/all_gather | solution.py:159
  245.8 163.6 %copy-start.4 = (f32[256,1280]{1,0:T(8,128)}, f32[256,1280]{1,0:T(8,128)S(1)}, u32[]{:S(2)}) copy-start(f32[256,1280]{1,0:T(8,128)S(1)} %get-tuple-element.572) | copy-start | bytes 3932164
  245.8 163.6 %copy-start.36 = (f32[256]{0:T(256)}, f32[256]{0:T(256)S(1)}, u32[]{:S(2)}) copy-start(f32[256]{0:T(256)S(1)} %add_rsqrt_fusion.2) | copy-start | bytes 3076
  247.0 100.6 %all-gather.12.cloned.1.call-start = ((), (), s32[]{:S(2)}) async-start(), calls=%async_computation.11 | async-start | bytes 3276800 | tf_op jit(solution)/shard_map/all_gather | solution.py:160
  247.6 159.3 %reduce-scatter.15.cloned.1.call-start = ((), (), s32[]{:S(2)}) async-start(), calls=%async_computation.12 | async-start | bytes 6553600 | tf_op jit(solution)/shard_map/reduce_scatter | solution.py:172
  355.4 54.6 %copy-start.12 = (bf16[256,1280]{1,0:T(8,128)(2,1)S(1)}, bf16[256,1280]{1,0:T(8,128)(2,1)}, u32[]{:S(2)}) copy-start(bf16[256,1280]{1,0:T(8,128)(2,1)} %param.25) | copy-start | bytes 1966084
  355.4 81.6 %all-gather.14.cloned.1.call-start = ((), (), s32[]{:S(2)}) async-start(), calls=%async_computation.13 | async-start | bytes 3276800 | tf_op jit(solution)/shard_map/all_gather | solution.py:177
  411.2 244.8 %all-reduce.5.cloned.1.call-start = ((), (), s32[]{:S(2)}) async-start(), calls=%async_computation.17 | async-start | bytes 7864320
  425.1 11.9 %copy-start.15 = (bf16[2,40,8,512]{3,2,0,1:T(8,128)(2,1)S(1)}, bf16[2,40,8,512]{3,2,0,1:T(8,128)(2,1)}, u32[]{:S(2)}) copy-start(bf16[2,40,8,512]{3,2,0,1:T(8,128)(2,1)} %copy-done.14) | copy-start | bytes 1966084
  425.1 275.7 %reduce-scatter.21.cloned.1.call-start = ((), (), s32[]{:S(2)}) async-start(), calls=%async_computation.16 | async-start | bytes 2211840
  441.6 364.5 %reduce-scatter.19.cloned.1.call-start = ((), (), s32[]{:S(2)}) async-start(), calls=%async_computation.15 | async-start | bytes 5898240
  461.9 11.3 %slice-start = ((s8[12582912]{0:T(1024)(128)(4,1)}), s8[4194304]{0:T(1024)(128)(4,1)S(1)}, s32[]{:S(2)}) async-start(s8[12582912]{0:T(1024)(128)(4,1)} %bitcast.157), calls=%async_computation.18 | async-start | bytes 8388608 | tf_op jit(solution)/shard_map/while
  461.9 11.3 %slice-start.1 = ((s8[12582912]{0:T(1024)(128)(4,1)}), s8[4194304]{0:T(1024)(128)(4,1)S(1)}, s32[]{:S(2)}) async-start(s8[12582912]{0:T(1024)(128)(4,1)} %bitcast.157), calls=%async_computation.19 | async-start | bytes 8388608 | tf_op jit(solution)/shard_map/while
  461.9 12.7 %slice-start.2 = ((s8[12582912]{0:T(1024)(128)(4,1)}), s8[4194304]{0:T(1024)(128)(4,1)S(1)}, s32[]{:S(2)}) async-start(s8[12582912]{0:T(1024)(128)(4,1)} %bitcast.157), calls=%async_computation.20 | async-start | bytes 8388608 | tf_op jit(solution)/shard_map/while
  502.6 11.3 %slice-start = ((s8[12582912]{0:T(1024)(128)(4,1)}), s8[4194304]{0:T(1024)(128)(4,1)S(1)}, s32[]{:S(2)}) async-start(s8[12582912]{0:T(1024)(128)(4,1)} %bitcast.157), calls=%async_computation.18 | async-start | bytes 8388608 | tf_op jit(solution)/shard_map/while
  502.6 11.3 %slice-start.1 = ((s8[12582912]{0:T(1024)(128)(4,1)}), s8[4194304]{0:T(1024)(128)(4,1)S(1)}, s32[]{:S(2)}) async-start(s8[12582912]{0:T(1024)(128)(4,1)} %bitcast.157), calls=%async_computation.19 | async-start | bytes 8388608 | tf_op jit(solution)/shard_map/while
  502.6 12.8 %slice-start.2 = ((s8[12582912]{0:T(1024)(128)(4,1)}), s8[4194304]{0:T(1024)(128)(4,1)S(1)}, s32[]{:S(2)}) async-start(s8[12582912]{0:T(1024)(128)(4,1)} %bitcast.157), calls=%async_computation.20 | async-start | bytes 8388608 | tf_op jit(solution)/shard_map/while
  534.7 47.6 %collective-permute-start.2 = (f32[1024,320]{0,1:T(8,128)S(1)}, f32[1024,320]{0,1:T(8,128)S(1)}, u32[]{:S(2)}, u32[]{:S(2)}) collective-permute-start(f32[1024,320]{0,1:T(8,128)S(1)} %slice.85), channel_id=1, source_target_pairs={{4,0},{8,4},{12,8},{16,12},{20,16},{24,20},{28,24},{5,1},{9,5},{13... | collective-permute-start | bytes 3932168 | tf_op jit(solution)/shard_map/ppermute | solution.py:25
  536.1 46.2 %copy-start.2 = (f32[2048,320]{0,1:T(8,128)S(1)}, f32[2048,320]{0,1:T(8,128)}, u32[]{:S(2)}) copy-start(f32[2048,320]{0,1:T(8,128)} %get-tuple-element.440) | copy-start | bytes 7864324
  536.1 73.4 %collective-permute-start.3 = (f32[1024,320]{0,1:T(8,128)S(1)}, f32[1024,320]{0,1:T(8,128)S(1)}, u32[]{:S(2)}, u32[]{:S(2)}) collective-permute-start(f32[1024,320]{0,1:T(8,128)S(1)} %slice.87), channel_id=1, source_target_pairs={{4,0},{8,4},{12,8},{16,12},{20,16},{24,20},{28,24},{5,1},{9,5},{13... | collective-permute-start | bytes 3932168 | tf_op jit(solution)/shard_map/ppermute | solution.py:25
  582.6 27.2 %copy-start.7 = (bf16[1024,1280]{1,0:T(8,128)(2,1)S(1)}, bf16[1024,1280]{1,0:T(8,128)(2,1)}, u32[]{:S(2)}) copy-start(bf16[1024,1280]{1,0:T(8,128)(2,1)} %param.24) | copy-start | bytes 7864324
  582.6 27.2 %copy-start.33 = (f32[1280]{0:T(1024)S(1)}, f32[1280]{0:T(1024)}, u32[]{:S(2)}) copy-start(f32[1280]{0:T(1024)} %copy-done.32) | copy-start | bytes 15364
  582.6 27.2 %copy-start.41 = (f32[1024]{0:T(1024)S(1)}, f32[1024]{0:T(1024)}, u32[]{:S(2)}) copy-start(f32[1024]{0:T(1024)} %copy-done.40) | copy-start | bytes 12292
  634.1 226.6 %reduce-scatter.17.cloned.1.call-start = ((), (), s32[]{:S(2)}) async-start(), calls=%async_computation.14 | async-start | bytes 6553600 | tf_op jit(solution)/shard_map/reduce_scatter | solution.py:239
  641.4 275.7 %reduce-scatter.13.cloned.1.call-start = ((), (), s32[]{:S(2)}) async-start(), calls=%async_computation.10 | async-start | bytes 3276800 | tf_op jit(solution)/shard_map/reduce_scatter | solution.py:164
  808.0 44.0 %copy-start.42 = (f32[6,320]{1,0:T(8,128)S(1)}, f32[6,320]{1,0:T(8,128)}, u32[]{:S(2)}) copy-start(f32[6,320]{1,0:T(8,128)} %param.33) | copy-start | bytes 23044
  852.0 50.7 %copy-start.31 = (f32[6,160]{1,0:T(8,128)}, f32[6,160]{1,0:T(8,128)S(1)}, u32[]{:S(2)}) copy-start(f32[6,160]{1,0:T(8,128)S(1)} %multiply_add_fusion.3) | copy-start | bytes 11524
  852.1 50.7 %copy-start.30 = (f32[6,320]{1,0:T(8,128)}, f32[6,320]{1,0:T(8,128)S(1)}, u32[]{:S(2)}) copy-start(f32[6,320]{1,0:T(8,128)S(1)} %multiply_add_fusion.2) | copy-start | bytes 23044
  852.1 50.7 %copy-start.18 = (f32[3,160,320]{1,2,0:T(8,128)S(1)}, f32[3,160,320]{1,2,0:T(8,128)}, u32[]{:S(2)}) copy-start(f32[3,160,320]{1,2,0:T(8,128)} %copy.67) | copy-start | bytes 1843204
  902.2 13.0 %copy-start.50 = (f32[80]{0:T(128)}, f32[80]{0:T(128)S(1)}, u32[]{:S(2)}) copy-start(f32[80]{0:T(128)S(1)} %get-tuple-element.559) | copy-start | bytes 964
  907.0 8.3 copy-start.49
  907.0 8.8 copy-start.46
  907.0 10.1 %copy-start.5 = (f32[256,1280]{1,0:T(8,128)S(1)}, f32[256,1280]{1,0:T(8,128)}, u32[]{:S(2)}) copy-start(f32[256,1280]{1,0:T(8,128)} %copy-done.4) | copy-start | bytes 3932164
  907.0 10.1 %copy-start.10 = (f32[256,1280]{1,0:T(8,128)S(1)}, f32[256,1280]{1,0:T(8,128)}, u32[]{:S(2)}) copy-start(f32[256,1280]{1,0:T(8,128)} %reduce-scatter.15.cloned.1.call-done) | copy-start | bytes 3932164
  907.0 10.1 %copy-start.13 = (bf16[256,1280]{1,0:T(8,128)(2,1)S(1)}, bf16[256,1280]{1,0:T(8,128)(2,1)}, u32[]{:S(2)}) copy-start(bf16[256,1280]{1,0:T(8,128)(2,1)} %param.25) | copy-start | bytes 1966084
  907.1 10.1 %copy-start.29 = (f32[1280]{0:T(1024)S(1)}, f32[1280]{0:T(1024)}, u32[]{:S(2)}) copy-start(f32[1280]{0:T(1024)} %copy-done.28) | copy-start | bytes 15364
  907.1 10.1 %copy-start.37 = (f32[256]{0:T(256)S(1)}, f32[256]{0:T(256)}, u32[]{:S(2)}) copy-start(f32[256]{0:T(256)} %copy-done.36) | copy-start | bytes 3076
  907.1 10.1 %copy-start.44 = (f32[256]{0:T(256)S(1)}, f32[256]{0:T(256)}, u32[]{:S(2)}) copy-start(f32[256]{0:T(256)} %copy-done.43) | copy-start | bytes 3076
  (34 other events, 96.3 us)
Sparse Core Ops, SparseCore 0:
  10.8 66.9 all-gather.5
  189.4 53.7 reduce-scatter.10
  246.2 47.5 all-gather.9
  295.8 24.6 all-gather.7
  322.0 25.5 all-gather.11
  355.5 51.3 reduce-scatter.14
  411.3 25.5 all-gather.13
  440.5 170.2 all-reduce.4
  614.8 85.8 reduce-scatter.20
  704.6 101.4 reduce-scatter.18
  808.8 51.8 reduce-scatter.16
  863.1 34.7 reduce-scatter.12
where the time goes:
time: 934 us; the launch traced here: 928 us
  waiting for transfers between devices  476 us (51%)
  matrix products  124 us (13%)
  blocking collectives  120 us (13%)
  other arithmetic  87.7 us (9%)
  local copies, waits for them, and re-layouts  84.7 us (9%)
  between operations  15.8 us (2%)
  starting transfers between devices  11.6 us (1%)
    unnamed x15, waiting for transfers between devices  147 us
    ppermute x4, waiting for transfers between devices, passed_along(): return lax.ppermute(shard, axis, pairs)  88.7 us
    psum x2, blocking collectives, shards(): lax.psum((row_part, col_part, old_total, gain_part, scale_part), ('seq',...  81.3 us
    reduce_scatter x1, waiting for transfers between devices, shards(): lax.psum_scatter(times_trans(grad_pre, w_mlp[0]), 'tensor', scatter_dimen...  51.5 us
    reduce_scatter x1, waiting for transfers between devices, shards(): lax.psum_scatter(times_trans(context, w_out), 'tensor', scatter_dimension...  47.5 us
    all_gather x1, waiting for transfers between devices, shards(): lax.all_gather(mlp.astype(jnp.bfloat16), 'seq', axis=1, tiled=True)  46.1 us
    unnamed x115, local copies, waits for them, and re-layouts  42.2 us
    all_gather x1, blocking collectives, shards(): lax.all_gather(out_proj.astype(jnp.bfloat16), 'seq', axis=0, tiled=True)  38.2 us
  transfers between devices with their start and end apart: 16, of which 14 were waited for; matrix products, arithmetic and copies ran while one was open for 21% of the time, Pallas kernels for 0%

commit v1 on v0

v1 whole, which is shorter than its diff:
```python
import functools
import math

import jax
import jax.numpy as jnp
from jax import lax
from jax.experimental import pallas as pl
from jax.experimental.pallas import tpu as pltpu
from jax.sharding import PartitionSpec as P

HD = 80
WINDOW = 1024
BLOCK = 256
SPAN = WINDOW + BLOCK
LANES = 128

EPSILON = 1e-06
LOG_BASE = 1.442695
BETA_TWO = 0.5
STEP_RATE = 0.3
CLIP_LEVEL = 0.1
VECTOR_RATE = 0.3
NEGATIVE = -1e30
SCALE_ROOT = LOG_BASE / math.sqrt(HD)
VMEM_LIMIT = 56 * 1024 * 1024

bf16 = jnp.bfloat16
f32 = jnp.float32


def dot(left, right, dims):
    return lax.dot_general(left, right, (dims, ((), ())), preferred_element_type=f32)


def vmem_call(body, outs, scratch, flops, *args):
    size = sum(math.prod(a.shape) * a.dtype.itemsize for a in (*args, *outs))
    space = pl.BlockSpec(memory_space=pltpu.VMEM)
    return pl.pallas_call(
        body,
        out_shape=outs,
        in_specs=[space] * len(args),
        out_specs=[space] * len(outs),
        scratch_shapes=scratch,
        compiler_params=pltpu.CompilerParams(vmem_limit_bytes=VMEM_LIMIT),
        cost_estimate=pl.CostEstimate(flops=int(flops), bytes_accessed=size, transcendentals=0),
    )(*args)


def hop(value, axis, flip):
    peers = lax.axis_size(axis)
    return lax.ppermute(value, axis, [(i, i ^ flip) for i in range(peers)])


def after(value, *earlier):
    return lax.optimization_barrier((value, *earlier))[0]


def put(table, piece, row):
    return lax.dynamic_update_slice_in_dim(table, piece, row, 0)


def outer_pieces(shard):
    peers = lax.axis_size("seq")
    return [shard] + [hop(shard, "seq", f) for f in range(2, peers, 2)]


def pair_up(piece):
    other = hop(piece, "seq", 1)
    low = lax.axis_index("seq") % 2 == 0
    return jnp.concatenate([jnp.where(low, piece, other), jnp.where(low, other, piece)], axis=0)


def assemble(pairs):
    rows, cols = pairs[0].shape
    outer = lax.axis_index("seq") // 2
    table = jnp.zeros((rows * len(pairs), cols), pairs[0].dtype)
    for f, pair in enumerate(pairs):
        table = put(table, pair, (outer ^ f) * rows)
    return table


def scatter_seq(part):
    peers, here = lax.axis_size("seq"), lax.axis_index("seq")
    full, cols = part.shape
    rows = full // peers
    pairs = part.reshape(peers // 2, 2, rows, cols)
    low = here % 2
    send = lax.dynamic_index_in_dim(pairs, 1 - low, 1, keepdims=False)
    keep = lax.dynamic_index_in_dim(pairs, low, 1, keepdims=False)
    half = keep.astype(f32) + hop(send.astype(bf16), "seq", 1).astype(f32)
    pick = lambda f: lax.dynamic_index_in_dim(half, (here // 2) ^ f, 0, keepdims=False)
    total = pick(0)
    for f in range(1, peers // 2):
        total = total + hop(pick(f).astype(bf16), "seq", 2 * f).astype(f32)
    return total


def spread(payload, axis):
    peers = lax.axis_size(axis)
    return lax.all_to_all(
        jnp.broadcast_to(payload, (peers, *payload.shape)), axis, split_axis=0, concat_axis=0
    )


def packed(*values):
    flat = jnp.concatenate([v.reshape(-1) for v in values])
    size = -(-flat.shape[0] // 1024) * 1024
    return jnp.pad(flat, (0, size - flat.shape[0])).reshape(size // 128, 128)


def unpacked(table, *shapes):
    flat, out, at = table.reshape(-1), [], 0
    for shape in shapes:
        size = math.prod(shape)
        out.append(flat[at : at + size].reshape(shape))
        at += size
    return out


def head_of(rows, h):
    zeros = jnp.zeros((rows.shape[0], LANES - HD), rows.dtype)
    return jnp.concatenate([rows[:, h * HD : (h + 1) * HD], zeros], axis=1)


def attend_kernel(heads, h_ref, w_ref, sc_ref, lo_ref, q_ref, k_ref, v_ref, c_ref, lse_ref, kh, vt, bias):
    cols = heads * HD
    rows = q_ref.shape[0]
    for i in range(h_ref.shape[0] // BLOCK):
        at = pl.ds(i * BLOCK, BLOCK)
        proj = dot(h_ref[at, :], w_ref[...], ((1,), (0,)))
        if i * BLOCK >= WINDOW:
            q_ref[pl.ds(i * BLOCK - WINDOW, BLOCK), :] = (proj[:, :cols] * sc_ref[...]).astype(bf16)
        k_rows = proj[:, cols : 2 * cols].astype(bf16)
        v_rows = proj[:, 2 * cols :].astype(bf16)
        k_ref[at, :] = k_rows
        v_ref[at, :] = v_rows
        vt[:, at] = v_rows.T
        for h in range(heads):
            kh[h, at, :] = head_of(k_rows, h)

    def block(b, carry):
        q0 = pl.multiple_of(b * BLOCK, BLOCK)
        k_place = q0 + lax.broadcasted_iota(jnp.int32, (SPAN, BLOCK), 0)
        q_place = q0 + WINDOW + lax.broadcasted_iota(jnp.int32, (SPAN, BLOCK), 1)
        seen = (k_place >= lo_ref[:, pl.ds(q0, BLOCK)]) & (k_place <= q_place)
        bias[...] = jnp.where(seen, 0.0, NEGATIVE)
        q_rows = q_ref[pl.ds(q0, BLOCK), :]
        mixed = []
        for h in range(heads):
            q_head = head_of(q_rows, h)
            s = dot(kh[h, pl.ds(q0, SPAN), :], q_head, ((1,), (1,))) + bias[...]
            top = jnp.max(s, axis=0, keepdims=True)
            p = jnp.exp(s - top)
            total = jnp.sum(p, axis=0, keepdims=True)
            part = dot(vt[h * HD : (h + 1) * HD, pl.ds(q0, SPAN)], p.astype(bf16), ((1,), (0,)))
            mixed.append((part / total).T)
            lse_ref[pl.ds(h, 1), pl.ds(q0, BLOCK)] = top + jnp.log(total)
        c_ref[pl.ds(q0, BLOCK), :] = jnp.concatenate(mixed, axis=1).astype(bf16)
        return carry

    lax.fori_loop(0, rows // BLOCK, block, 0)


def attend_back_kernel(
    heads, q_ref, k_ref, v_ref, g_ref, sc_ref, lo_ref, lse_ref, dq_ref, dkv_ref, part_ref, kh, vh, kt, dk, dv, bias
):
    rows = q_ref.shape[0]
    kt[...] = k_ref[...].T
    for h in range(heads):
        kh[h] = head_of(k_ref[...], h)
        vh[h] = head_of(v_ref[...], h)
    dk[...] = jnp.zeros_like(dk)
    dv[...] = jnp.zeros_like(dv)
    part_ref[...] = jnp.zeros_like(part_ref)

    def block(b, carry):
        q0 = pl.multiple_of(b * BLOCK, BLOCK)
        at, keys = pl.ds(q0, BLOCK), pl.ds(q0, SPAN)
        k_place = q0 + lax.broadcasted_iota(jnp.int32, (SPAN, BLOCK), 0)
        q_place = q0 + WINDOW + lax.broadcasted_iota(jnp.int32, (SPAN, BLOCK), 1)
        seen = (k_place >= lo_ref[:, at]) & (k_place <= q_place)
        bias[...] = jnp.where(seen, 0.0, NEGATIVE)
        q_rows, g_rows = q_ref[at, :], g_ref[at, :]
        grads = []
        for h in range(heads):
            q_head = head_of(q_rows, h)
            g_head = head_of(g_rows, h)
            s = dot(kh[h, keys, :], q_head, ((1,), (1,))) + bias[...]
            p = jnp.exp(s - lse_ref[pl.ds(h, 1), at])
            dp = dot(vh[h, keys, :], g_head, ((1,), (1,)))
            inner = jnp.sum(p * dp, axis=0, keepdims=True)
            ds = (p * (dp - inner)).astype(bf16)
            dv[h, keys, :] += dot(p.astype(bf16), g_head, ((1,), (0,)))
            dk[h, keys, :] += dot(ds, q_head, ((1,), (0,)))
            grads.append(dot(kt[h * HD : (h + 1) * HD, keys], ds, ((1,), (0,))).T)
        grad = jnp.concatenate(grads, axis=1)
        part_ref[...] += jnp.sum(grad * q_rows.astype(f32), axis=0, keepdims=True)
        dq_ref[at, :] = (grad * sc_ref[...]).astype(bf16)
        return carry

    lax.fori_loop(0, rows // BLOCK, block, 0)
    for i in range(k_ref.shape[0] // BLOCK):
        at = pl.ds(i * BLOCK, BLOCK)
        for j, table in enumerate((dk, dv)):
            dkv_ref[j, at, :] = jnp.concatenate(
                [table[h, at, :HD] for h in range(heads)], axis=1
            ).astype(bf16)


def share_kernel(peers, *refs):
    ctx, mats = refs[:peers], refs[peers : 2 * peers]
    x_ref, cot_ref, gain_ref = refs[2 * peers : 2 * peers + 3]
    outs = refs[2 * peers + 3 :]
    res_ref, gmid_ref, part_ref, h2_ref, gm_ref, hid_ref, gpre_ref = outs[:7]
    gctx = outs[7 : 7 + peers]
    w_out, w_in, w_back = outs[7 + peers :]
    cols = ctx[0].shape[1]
    for r, m in enumerate(mats):
        for j, w in enumerate((w_out, w_in, w_back)):
            w[:, r * cols : (r + 1) * cols] = m[:, j * cols : (j + 1) * cols]
    gain = gain_ref[...]
    mixed = jnp.concatenate([c[...] for c in ctx], axis=1)
    mid = x_ref[...].astype(f32) + dot(mixed, w_out[...], ((1,), (1,)))
    factor = lax.rsqrt(jnp.mean(mid * mid, axis=-1, keepdims=True) + EPSILON)
    normed = mid * factor
    h2 = (normed * gain).astype(bf16)
    h2_ref[...] = h2
    cot = cot_ref[...]
    pre = dot(h2, w_in[...], ((1,), (0,)))
    g_hid = dot(cot, w_back[...], ((1,), (0,)))
    sig = 1.0 / (1.0 + jnp.exp(-pre))
    hidden = (pre * sig).astype(bf16)
    g_pre = (g_hid * sig * (1.0 + pre * (1.0 - sig))).astype(bf16)
    for r in range(peers):
        hid_ref[r] = hidden[:, r * cols : (r + 1) * cols]
        gpre_ref[r] = g_pre[:, r * cols : (r + 1) * cols]
    res_ref[...] = mid + dot(hidden, w_back[...], ((1,), (1,)))
    g_h2 = dot(g_pre, w_in[...], ((1,), (1,)))
    part_ref[...] = jnp.sum(g_h2 * normed, axis=0, keepdims=True)
    scaled = g_h2 * gain
    back = factor * (scaled - normed * jnp.mean(scaled * normed, axis=-1, keepdims=True))
    g_mid = cot.astype(f32) + back
    gmid_ref[...] = g_mid
    gm = g_mid.astype(bf16)
    gm_ref[...] = gm
    g_mixed = dot(gm, w_out[...], ((1,), (0,))).astype(bf16)
    for r, out in enumerate(gctx):
        out[...] = g_mixed[:, r * cols : (r + 1) * cols]


def share_grads_kernel(peers, *refs):
    ctx = refs[:peers]
    gm_ref, h2_ref, cot_ref, gpre_ref, hid_ref = refs[peers : peers + 5]
    outs = refs[peers + 5 :]
    lefts = (gm_ref[...].T, h2_ref[...].T, cot_ref[...].T)
    split = outs[0].shape[-1]
    for r in range(peers):
        parts = [
            dot(left, right, ((1,), (0,))).astype(bf16)
            for left, right in zip(lefts, (ctx[r][...], gpre_ref[r], hid_ref[r]))
        ]
        whole = jnp.concatenate(parts, axis=1)
        outs[r % 2][r // 2] = whole[:, :split]
        outs[2 + r % 2][r // 2] = whole[:, split:]


def shards(
    tokens,
    cotangent,
    lengths,
    qkv,
    out_proj,
    mlp,
    gains,
    query_scale,
    row_second,
    col_second,
    gain_second,
    scale_second,
):
    n_tensor, n_seq = lax.axis_size("tensor"), lax.axis_size("seq")
    seq_index, ten_index = lax.axis_index("seq"), lax.axis_index("tensor")
    tok_dev, width = tokens.shape
    share = cotangent.shape[0]
    rows_own, cols_own = qkv.shape[1], qkv.shape[2]
    heads = cols_own // HD
    row_first = ten_index * share
    flips = list(range(n_tensor))
    sds = jax.ShapeDtypeStruct

    x_share = lax.dynamic_slice_in_dim(tokens, row_first, share, 0)
    rim_own = lax.ppermute(x_share, "seq", [(i, i + 1) for i in range(n_seq - 1)])

    shard_m = jnp.concatenate([out_proj, mlp[0], mlp[1]], axis=1).astype(bf16)
    shard_qkv = jnp.concatenate([qkv[0], qkv[1], qkv[2]], axis=1).astype(bf16)
    outer_m = outer_pieces(shard_m)
    pairs_m = [pair_up(piece) for piece in outer_m]
    rim_outer = [rim_own] + [hop(rim_own, "tensor", f) for f in flips[2::2]]
    rim_inner = [hop(piece, "tensor", 1) for piece in rim_outer]
    mats = [None] * n_tensor
    mats[0] = assemble(pairs_m)
    for f in flips[2::2]:
        mats[f] = assemble([hop(pair, "tensor", f) for pair in pairs_m])
    for f in flips[::2]:
        mats[f + 1] = hop(mats[f], "tensor", 1)
    outer_q = outer_pieces(after(shard_qkv, outer_m[-1], rim_own))
    w_qkv = assemble([pair_up(piece) for piece in outer_q])

    rim = jnp.zeros((WINDOW + tok_dev, width), bf16)
    rim = put(rim, tokens, WINDOW)
    for f, one, two in zip(flips[::2], rim_outer, rim_inner):
        rim = put(rim, one, (ten_index ^ f) * share)
        rim = put(rim, two, (ten_index ^ f ^ 1) * share)
    x_all = rim.astype(f32)
    factor_all = lax.rsqrt(jnp.mean(x_all * x_all, axis=-1, keepdims=True) + EPSILON)
    h_all = (x_all * factor_all * gains[0]).astype(bf16)

    places = seq_index * tok_dev + jnp.arange(tok_dev, dtype=jnp.int32)
    ends = jnp.cumsum(lengths[0])
    passed = ends[None, :] <= places[:, None]
    doc_start = jnp.max(jnp.where(passed, ends[None, :], 0), axis=1)
    lo = jnp.maximum(places - (WINDOW - 1), doc_start)
    lo = jnp.where(places >= ends[-1], places, lo)
    lo = (lo - (seq_index * tok_dev - WINDOW)).astype(jnp.int32)[None, :]

    factor = jax.nn.softplus(query_scale) * SCALE_ROOT
    scale_cols = jnp.tile(factor, heads)[None, :]
    table = WINDOW + tok_dev
    pair_flops = tok_dev * SPAN * cols_own * 2
    queries, key_rows, value_rows, context, log_totals = vmem_call(
        functools.partial(attend_kernel, heads),
        (
            sds((tok_dev, cols_own), bf16),
            sds((table, cols_own), bf16),
            sds((table, cols_own), bf16),
            sds((tok_dev, cols_own), bf16),
            sds((heads, tok_dev), f32),
        ),
        [
            pltpu.VMEM((heads, table, LANES), bf16),
            pltpu.VMEM((cols_own, table), bf16),
            pltpu.VMEM((SPAN, BLOCK), f32),
        ],
        2 * table * width * 3 * cols_own + 6 * pair_flops,
        h_all,
        w_qkv,
        scale_cols,
        lo,
    )

    def share_of(values, f):
        return lax.dynamic_slice_in_dim(values, (ten_index ^ f) * share, share, 0)

    ctx = [share_of(context, f) for f in flips]
    ctx = [ctx[0]] + [hop(ctx[f], "tensor", f) for f in flips[1:]]
    shape_share = (share, width)
    outs = vmem_call(
        functools.partial(share_kernel, n_tensor),
        (
            sds(shape_share, f32),
            sds(shape_share, f32),
            sds((1, width), f32),
            sds(shape_share, bf16),
            sds(shape_share, bf16),
            sds((n_tensor, share, cols_own), bf16),
            sds((n_tensor, share, cols_own), bf16),
            *[sds((share, cols_own), bf16) for _ in flips],
        ),
        [pltpu.VMEM((width, width), bf16) for _ in range(3)],
        2 * 6 * share * width * width,
        *ctx,
        *mats,
        x_share,
        cotangent,
        gains[1:],
    )
    result, grad_mid, gain_two_grad, h_two, grad_mid_low, hidden, grad_pre = outs[:7]
    gctx = list(outs[7:])
    gctx = [gctx[0]] + [hop(gctx[f], "tensor", f) for f in flips[1:]]
    grad_context = jnp.zeros((tok_dev, cols_own), bf16)
    for f in flips:
        grad_context = put(grad_context, gctx[f], (ten_index ^ f) * share)

    split = -(-3 * cols_own // 256) * 128
    chunks = [sds((n_tensor // 2, width, c), bf16) for c in (split, 3 * cols_own - split)]
    halves = vmem_call(
        functools.partial(share_grads_kernel, n_tensor),
        (chunks[0], chunks[0], chunks[1], chunks[1]),
        [],
        2 * 3 * share * width * width,
        *ctx,
        grad_mid_low,
        h_two,
        cotangent,
        grad_pre,
        hidden,
    )
    own_m = []
    for even, odd in (halves[:2], halves[2:]):
        from_core = hop(odd, "tensor", 1)
        sums = [even[i].astype(f32) + from_core[i].astype(f32) for i in range(n_tensor // 2)]
        grad_m = sums[0]
        for i in range(1, n_tensor // 2):
            grad_m = grad_m + hop(sums[i].astype(bf16), "tensor", 2 * i).astype(f32)
        own_m.append(scatter_seq(grad_m))
    own_m = jnp.concatenate(own_m, axis=1)

    grad_q, grad_kv, scale_raw = vmem_call(
        functools.partial(attend_back_kernel, heads),
        (
            sds((tok_dev, cols_own), bf16),
            sds((2, table, cols_own), bf16),
            sds((1, cols_own), f32),
        ),
        [
            pltpu.VMEM((heads, table, LANES), bf16),
            pltpu.VMEM((heads, table, LANES), bf16),
            pltpu.VMEM((cols_own, table), bf16),
            pltpu.VMEM((heads, table, LANES), f32),
            pltpu.VMEM((heads, table, LANES), f32),
            pltpu.VMEM((SPAN, BLOCK), f32),
        ],
        14 * pair_flops,
        queries,
        key_rows,
        value_rows,
        grad_context,
        scale_cols,
        lo,
        log_totals,
    )
    scale_part = (
        jnp.sum((scale_raw / scale_cols).reshape(heads, HD), axis=0)
        * SCALE_ROOT
        * jax.nn.sigmoid(query_scale)
    )
    grad_w = jnp.concatenate(
        [
            dot(h_all[WINDOW:], grad_q, ((0,), (0,))),
            dot(h_all, grad_kv[0], ((0,), (0,))),
            dot(h_all, grad_kv[1], ((0,), (0,))),
        ],
        axis=1,
    ).astype(bf16)
    own_qkv = scatter_seq(grad_w)

    back = lax.ppermute(grad_kv[:, :WINDOW], "seq", [(i, i - 1) for i in range(1, n_seq)])
    own_kv = grad_kv[:, WINDOW:].astype(f32)
    own_kv = own_kv.at[:, tok_dev - WINDOW :].add(back.astype(f32)).astype(bf16)
    grad_proj = jnp.concatenate([grad_q, own_kv[0], own_kv[1]], axis=1)
    partial_one = dot(grad_proj, w_qkv, ((1,), (1,))).astype(bf16)
    odd_rows = jnp.stack([share_of(partial_one, f + 1) for f in flips[::2]])
    even_rows = [share_of(partial_one, f).astype(f32) for f in flips[::2]]
    from_core_rows = hop(odd_rows, "tensor", 1).astype(f32)
    sums = [rows + from_core_rows[i] for i, rows in enumerate(even_rows)]
    grad_one = sums[0]
    for i in range(1, n_tensor // 2):
        grad_one = grad_one + hop(sums[i].astype(bf16), "tensor", 2 * i).astype(f32)
    x_part = x_share.astype(f32)
    factor_one = lax.rsqrt(jnp.mean(x_part * x_part, axis=-1, keepdims=True) + EPSILON)
    norm_one = x_part * factor_one
    gain_one_grad = jnp.sum(grad_one * norm_one, axis=0)
    scaled = grad_one * gains[0]
    tokens_grad = grad_mid + factor_one * (
        scaled - norm_one * jnp.mean(scaled * norm_one, axis=-1, keepdims=True)
    )

    stacked = jnp.stack(
        [g[:, i * cols_own : (i + 1) * cols_own] for g in (own_qkv, own_m) for i in range(3)]
    )
    squares = stacked * stacked
    col_part = jnp.sum(squares, axis=1)
    row_part = jnp.sum(squares, axis=2)
    seq_sums = jnp.sum(spread(packed(col_part, jnp.sum(row_second, axis=1)), "seq"), axis=0)
    col_square, old_sums = unpacked(seq_sums, (6, cols_own), (6,))
    ten_sums = jnp.sum(spread(packed(row_part, jnp.sum(col_square, axis=1)), "tensor"), axis=0)
    row_square, all_square = unpacked(ten_sums, (6, rows_own), (6,))
    total_cols = cols_own * n_tensor
    row_new = BETA_TWO * row_second + (1.0 - BETA_TWO) * row_square / total_cols
    col_new = BETA_TWO * col_second + (1.0 - BETA_TWO) * col_square / width
    row_mean = (BETA_TWO * old_sums + (1.0 - BETA_TWO) * all_square / total_cols) / width
    update = stacked * lax.rsqrt(
        row_new[:, :, None] * col_new[:, None, :] / row_mean[:, None, None]
    )
    update_part = jnp.sum(update * update, axis=(1, 2))

    gain_part = jnp.stack([gain_one_grad, gain_two_grad[0]])
    gain_part = gain_part.reshape(2, n_seq, rows_own).transpose(1, 0, 2).reshape(n_seq, 2 * rows_own)
    rest = jnp.broadcast_to(jnp.concatenate([scale_part, update_part]), (n_seq, HD + 6))
    last = jnp.concatenate([gain_part, rest], axis=1)
    size = -(-last.shape[1] // 1024) * 1024
    last = jnp.pad(last, ((0, 0), (0, size - last.shape[1]))).reshape(n_seq, 1, size // 128, 128)
    last = jnp.broadcast_to(last, (n_seq, n_tensor, size // 128, 128))
    last = last.reshape(n_seq * n_tensor, size // 128, 128)
    got = lax.all_to_all(last, ("seq", "tensor"), split_axis=0, concat_axis=0)
    gains_grad, scale_grad, update_square = unpacked(
        jnp.sum(got, axis=0), (2, rows_own), (HD,), (6,)
    )
    update_rms = jnp.sqrt(update_square / (width * total_cols))
    weights_old = jnp.concatenate([qkv, out_proj[None], mlp], axis=0)
    fresh = (
        weights_old - STEP_RATE * update / jnp.maximum(1.0, update_rms / CLIP_LEVEL)[:, None, None]
    )
    gains_own = lax.dynamic_slice_in_dim(gains, seq_index * rows_own, rows_own, 1)
    gain_second_new = BETA_TWO * gain_second + (1.0 - BETA_TWO) * gains_grad * gains_grad
    gains_new = gains_own - VECTOR_RATE * gains_grad * lax.rsqrt(gain_second_new)
    scale_second_new = BETA_TWO * scale_second + (1.0 - BETA_TWO) * scale_grad * scale_grad
    scale_new = query_scale - VECTOR_RATE * scale_grad * lax.rsqrt(scale_second_new)
    return (
        result,
        tokens_grad,
        stacked[:3],
        stacked[3],
        stacked[4:],
        gains_grad,
        scale_grad,
        fresh[:3],
        fresh[3],
        fresh[4:],
        gains_new,
        scale_new,
        row_new,
        col_new,
        update_rms,
        gain_second_new,
        scale_second_new,
    )


def solution(mesh):
    return jax.shard_map(
        shards,
        mesh=mesh,
        in_specs=(
            P("seq", None),
            P(("seq", "tensor"), None),
            P(),
            P(None, "seq", "tensor"),
            P("seq", "tensor"),
            P(None, "seq", "tensor"),
            P(),
            P(),
            P(None, "seq"),
            P(None, "tensor"),
            P(None, "seq"),
            P(),
        ),
        out_specs=(
            P(("seq", "tensor"), None),
            P(("seq", "tensor"), None),
            P(None, "seq", "tensor"),
            P("seq", "tensor"),
            P(None, "seq", "tensor"),
            P(None, "seq"),
            P(),
            P(None, "seq", "tensor"),
            P("seq", "tensor"),
            P(None, "seq", "tensor"),
            P(None, "seq"),
            P(),
            P(None, "seq"),
            P(None, "tensor"),
            P(),
            P(None, "seq"),
            P(),
        ),
        check_vma=False,
    )
```

time: 934 us -> 508 us (0.54)
  waiting for transfers between devices: 476 us -> 162 us
  blocking collectives: 120 us -> 0 us
  matrix products: 124 us -> 13.7 us
  starting transfers between devices: 11.6 us -> 91.6 us
  Pallas kernels: 0 us -> 72.3 us
  between operations: 15.8 us -> 1.85 us
  other arithmetic: 87.7 us -> 74.4 us
    unnamed x15 -> x0, waiting for transfers between devices: 147 us -> none
    all_gather x5 -> x0, waiting for transfers between devices: 133 us -> none  [the longest x1 46.1 us: shards(): lax.all_gather(mlp.astype(jnp.bfloat16), 'seq', axis=1, tiled=True)]
    reduce_scatter x4 -> x0, waiting for transfers between devices: 107 us -> none  [the longest x1 51.5 us: shards(): lax.psum_scatter(times_trans(grad_pre, w_mlp[0]), 'tensor', scatter_dimen...]
    dot_general x25 -> x4, matrix products: 120 us -> 13.7 us  [dot(): lax.dot_general(left, right, (dims, ((), ())), preferred_element_type=f32)]
    psum x2 -> x0, blocking collectives: 81.3 us -> none  [shards(): lax.psum((row_part, col_part, old_total, gain_part, scale_part), ('seq',...]
    pallas_call x0 -> x4, Pallas kernels: none -> 72.3 us  [vmem_call(): pl.pallas_call(body, out_shape=outs, in_specs=[space] * len(args), out_sp...]
    ppermute x4 -> x49, starting transfers between devices: 10.9 us -> 78.6 us  [the longest x47 74.2 us: hop(): return lax.ppermute(value, axis, [(i, i ^ flip) for i in range(peers)])]
    ppermute x4 -> x49, waiting for transfers between devices: 88.7 us -> 149 us  [the longest x47 149 us: hop(): return lax.ppermute(value, axis, [(i, i ^ flip) for i in range(peers)])]
  transfers between devices with their start and end apart: 16 -> 52, of which waited for: 14 -> 20; matrix products, arithmetic and copies ran while one was open for 21% -> 26% of each run, Pallas kernels for 0% -> 7%
where the time goes in v1:
time: 508 us; the launch traced here: 503 us
  waiting for transfers between devices  162 us (32%)
  starting transfers between devices  91.6 us (18%)
  local copies, waits for them, and re-layouts  87 us (17%)
  other arithmetic  74.4 us (15%)
  Pallas kernels  72.3 us (14%)
  matrix products  13.7 us (3%)
    ppermute x47, waiting for transfers between devices, hop(): return lax.ppermute(value, axis, [(i, i ^ flip) for i in range(peers)])  149 us
    ppermute x47, starting transfers between devices, hop(): return lax.ppermute(value, axis, [(i, i ^ flip) for i in range(peers)])  74.2 us
    pallas_call x4, Pallas kernels, vmem_call(): pl.pallas_call(body, out_shape=outs, in_specs=[space] * len(args), out_sp...  72.3 us
    dynamic_update_slice x15, local copies, waits for them, and re-layouts, put(): return lax.dynamic_update_slice_in_dim(table, piece, row, 0)  21.3 us
    dot_general x4, matrix products, dot(): lax.dot_general(left, right, (dims, ((), ())), preferred_element_type=f32)  13.7 us
    unnamed x112, local copies, waits for them, and re-layouts  12.6 us
    ppermute x3, local copies, waits for them, and re-layouts, hop(): return lax.ppermute(value, axis, [(i, i ^ flip) for i in range(peers)])  11.4 us
  transfers between devices with their start and end apart: 52, of which 20 were waited for; matrix products, arithmetic and copies ran while one was open for 26% of the time, Pallas kernels for 7%

profile of v1, /device:TPU:0, one launch (start us, length us, event | category | flops | bytes accessed | tf_op | source)
XLA Modules:
  0.0 502.9 jit_solution(4943689585802189537)
XLA Ops:
  3.7 3.0 collective-permute-start.15
  12.4 3.1 collective-permute-start
  17.4 2.7 dynamic_update_slice.63
  30.4 3.8 collective-permute-done.18
  40.6 3.7 collective-permute-done.19
  52.6 2.8 copy.64
  59.8 11.1 %collective-permute-start.6 = (bf16[160,960]{1,0:T(8,128)(2,1)}, bf16[160,960]{1,0:T(8,128)(2,1)}, u32[]{:S(2)}, u32[]{:S(2)}) collective-permute-start(bf16[160,960]{1,0:T(8,128)(2,1)} %pad_maximum_fusion.8), channel_id=1, source_target_pairs={{0,8},{4,12},{8,0},{12,4},{16,24},{20,28},{24,16},{28,20},{1,9},{5... | collective-permute-start | bytes 921608 | tf_op jit(solution)/shard_map/ppermute | solution.py:51
  74.7 3.5 collective-permute-start.8
  79.7 2.7 collective-permute-start.10
  88.3 11.1 %collective-permute-done.8 = bf16[160,960]{1,0:T(8,128)(2,1)} collective-permute-done((bf16[160,960]{1,0:T(8,128)(2,1)}, bf16[160,960]{1,0:T(8,128)(2,1)}, u32[]{:S(2)}, u32[]{:S(2)}) %collective-permute-start.8) | collective-permute-done | bytes 307232 | tf_op jit(solution)/shard_map/ppermute | solution.py:51
  103.3 4.4 copy.65
  112.5 5.7 %collective-permute-done.11 = bf16[160,960]{1,0:T(8,128)(2,1)S(1)} collective-permute-done((bf16[160,960]{1,0:T(8,128)(2,1)}, bf16[160,960]{1,0:T(8,128)(2,1)S(1)}, u32[]{:S(2)}, u32[]{:S(2)}) %collective-permute-start.11) | collective-permute-done | bytes 307232 | tf_op jit(solution)/shard_map/ppermute | solution.py:51
  119.2 5.5 %collective-permute-done.2 = bf16[256,1280]{1,0:T(8,128)(2,1)S(1)} collective-permute-done((bf16[256,1280]{1,0:T(8,128)(2,1)}, bf16[256,1280]{1,0:T(8,128)(2,1)S(1)}, u32[]{:S(2)}, u32[]{:S(2)}) %collective-permute-start.2) | collective-permute-done | bytes 655392 | tf_op jit(solution)/shard_map/ppermute | solution.py:51
  130.2 3.6 fusion.2.h_ref
  133.7 23.9 %shard_map.256 = (bf16[1024,320]{1,0:T(8,128)(2,1)}, bf16[2048,320]{1,0:T(8,128)(2,1)}, bf16[2048,320]{1,0:T(8,128)(2,1)}, bf16[1024,320]{1,0:T(8,128)(2,1)}, f32[4,1024]{1,0:T(4,128)}) custom-call(bf16[2048,1280]{1,0:T(8,128)(2,1)} %fusion.2.h_ref, bf16[1280,960]{1,0:T(8,128)(2,1)} %maximum_dynamic-update-slice_fusion.3.w_ref, ...), custom_call_target="tpu_custom_call" | custom-call | flops 10066329600 | bytes 11654400 | tf_op jit(solution)/shard_map/pallas_call | solution.py:38
  161.5 4.4 copy.66.refs_5_
  165.9 4.5 copy.67.refs_7_
  171.1 13.5 %shard_map.257 = (f32[256,1280]{1,0:T(8,128)}, f32[256,1280]{1,0:T(8,128)}, f32[1,1280]{1,0:T(1,128)}, bf16[256,1280]{1,0:T(8,128)(2,1)}, bf16[256,1280]{1,0:T(8...) custom-call(bf16[256,320]{1,0:T(8,128)(2,1)} %get-tuple-element.121., ...), custom_call_target="tpu_custom_call" | custom-call | flops 5033164800 | bytes 17704960 | tf_op jit(solution)/shard_map/pallas_call | solution.py:38
  185.4 3.5 fusion.74
  189.0 8.4 %copy.71 = bf16[1280,2048]{1,0:T(8,128)(2,1)} copy(bf16[1280,2048]{0,1:T(8,128)(2,1)} %fusion.74) | data formatting | bytes 10485760 | tf_op jit(solution)/shard_map/dot_general | solution.py:32
  199.0 6.2 %collective-permute-done.28 = bf16[256,320]{1,0:T(8,128)(2,1)S(1)} collective-permute-done((bf16[256,320]{1,0:T(8,128)(2,1)S(1)}, bf16[256,320]{1,0:T(8,128)(2,1)S(1)}, u32[]{:S(2)}, u32[]{:S(2)}) %collective-permute-start.28) | collective-permute-done | bytes 163872 | tf_op jit(solution)/shard_map/ppermute | solution.py:51
  208.5 25.5 %shard_map.258 = (bf16[1024,320]{1,0:T(8,128)(2,1)}, bf16[2,2048,320]{2,1,0:T(8,128)(2,1)}, f32[1,320]{1,0:T(1,128)}) custom-call(bf16[1024,320]{1,0:T(8,128)(2,1)} %get-tuple-element.65.q_ref, bf16[2048,320]{1,0:T(8,128)(2,1)} %get-tuple-element.66.k_ref, bf16[2048,320]{1,0:T(8,128)(2,1)} %get-tuple-element.67.v_ref, bf16[1024,320]{1,0:T(8,128)(2,1)} %copy-done.22, ...), custom_call_target="tpu_custom_call" | custom-call | flops 11744051200 | bytes 7232000 | tf_op jit(solution)/shard_map/pallas_call | solution.py:38
  234.0 5.4 %fusion.18 = bf16[4,2,160,320]{3,2,1,0:T(8,128)(2,1)} fusion(bf16[4,2,160,2048]{3,2,1,0:T(8,128)(2,1)S(1)} %bitcast.173, bf16[2,2048,320]{2,1,0:T(8,128)(2,1)} %get-tuple-element.74), kind=kOutput, calls=%fused_computation.34 | convolution fusion | flops 1678131200 | bytes 7634944 | tf_op jit(solution)/shard_map/dot_general | solution.py:32
  239.4 3.9 fusion.21
  245.8 2.9 pad_maximum_fusion
  255.6 9.4 %shard_map.259 = (bf16[2,1280,512]{2,1,0:T(8,128)(2,1)}, bf16[2,1280,512]{2,1,0:T(8,128)(2,1)}, bf16[2,1280,448]{2,1,0:T(8,128)(2,1)}, bf16[2,1280,448]{2,1,0:T(8,128)(2,1)}) custom-call(bf16[256,320]{1,0:T(8,128)(2,1)} %get-tuple-element.121.refs_0_, bf16[256,320]{1,0:T(8,128)(2,1)} %copy-done.38, bf16[256,320]{1,0:T(8,128)(2,1)} %copy-done.39, ...), custom_call_target="tpu_custom_call" | custom-call | flops 2516582400 | bytes 13762560 | tf_op jit(solution)/shard_map/pallas_call | solution.py:38
  265.0 4.7 copy.75
  271.6 36.0 %collective-permute-done.33 = bf16[4,160,960]{2,1,0:T(8,128)(2,1)} collective-permute-done((bf16[4,160,960]{2,1,0:T(8,128)(2,1)}, bf16[4,160,960]{2,1,0:T(8,128)(2,1)}, u32[]{:S(2)}, u32[]{:S(2)}) %collective-permute-start.33) | collective-permute-done | bytes 1228832 | tf_op jit(solution)/shard_map/ppermute | solution.py:51
  311.2 4.3 collective-permute-start.36
  321.0 3.3 convolution_convert_fusion
  326.2 10.6 %collective-permute-done.35 = bf16[160,960]{1,0:T(8,128)(2,1)S(1)} collective-permute-done((bf16[160,960]{1,0:T(8,128)(2,1)S(1)}, bf16[160,960]{1,0:T(8,128)(2,1)S(1)}, u32[]{:S(2)}, u32[]{:S(2)}) %collective-permute-start.35) | collective-permute-done | bytes 307232 | tf_op jit(solution)/shard_map/ppermute | solution.py:51
  338.4 3.2 fusion.68
  343.1 2.8 fusion.31
  352.0 3.1 fusion.30
  361.5 15.4 %collective-permute-done.44 = bf16[1280,448]{0,1:T(8,128)(2,1)} collective-permute-done((bf16[1280,448]{0,1:T(8,128)(2,1)}, bf16[1280,448]{0,1:T(8,128)(2,1)}, u32[]{:S(2)}, u32[]{:S(2)}) %collective-permute-start.44) | collective-permute-done | bytes 1146912 | tf_op jit(solution)/shard_map/ppermute | solution.py:51
  384.3 20.6 %collective-permute-done.38 = bf16[1280,512]{1,0:T(8,128)(2,1)} collective-permute-done((bf16[1280,512]{1,0:T(8,128)(2,1)}, bf16[1280,512]{1,0:T(8,128)(2,1)}, u32[]{:S(2)}, u32[]{:S(2)}) %collective-permute-start.38) | collective-permute-done | bytes 1310752 | tf_op jit(solution)/shard_map/ppermute | solution.py:51
  410.0 6.0 %collective-permute-done.32 = bf16[256,1280]{1,0:T(8,128)(2,1)} collective-permute-done((bf16[256,1280]{1,0:T(8,128)(2,1)S(1)}, bf16[256,1280]{1,0:T(8,128)(2,1)}, u32[]{:S(2)}, u32[]{:S(2)}) %collective-permute-start.32) | collective-permute-done | bytes 655392 | tf_op jit(solution)/shard_map/ppermute | solution.py:51
  418.3 7.6 %collective-permute-start.46 = (bf16[160,448]{1,0:T(8,128)(2,1)S(1)}, bf16[160,448]{1,0:T(8,128)(2,1)S(1)}, u32[]{:S(2)}, u32[]{:S(2)}) collective-permute-start(bf16[160,448]{1,0:T(8,128)(2,1)S(1)} %get-tuple-element.112), channel_id=1, source_target_pairs={{0,8},{4,12},{8,0},{12,4},{16,24},{20,28},{24,16},{28,20},{1,9},{5... | collective-permute-start | bytes 430088 | tf_op jit(solution)/shard_map/ppermute | solution.py:51
  430.7 2.8 collective-permute-done.46
  433.5 2.9 collective-permute-start.42
  436.4 4.7 collective-permute-done.47
  441.3 12.0 %collective-permute-done.41 = bf16[160,512]{1,0:T(8,128)(2,1)S(1)} collective-permute-done((bf16[160,512]{1,0:T(8,128)(2,1)S(1)}, bf16[160,512]{1,0:T(8,128)(2,1)S(1)}, u32[]{:S(2)}, u32[]{:S(2)}) %collective-permute-start.41) | collective-permute-done | bytes 163872 | tf_op jit(solution)/shard_map/ppermute | solution.py:51
  456.0 5.9 %all-to-all-start = ((f32[8,16,128]{2,1,0:T(8,128)}), f32[8,16,128]{2,1,0:T(8,128)}, u32[]{:S(2)}, u32[]{:S(2)}) async-start(f32[8,16,128]{2,1,0:T(8,128)} %broadcast_in_dim.26), calls=%async_computation | async-start | bytes 131072 | tf_op jit(solution)/shard_map/all_to_all | solution.py:100
  461.9 2.7 fusion.27
  465.4 3.5 all-to-all-done
  471.9 3.9 all-to-all-start.1
  484.6 3.3 all-to-all-start.2
  488.8 7.3 %all-to-all-done.2 = f32[32,8,128]{2,1,0:T(8,128)} async-done(((f32[32,8,128]{2,1,0:T(8,128)}), f32[32,8,128]{2,1,0:T(8,128)}, u32[]{:S(2)}, u32[]{:S(2)}) %all-to-all-start.2) | async-done | bytes 131104 | tf_op jit(solution)/shard_map/all_to_all | solution.py:495
  (322 shorter events, 156.1 us)
Async XLA Ops:
  3.7 22.6 %collective-permute-start.15 = (bf16[160,960]{1,0:T(8,128)(2,1)}, bf16[160,960]{1,0:T(8,128)(2,1)}, u32[]{:S(2)}, u32[]{:S(2)}) collective-permute-start(bf16[160,960]{1,0:T(8,128)(2,1)} %pad_maximum_fusion.9), channel_id=1, source_target_pairs={{0,4},{4,0},{8,12},{12,8},{16,20},{20,16},{24,28},{28,24},{1,5},{5... | collective-permute-start | bytes 921608 | tf_op jit(solution)/shard_map/ppermute | solution.py:51
  6.7 18.6 %collective-permute-start.16 = (bf16[160,960]{1,0:T(8,128)(2,1)}, bf16[160,960]{1,0:T(8,128)(2,1)}, u32[]{:S(2)}, u32[]{:S(2)}) collective-permute-start(bf16[160,960]{1,0:T(8,128)(2,1)} %pad_maximum_fusion.9), channel_id=1, source_target_pairs={{0,8},{4,12},{8,0},{12,4},{16,24},{20,28},{24,16},{28,20},{1,9},{5... | collective-permute-start | bytes 921608 | tf_op jit(solution)/shard_map/ppermute | solution.py:51
  8.3 25.9 %collective-permute-start.18 = (bf16[160,960]{1,0:T(8,128)(2,1)}, bf16[160,960]{1,0:T(8,128)(2,1)}, u32[]{:S(2)}, u32[]{:S(2)}) collective-permute-start(bf16[160,960]{1,0:T(8,128)(2,1)} %pad_maximum_fusion.9), channel_id=1, source_target_pairs={{0,16},{4,20},{8,24},{12,28},{16,0},{20,4},{24,8},{28,12},{1,17},{... | collective-permute-start | bytes 921608 | tf_op jit(solution)/shard_map/ppermute | solution.py:51
  10.9 23.8 %collective-permute-start.4 = (bf16[160,960]{1,0:T(8,128)(2,1)}, bf16[160,960]{1,0:T(8,128)(2,1)}, u32[]{:S(2)}, u32[]{:S(2)}) collective-permute-start(bf16[160,960]{1,0:T(8,128)(2,1)} %pad_maximum_fusion.9), channel_id=1, source_target_pairs={{0,24},{4,28},{8,16},{12,20},{16,8},{20,12},{24,0},{28,4},{1,25},{... | collective-permute-start | bytes 921608 | tf_op jit(solution)/shard_map/ppermute | solution.py:51
  12.4 43.0 %collective-permute-start = (bf16[256,1280]{1,0:T(8,128)(2,1)S(1)}, bf16[256,1280]{1,0:T(8,128)(2,1)}, u32[]{:S(2)}, u32[]{:S(2)}) collective-permute-start(bf16[256,1280]{1,0:T(8,128)(2,1)S(1)} %get-tuple-element.102.refs_8_), channel_id=1, source_target_pairs={{0,4},{4,8},{8,12},{12,16},{16,20},{20,24},{24,28},{1,5},{5,9},{9,... | collective-permute-start | bytes 1966088 | tf_op jit(solution)/shard_map/ppermute | solution.py:292
  25.3 11.6 %collective-permute-start.17 = (bf16[160,960]{1,0:T(8,128)(2,1)}, bf16[160,960]{1,0:T(8,128)(2,1)S(1)}, u32[]{:S(2)}, u32[]{:S(2)}) collective-permute-start(bf16[160,960]{1,0:T(8,128)(2,1)} %collective-permute-done.16), channel_id=1, source_target_pairs={{0,4},{4,0},{8,12},{12,8},{16,20},{20,16},{24,28},{28,24},{1,5},{5... | collective-permute-start | bytes 921608 | tf_op jit(solution)/shard_map/ppermute | solution.py:51
  28.9 30.9 %collective-permute-start.22 = (bf16[320,960]{1,0:T(8,128)(2,1)}, bf16[320,960]{1,0:T(8,128)(2,1)}, u32[]{:S(2)}, u32[]{:S(2)}) collective-permute-start(bf16[320,960]{1,0:T(8,128)(2,1)} %get-tuple-element.131), channel_id=1, source_target_pairs={{0,2},{1,3},{2,0},{3,1},{4,6},{5,7},{6,4},{7,5},{8,10},{9,11},{10,... | collective-permute-start | bytes 1843208 | tf_op jit(solution)/shard_map/ppermute | solution.py:51
  34.2 10.2 %collective-permute-start.19 = (bf16[160,960]{1,0:T(8,128)(2,1)}, bf16[160,960]{1,0:T(8,128)(2,1)S(1)}, u32[]{:S(2)}, u32[]{:S(2)}) collective-permute-start(bf16[160,960]{1,0:T(8,128)(2,1)} %collective-permute-done.18), channel_id=1, source_target_pairs={{0,4},{4,0},{8,12},{12,8},{16,20},{20,16},{24,28},{28,24},{1,5},{5... | collective-permute-start | bytes 921608 | tf_op jit(solution)/shard_map/ppermute | solution.py:51
  34.7 14.4 %collective-permute-start.20 = (bf16[160,960]{1,0:T(8,128)(2,1)}, bf16[160,960]{1,0:T(8,128)(2,1)S(1)}, u32[]{:S(2)}, u32[]{:S(2)}) collective-permute-start(bf16[160,960]{1,0:T(8,128)(2,1)} %collective-permute-done.4), channel_id=1, source_target_pairs={{0,4},{4,0},{8,12},{12,8},{16,20},{20,16},{24,28},{28,24},{1,5},{5... | collective-permute-start | bytes 921608 | tf_op jit(solution)/shard_map/ppermute | solution.py:51
  38.9 43.5 %collective-permute-start.23 = (bf16[320,960]{1,0:T(8,128)(2,1)}, bf16[320,960]{1,0:T(8,128)(2,1)}, u32[]{:S(2)}, u32[]{:S(2)}) collective-permute-start(bf16[320,960]{1,0:T(8,128)(2,1)} %get-tuple-element.129), channel_id=1, source_target_pairs={{0,2},{1,3},{2,0},{3,1},{4,6},{5,7},{6,4},{7,5},{8,10},{9,11},{10,... | collective-permute-start | bytes 1843208 | tf_op jit(solution)/shard_map/ppermute | solution.py:51
  46.4 39.9 %collective-permute-start.24 = (bf16[320,960]{1,0:T(8,128)(2,1)}, bf16[320,960]{1,0:T(8,128)(2,1)}, u32[]{:S(2)}, u32[]{:S(2)}) collective-permute-start(bf16[320,960]{1,0:T(8,128)(2,1)} %get-tuple-element.127), channel_id=1, source_target_pairs={{0,2},{1,3},{2,0},{3,1},{4,6},{5,7},{6,4},{7,5},{8,10},{9,11},{10,... | collective-permute-start | bytes 1843208 | tf_op jit(solution)/shard_map/ppermute | solution.py:51
  51.1 48.4 %collective-permute-start.25 = (bf16[320,960]{1,0:T(8,128)(2,1)}, bf16[320,960]{1,0:T(8,128)(2,1)}, u32[]{:S(2)}, u32[]{:S(2)}) collective-permute-start(bf16[320,960]{1,0:T(8,128)(2,1)} %get-tuple-element.125), channel_id=1, source_target_pairs={{0,2},{1,3},{2,0},{3,1},{4,6},{5,7},{6,4},{7,5},{8,10},{9,11},{10,... | collective-permute-start | bytes 1843208 | tf_op jit(solution)/shard_map/ppermute | solution.py:51
  55.4 19.3 %collective-permute-start.5 = (bf16[160,960]{1,0:T(8,128)(2,1)}, bf16[160,960]{1,0:T(8,128)(2,1)S(1)}, u32[]{:S(2)}, u32[]{:S(2)}) collective-permute-start(bf16[160,960]{1,0:T(8,128)(2,1)} %pad_maximum_fusion.8), channel_id=1, source_target_pairs={{0,4},{4,0},{8,12},{12,8},{16,20},{20,16},{24,28},{28,24},{1,5},{5... | collective-permute-start | bytes 921608 | tf_op jit(solution)/shard_map/ppermute | solution.py:51
  59.8 19.9 %collective-permute-start.6 = (bf16[160,960]{1,0:T(8,128)(2,1)}, bf16[160,960]{1,0:T(8,128)(2,1)}, u32[]{:S(2)}, u32[]{:S(2)}) collective-permute-start(bf16[160,960]{1,0:T(8,128)(2,1)} %pad_maximum_fusion.8), channel_id=1, source_target_pairs={{0,8},{4,12},{8,0},{12,4},{16,24},{20,28},{24,16},{28,20},{1,9},{5... | collective-permute-start | bytes 921608 | tf_op jit(solution)/shard_map/ppermute | solution.py:51
  74.7 24.7 %collective-permute-start.8 = (bf16[160,960]{1,0:T(8,128)(2,1)}, bf16[160,960]{1,0:T(8,128)(2,1)}, u32[]{:S(2)}, u32[]{:S(2)}) collective-permute-start(bf16[160,960]{1,0:T(8,128)(2,1)} %pad_maximum_fusion.8), channel_id=1, source_target_pairs={{0,16},{4,20},{8,24},{12,28},{16,0},{20,4},{24,8},{28,12},{1,17},{... | collective-permute-start | bytes 921608 | tf_op jit(solution)/shard_map/ppermute | solution.py:51
  79.7 28.0 %collective-permute-start.10 = (bf16[160,960]{1,0:T(8,128)(2,1)}, bf16[160,960]{1,0:T(8,128)(2,1)}, u32[]{:S(2)}, u32[]{:S(2)}) collective-permute-start(bf16[160,960]{1,0:T(8,128)(2,1)} %pad_maximum_fusion.8), channel_id=1, source_target_pairs={{0,24},{4,28},{8,16},{12,20},{16,8},{20,12},{24,0},{28,4},{1,25},{... | collective-permute-start | bytes 921608 | tf_op jit(solution)/shard_map/ppermute | solution.py:51
  82.5 26.0 %collective-permute-start.7 = (bf16[160,960]{1,0:T(8,128)(2,1)}, bf16[160,960]{1,0:T(8,128)(2,1)}, u32[]{:S(2)}, u32[]{:S(2)}) collective-permute-start(bf16[160,960]{1,0:T(8,128)(2,1)} %collective-permute-done.6), channel_id=1, source_target_pairs={{0,4},{4,0},{8,12},{12,8},{16,20},{20,16},{24,28},{28,24},{1,5},{5... | collective-permute-start | bytes 921608 | tf_op jit(solution)/shard_map/ppermute | solution.py:51
  86.3 75.1 %collective-permute-start.21 = (bf16[1280,960]{0,1:T(8,128)(2,1)S(1)}, bf16[1280,960]{0,1:T(8,128)(2,1)}, u32[]{:S(2)}, u32[]{:S(2)}) collective-permute-start(bf16[1280,960]{0,1:T(8,128)(2,1)S(1)} %copy-done.17), channel_id=1, source_target_pairs={{0,1},{1,0},{2,3},{3,2},{4,5},{5,4},{6,7},{7,6},{8,9},{9,8},{10,11... | collective-permute-start | bytes 7372808 | tf_op jit(solution)/shard_map/ppermute | solution.py:51
  99.5 27.0 %collective-permute-start.1 = (bf16[256,1280]{1,0:T(8,128)(2,1)}, bf16[256,1280]{1,0:T(8,128)(2,1)}, u32[]{:S(2)}, u32[]{:S(2)}) collective-permute-start(bf16[256,1280]{1,0:T(8,128)(2,1)} %collective-permute-done), channel_id=1, source_target_pairs={{0,1},{1,0},{2,3},{3,2},{4,5},{5,4},{6,7},{7,6},{8,9},{9,8},{10,11... | collective-permute-start | bytes 1966088 | tf_op jit(solution)/shard_map/ppermute | solution.py:51
  99.5 10.9 %collective-permute-start.9 = (bf16[160,960]{1,0:T(8,128)(2,1)}, bf16[160,960]{1,0:T(8,128)(2,1)}, u32[]{:S(2)}, u32[]{:S(2)}) collective-permute-start(bf16[160,960]{1,0:T(8,128)(2,1)} %collective-permute-done.8), channel_id=1, source_target_pairs={{0,4},{4,0},{8,12},{12,8},{16,20},{20,16},{24,28},{28,24},{1,5},{5... | collective-permute-start | bytes 921608 | tf_op jit(solution)/shard_map/ppermute | solution.py:51
  107.7 17.0 %collective-permute-start.2 = (bf16[256,1280]{1,0:T(8,128)(2,1)}, bf16[256,1280]{1,0:T(8,128)(2,1)S(1)}, u32[]{:S(2)}, u32[]{:S(2)}) collective-permute-start(bf16[256,1280]{1,0:T(8,128)(2,1)} %collective-permute-done), channel_id=1, source_target_pairs={{0,2},{1,3},{2,0},{3,1},{4,6},{5,7},{6,4},{7,5},{8,10},{9,11},{10,... | collective-permute-start | bytes 1966088 | tf_op jit(solution)/shard_map/ppermute | solution.py:51
  108.5 9.7 %collective-permute-start.11 = (bf16[160,960]{1,0:T(8,128)(2,1)}, bf16[160,960]{1,0:T(8,128)(2,1)S(1)}, u32[]{:S(2)}, u32[]{:S(2)}) collective-permute-start(bf16[160,960]{1,0:T(8,128)(2,1)} %collective-permute-done.10), channel_id=1, source_target_pairs={{0,4},{4,0},{8,12},{12,8},{16,20},{20,16},{24,28},{28,24},{1,5},{5... | collective-permute-start | bytes 921608 | tf_op jit(solution)/shard_map/ppermute | solution.py:51
  110.4 55.5 %collective-permute-start.26 = (bf16[1280,960]{0,1:T(8,128)(2,1)}, bf16[1280,960]{0,1:T(8,128)(2,1)}, u32[]{:S(2)}, u32[]{:S(2)}) collective-permute-start(bf16[1280,960]{0,1:T(8,128)(2,1)} %copy.65), channel_id=1, source_target_pairs={{0,1},{1,0},{2,3},{3,2},{4,5},{5,4},{6,7},{7,6},{8,9},{9,8},{10,11... | collective-permute-start | bytes 7372808 | tf_op jit(solution)/shard_map/ppermute | solution.py:51
  159.6 10.8 %collective-permute-start.12 = (bf16[256,320]{1,0:T(8,128)(2,1)S(1)}, bf16[256,320]{1,0:T(8,128)(2,1)S(1)}, u32[]{:S(2)}, u32[]{:S(2)}) collective-permute-start(bf16[256,320]{1,0:T(8,128)(2,1)S(1)} %get-tuple-element.120), channel_id=1, source_target_pairs={{0,1},{1,0},{2,3},{3,2},{4,5},{5,4},{6,7},{7,6},{8,9},{9,8},{10,11... | collective-permute-start | bytes 491528 | tf_op jit(solution)/shard_map/ppermute | solution.py:51
  160.1 10.3 %collective-permute-start.13 = (bf16[256,320]{1,0:T(8,128)(2,1)S(1)}, bf16[256,320]{1,0:T(8,128)(2,1)S(1)}, u32[]{:S(2)}, u32[]{:S(2)}) collective-permute-start(bf16[256,320]{1,0:T(8,128)(2,1)S(1)} %get-tuple-element.119), channel_id=1, source_target_pairs={{0,2},{1,3},{2,0},{3,1},{4,6},{5,7},{6,4},{7,5},{8,10},{9,11},{10,... | collective-permute-start | bytes 491528 | tf_op jit(solution)/shard_map/ppermute | solution.py:51
  160.9 9.6 %collective-permute-start.14 = (bf16[256,320]{1,0:T(8,128)(2,1)S(1)}, bf16[256,320]{1,0:T(8,128)(2,1)}, u32[]{:S(2)}, u32[]{:S(2)}) collective-permute-start(bf16[256,320]{1,0:T(8,128)(2,1)S(1)} %get-tuple-element.118), channel_id=1, source_target_pairs={{0,3},{1,2},{2,1},{3,0},{4,7},{5,6},{6,5},{7,4},{8,11},{9,10},{10,... | collective-permute-start | bytes 491528 | tf_op jit(solution)/shard_map/ppermute | solution.py:51
  184.6 14.3 %collective-permute-start.27 = (bf16[256,320]{1,0:T(8,128)(2,1)}, bf16[256,320]{1,0:T(8,128)(2,1)S(1)}, u32[]{:S(2)}, u32[]{:S(2)}) collective-permute-start(bf16[256,320]{1,0:T(8,128)(2,1)} %get-tuple-element.69), channel_id=1, source_target_pairs={{0,1},{1,0},{2,3},{3,2},{4,5},{5,4},{6,7},{7,6},{8,9},{9,8},{10,11... | collective-permute-start | bytes 491528 | tf_op jit(solution)/shard_map/ppermute | solution.py:51
  249.8 57.8 %collective-permute-start.33 = (bf16[4,160,960]{2,1,0:T(8,128)(2,1)}, bf16[4,160,960]{2,1,0:T(8,128)(2,1)}, u32[]{:S(2)}, u32[]{:S(2)}) collective-permute-start(bf16[4,160,960]{2,1,0:T(8,128)(2,1)} %dynamic-slice_bitcast_fusion), channel_id=1, source_target_pairs={{0,4},{4,0},{8,12},{12,8},{16,20},{20,16},{24,28},{28,24},{1,5},{5... | collective-permute-start | bytes 3686408 | tf_op jit(solution)/shard_map/ppermute | solution.py:51
  254.1 57.1 %collective-permute-start.30 = (bf16[2,1024,320]{1,2,0:T(8,128)(2,1)}, bf16[2,1024,320]{1,2,0:T(8,128)(2,1)}, u32[]{:S(2)}, u32[]{:S(2)}) collective-permute-start(bf16[2,1024,320]{1,2,0:T(8,128)(2,1)} %copy.68), channel_id=1, source_target_pairs={{4,0},{8,4},{12,8},{16,12},{20,16},{24,20},{28,24},{5,1},{9,5},{13... | collective-permute-start | bytes 3932168 | tf_op jit(solution)/shard_map/ppermute | solution.py:447
  269.7 68.7 %collective-permute-start.43 = (bf16[2,1280,448]{1,2,0:T(8,128)(2,1)}, bf16[2,1280,448]{1,2,0:T(8,128)(2,1)}, u32[]{:S(2)}, u32[]{:S(2)}) collective-permute-start(bf16[2,1280,448]{1,2,0:T(8,128)(2,1)} %copy.75), channel_id=1, source_target_pairs={{0,1},{1,0},{2,3},{3,2},{4,5},{5,4},{6,7},{7,6},{8,9},{9,8},{10,11... | collective-permute-start | bytes 6881288 | tf_op jit(solution)/shard_map/ppermute | solution.py:51
  270.2 81.8 %collective-permute-start.37 = (bf16[2,1280,512]{2,1,0:T(8,128)(2,1)}, bf16[2,1280,512]{2,1,0:T(8,128)(2,1)}, u32[]{:S(2)}, u32[]{:S(2)}) collective-permute-start(bf16[2,1280,512]{2,1,0:T(8,128)(2,1)} %get-tuple-element.80), channel_id=1, source_target_pairs={{0,1},{1,0},{2,3},{3,2},{4,5},{5,4},{6,7},{7,6},{8,9},{9,8},{10,11... | collective-permute-start | bytes 7864328 | tf_op jit(solution)/shard_map/ppermute | solution.py:51
  311.1 15.1 %collective-permute-start.34 = (bf16[160,960]{1,0:T(8,128)(2,1)S(1)}, bf16[160,960]{1,0:T(8,128)(2,1)S(1)}, u32[]{:S(2)}, u32[]{:S(2)}) collective-permute-start(bf16[160,960]{1,0:T(8,128)(2,1)S(1)} %get-tuple-element.103), channel_id=1, source_target_pairs={{0,8},{4,12},{8,0},{12,4},{16,24},{20,28},{24,16},{28,20},{1,9},{5... | collective-permute-start | bytes 921608 | tf_op jit(solution)/shard_map/ppermute | solution.py:51
  311.2 25.6 %collective-permute-start.35 = (bf16[160,960]{1,0:T(8,128)(2,1)S(1)}, bf16[160,960]{1,0:T(8,128)(2,1)S(1)}, u32[]{:S(2)}, u32[]{:S(2)}) collective-permute-start(bf16[160,960]{1,0:T(8,128)(2,1)S(1)} %get-tuple-element.105), channel_id=1, source_target_pairs={{0,16},{4,20},{8,24},{12,28},{16,0},{20,4},{24,8},{28,12},{1,17},{... | collective-permute-start | bytes 921608 | tf_op jit(solution)/shard_map/ppermute | solution.py:51
  311.2 25.5 %collective-permute-start.36 = (bf16[160,960]{1,0:T(8,128)(2,1)S(1)}, bf16[160,960]{1,0:T(8,128)(2,1)S(1)}, u32[]{:S(2)}, u32[]{:S(2)}) collective-permute-start(bf16[160,960]{1,0:T(8,128)(2,1)S(1)} %get-tuple-element.104), channel_id=1, source_target_pairs={{0,24},{4,28},{8,16},{12,20},{16,8},{20,12},{24,0},{28,4},{1,25},{... | collective-permute-start | bytes 921608 | tf_op jit(solution)/shard_map/ppermute | solution.py:51
  326.2 29.8 %collective-permute-start.31 = (bf16[2,256,1280]{2,1,0:T(8,128)(2,1)}, bf16[2,256,1280]{2,1,0:T(8,128)(2,1)}, u32[]{:S(2)}, u32[]{:S(2)}) collective-permute-start(bf16[2,256,1280]{2,1,0:T(8,128)(2,1)} %pad_maximum_fusion.1), channel_id=1, source_target_pairs={{0,1},{1,0},{2,3},{3,2},{4,5},{5,4},{6,7},{7,6},{8,9},{9,8},{10,11... | collective-permute-start | bytes 3932168 | tf_op jit(solution)/shard_map/ppermute | solution.py:51
  348.4 28.5 %collective-permute-start.44 = (bf16[1280,448]{0,1:T(8,128)(2,1)}, bf16[1280,448]{0,1:T(8,128)(2,1)}, u32[]{:S(2)}, u32[]{:S(2)}) collective-permute-start(bf16[1280,448]{0,1:T(8,128)(2,1)} %copy.78), channel_id=1, source_target_pairs={{0,2},{1,3},{2,0},{3,1},{4,6},{5,7},{6,4},{7,5},{8,10},{9,11},{10,... | collective-permute-start | bytes 3440648 | tf_op jit(solution)/shard_map/ppermute | solution.py:51
  355.1 49.9 %collective-permute-start.38 = (bf16[1280,512]{1,0:T(8,128)(2,1)}, bf16[1280,512]{1,0:T(8,128)(2,1)}, u32[]{:S(2)}, u32[]{:S(2)}) collective-permute-start(bf16[1280,512]{1,0:T(8,128)(2,1)} %fusion.30), channel_id=1, source_target_pairs={{0,2},{1,3},{2,0},{3,1},{4,6},{5,7},{6,4},{7,5},{8,10},{9,11},{10,... | collective-permute-start | bytes 3932168 | tf_op jit(solution)/shard_map/ppermute | solution.py:51
  360.3 55.7 %collective-permute-start.32 = (bf16[256,1280]{1,0:T(8,128)(2,1)S(1)}, bf16[256,1280]{1,0:T(8,128)(2,1)}, u32[]{:S(2)}, u32[]{:S(2)}) collective-permute-start(bf16[256,1280]{1,0:T(8,128)(2,1)S(1)} %fusion.33), channel_id=1, source_target_pairs={{0,2},{1,3},{2,0},{3,1},{4,6},{5,7},{6,4},{7,5},{8,10},{9,11},{10,... | collective-permute-start | bytes 1966088 | tf_op jit(solution)/shard_map/ppermute | solution.py:51
  381.8 36.2 %collective-permute-start.45 = (bf16[4,160,448]{2,1,0:T(8,128)(2,1)S(1)}, bf16[4,160,448]{2,1,0:T(8,128)(2,1)S(1)}, u32[]{:S(2)}, u32[]{:S(2)}) collective-permute-start(bf16[4,160,448]{2,1,0:T(8,128)(2,1)S(1)} %fusion.37), channel_id=1, source_target_pairs={{0,4},{4,0},{8,12},{12,8},{16,20},{20,16},{24,28},{28,24},{1,5},{5... | collective-permute-start | bytes 1720328 | tf_op jit(solution)/shard_map/ppermute | solution.py:51
  407.5 20.9 %collective-permute-start.39 = (bf16[4,160,512]{2,1,0:T(8,128)(2,1)S(1)}, bf16[4,160,512]{2,1,0:T(8,128)(2,1)S(1)}, u32[]{:S(2)}, u32[]{:S(2)}) collective-permute-start(bf16[4,160,512]{2,1,0:T(8,128)(2,1)S(1)} %fusion.36), channel_id=1, source_target_pairs={{0,4},{4,0},{8,12},{12,8},{16,20},{20,16},{24,28},{28,24},{1,5},{5... | collective-permute-start | bytes 1966088 | tf_op jit(solution)/shard_map/ppermute | solution.py:51
  418.3 15.3 %collective-permute-start.46 = (bf16[160,448]{1,0:T(8,128)(2,1)S(1)}, bf16[160,448]{1,0:T(8,128)(2,1)S(1)}, u32[]{:S(2)}, u32[]{:S(2)}) collective-permute-start(bf16[160,448]{1,0:T(8,128)(2,1)S(1)} %get-tuple-element.112), channel_id=1, source_target_pairs={{0,8},{4,12},{8,0},{12,4},{16,24},{20,28},{24,16},{28,20},{1,9},{5... | collective-permute-start | bytes 430088 | tf_op jit(solution)/shard_map/ppermute | solution.py:51
  425.9 15.2 %collective-permute-start.47 = (bf16[160,448]{1,0:T(8,128)(2,1)S(1)}, bf16[160,448]{1,0:T(8,128)(2,1)S(1)}, u32[]{:S(2)}, u32[]{:S(2)}) collective-permute-start(bf16[160,448]{1,0:T(8,128)(2,1)S(1)} %get-tuple-element.114), channel_id=1, source_target_pairs={{0,16},{4,20},{8,24},{12,28},{16,0},{20,4},{24,8},{28,12},{1,17},{... | collective-permute-start | bytes 430088 | tf_op jit(solution)/shard_map/ppermute | solution.py:51
  425.9 15.2 %collective-permute-start.48 = (bf16[160,448]{1,0:T(8,128)(2,1)S(1)}, bf16[160,448]{1,0:T(8,128)(2,1)S(1)}, u32[]{:S(2)}, u32[]{:S(2)}) collective-permute-start(bf16[160,448]{1,0:T(8,128)(2,1)S(1)} %get-tuple-element.113), channel_id=1, source_target_pairs={{0,24},{4,28},{8,16},{12,20},{16,8},{20,12},{24,0},{28,4},{1,25},{... | collective-permute-start | bytes 430088 | tf_op jit(solution)/shard_map/ppermute | solution.py:51
  428.7 12.6 %collective-permute-start.40 = (bf16[160,512]{1,0:T(8,128)(2,1)S(1)}, bf16[160,512]{1,0:T(8,128)(2,1)S(1)}, u32[]{:S(2)}, u32[]{:S(2)}) collective-permute-start(bf16[160,512]{1,0:T(8,128)(2,1)S(1)} %get-tuple-element.115), channel_id=1, source_target_pairs={{0,8},{4,12},{8,0},{12,4},{16,24},{20,28},{24,16},{28,20},{1,9},{5... | collective-permute-start | bytes 491528 | tf_op jit(solution)/shard_map/ppermute | solution.py:51
  429.8 23.5 %collective-permute-start.41 = (bf16[160,512]{1,0:T(8,128)(2,1)S(1)}, bf16[160,512]{1,0:T(8,128)(2,1)S(1)}, u32[]{:S(2)}, u32[]{:S(2)}) collective-permute-start(bf16[160,512]{1,0:T(8,128)(2,1)S(1)} %get-tuple-element.117), channel_id=1, source_target_pairs={{0,16},{4,20},{8,24},{12,28},{16,0},{20,4},{24,8},{28,12},{1,17},{... | collective-permute-start | bytes 491528 | tf_op jit(solution)/shard_map/ppermute | solution.py:51
  433.5 19.7 %collective-permute-start.42 = (bf16[160,512]{1,0:T(8,128)(2,1)S(1)}, bf16[160,512]{1,0:T(8,128)(2,1)S(1)}, u32[]{:S(2)}, u32[]{:S(2)}) collective-permute-start(bf16[160,512]{1,0:T(8,128)(2,1)S(1)} %get-tuple-element.116), channel_id=1, source_target_pairs={{0,24},{4,28},{8,16},{12,20},{16,8},{20,12},{24,0},{28,4},{1,25},{... | collective-permute-start | bytes 491528 | tf_op jit(solution)/shard_map/ppermute | solution.py:51
  456.0 12.9 %all-to-all-start = ((f32[8,16,128]{2,1,0:T(8,128)}), f32[8,16,128]{2,1,0:T(8,128)}, u32[]{:S(2)}, u32[]{:S(2)}) async-start(f32[8,16,128]{2,1,0:T(8,128)} %broadcast_in_dim.26), calls=%async_computation | async-start | bytes 131072 | tf_op jit(solution)/shard_map/all_to_all | solution.py:100
  484.6 11.5 %all-to-all-start.2 = ((f32[32,8,128]{2,1,0:T(8,128)}), f32[32,8,128]{2,1,0:T(8,128)}, u32[]{:S(2)}, u32[]{:S(2)}) async-start(f32[32,8,128]{2,1,0:T(8,128)} %bitcast.177), calls=%async_computation.2 | async-start | bytes 262144 | tf_op jit(solution)/shard_map/all_to_all | solution.py:495
  (57 other events, 604.7 us)

commit v2 on v1

v2 whole, which is shorter than its diff:
```python
import functools
import math

import jax
import jax.numpy as jnp
from jax import lax
from jax.experimental import pallas as pl
from jax.experimental.pallas import tpu as pltpu
from jax.sharding import PartitionSpec as P

HD = 80
WINDOW = 1024
BLOCK = 256
SPAN = WINDOW + BLOCK
LANES = 128

EPSILON = 1e-06
LOG_BASE = 1.442695
BETA_TWO = 0.5
STEP_RATE = 0.3
CLIP_LEVEL = 0.1
VECTOR_RATE = 0.3
NEGATIVE = -1e30
SCALE_ROOT = LOG_BASE / math.sqrt(HD)
MIB = 1024 * 1024

bf16 = jnp.bfloat16
f32 = jnp.float32


def dot(left, right, dims):
    return lax.dot_general(left, right, (dims, ((), ())), preferred_element_type=f32)


def vmem_call(body, outs, scratch, flops, limit, *args):
    size = sum(math.prod(a.shape) * a.dtype.itemsize for a in (*args, *outs))
    space = pl.BlockSpec(memory_space=pltpu.VMEM)
    scalars = pl.BlockSpec(memory_space=pltpu.SMEM)
    return pl.pallas_call(
        body,
        out_shape=outs,
        in_specs=[scalars if a.ndim == 1 else space for a in args],
        out_specs=[space] * len(outs),
        scratch_shapes=scratch,
        compiler_params=pltpu.CompilerParams(vmem_limit_bytes=limit * MIB),
        cost_estimate=pl.CostEstimate(flops=8 * int(flops), bytes_accessed=size, transcendentals=0),
    )(*args)


def hop(value, axis, flip):
    peers = lax.axis_size(axis)
    return lax.ppermute(value, axis, [(i, i ^ flip) for i in range(peers)])


def after(value, *earlier):
    return lax.optimization_barrier((value, *earlier))[0]


def put(table, piece, row):
    return lax.dynamic_update_slice_in_dim(table, piece, row, 0)


def pair_up(piece):
    other = hop(piece, "seq", 1)
    low = lax.axis_index("seq") % 2 == 0
    return jnp.concatenate([jnp.where(low, piece, other), jnp.where(low, other, piece)], axis=0)


def gather_pairs(shard, first, second):
    peers = lax.axis_size("seq")
    pairs = {}
    for f in range(0, peers // 2, 2):
        pairs[f] = pair_up(after(hop(after(shard, first), "seq", 2 * f), first) if f else shard)
    for f in range(0, peers // 2, 2):
        pairs[f + 1] = hop(after(pairs[f], second(f, pairs)), "seq", 2)
    return pairs


def gather_groups(shard):
    peers = lax.axis_size("seq")
    evens = list(range(0, peers // 2, 2))
    groups = [shard[None]]
    if evens[1:]:
        groups.append(jnp.stack([hop(shard, "seq", 2 * f) for f in evens[1:]]))
    others = [hop(group, "seq", 1) for group in groups]
    groups.append(hop(jnp.concatenate(groups, axis=0), "seq", 2))
    others.append(hop(groups[-1], "seq", 1))
    return groups, others, evens + [f + 1 for f in evens]


def scatter_step(total, left, k):
    at = len(left) - 1 - left.index(k)
    bit = (lax.axis_index("seq") >> k) & 1
    send = lax.dynamic_index_in_dim(total, 1 - bit, at, keepdims=False).astype(bf16)
    return send, lax.dynamic_index_in_dim(total, bit, at, keepdims=False)


def scatter_seq(total, left, order, *earlier):
    left = list(left)
    for k in order:
        send, keep = scatter_step(total, left, k)
        send = after(send, *earlier) if k == order[-1] else send
        left.remove(k)
        came = hop(send, "seq", 1 << k)
        if left:
            total = keep.astype(f32) + came.astype(f32)
    return keep, came


def summed(value, axis):
    flip = 1
    while flip < lax.axis_size(axis):
        value = value + hop(value, axis, flip)
        flip *= 2
    return value


def packed(*values):
    flat = jnp.concatenate([v.reshape(-1) for v in values])
    size = -(-flat.shape[0] // 1024) * 1024
    return jnp.pad(flat, (0, size - flat.shape[0])).reshape(size // 128, 128)


def unpacked(table, *shapes):
    flat, out, at = table.reshape(-1), [], 0
    for shape in shapes:
        size = math.prod(shape)
        out.append(flat[at : at + size].reshape(shape))
        at += size
    return out


def head_of(rows, h):
    zeros = jnp.zeros((rows.shape[0], LANES - HD), rows.dtype)
    return jnp.concatenate([rows[:, h * HD : (h + 1) * HD], zeros], axis=1)


def attend_kernel(heads, counts, *refs):
    n_near, n_rim = counts
    at_ref, tok_ref = refs[:2]
    rims = refs[2 : 2 + n_rim]
    near = refs[2 + n_rim : 2 + n_rim + n_near]
    far = refs[2 + n_rim + n_near : 2 + n_rim + 2 * n_near]
    gain_ref, sc_ref, lo_ref = refs[2 + n_rim + 2 * n_near : 5 + n_rim + 2 * n_near]
    h_ref, q_ref, k_ref, v_ref, c_ref, lse_ref, w_ref, kh, vt, bias = refs[5 + n_rim + 2 * n_near :]
    cols = heads * HD
    rows = q_ref.shape[0]

    low, spot = at_ref[0], 1
    for one, two in zip(near, far):
        for i in range(one.shape[0]):
            at = pl.ds(pl.multiple_of(at_ref[spot], 16), 2 * one.shape[1])
            spot += 1

            @pl.when(low == 0)
            def _():
                w_ref[at, :] = jnp.concatenate([one[i], two[i]], axis=0)

            @pl.when(low == 1)
            def _():
                w_ref[at, :] = jnp.concatenate([two[i], one[i]], axis=0)

    def norm(values):
        values = values.astype(f32)
        factor = lax.rsqrt(jnp.mean(values * values, axis=-1, keepdims=True) + EPSILON)
        return (values * factor * gain_ref[...]).astype(bf16)

    for rim in rims:
        share = rim.shape[0]
        h_ref[pl.ds(pl.multiple_of(at_ref[spot], 16), share), :] = norm(rim[...])
        spot += 1
    for i in range(rows // BLOCK):
        h_ref[WINDOW + i * BLOCK : WINDOW + (i + 1) * BLOCK, :] = norm(
            tok_ref[i * BLOCK : (i + 1) * BLOCK, :]
        )

    for i in range(h_ref.shape[0] // BLOCK):
        at = pl.ds(i * BLOCK, BLOCK)
        proj = dot(h_ref[at, :], w_ref[:, : 3 * cols], ((1,), (0,)))
        if i * BLOCK >= WINDOW:
            q_ref[pl.ds(i * BLOCK - WINDOW, BLOCK), :] = (proj[:, :cols] * sc_ref[...]).astype(bf16)
        k_rows = proj[:, cols : 2 * cols].astype(bf16)
        v_rows = proj[:, 2 * cols :].astype(bf16)
        k_ref[at, :] = k_rows
        v_ref[at, :] = v_rows
        vt[:, at] = v_rows.T
        for h in range(heads):
            kh[h, at, :] = head_of(k_rows, h)

    def block(b, carry):
        q0 = pl.multiple_of(b * BLOCK, BLOCK)
        k_place = q0 + lax.broadcasted_iota(jnp.int32, (SPAN, BLOCK), 0)
        q_place = q0 + WINDOW + lax.broadcasted_iota(jnp.int32, (SPAN, BLOCK), 1)
        seen = (k_place >= lo_ref[:, pl.ds(q0, BLOCK)]) & (k_place <= q_place)
        bias[...] = jnp.where(seen, 0.0, NEGATIVE)
        q_rows = q_ref[pl.ds(q0, BLOCK), :]
        mixed = []
        for h in range(heads):
            q_head = head_of(q_rows, h)
            s = dot(kh[h, pl.ds(q0, SPAN), :], q_head, ((1,), (1,))) + bias[...]
            top = jnp.max(s, axis=0, keepdims=True)
            p = jnp.exp(s - top)
            total = jnp.sum(p, axis=0, keepdims=True)
            part = dot(vt[h * HD : (h + 1) * HD, pl.ds(q0, SPAN)], p.astype(bf16), ((1,), (0,)))
            mixed.append((part / total).T)
            lse_ref[pl.ds(h, 1), pl.ds(q0, BLOCK)] = top + jnp.log(total)
        c_ref[pl.ds(q0, BLOCK), :] = jnp.concatenate(mixed, axis=1).astype(bf16)
        return carry

    lax.fori_loop(0, rows // BLOCK, block, 0)


def attend_back_kernel(heads, n_parts, at_ref, *refs):
    parts = refs[:n_parts]
    q_ref, k_ref, v_ref, sc_ref, lo_ref, lse_ref, h_ref = refs[n_parts : n_parts + 7]
    outs = refs[n_parts + 7 :]
    dq_ref, dkv_ref, part_ref = outs[:3]
    send_ref, keep_ref = outs[3:5]
    kh, vh, kt, ht, g_ref, dk, dv, bias = outs[5:]
    rows, cols = q_ref.shape
    for i, part in enumerate(parts):
        share = part.shape[0]
        g_ref[pl.ds(pl.multiple_of(at_ref[1 + i], 16), share), :] = part[...]
    kt[...] = k_ref[...].T
    for h in range(heads):
        kh[h] = head_of(k_ref[...], h)
        vh[h] = head_of(v_ref[...], h)
    dk[...] = jnp.zeros_like(dk)
    dv[...] = jnp.zeros_like(dv)
    part_ref[...] = jnp.zeros_like(part_ref)

    def block(b, carry):
        q0 = pl.multiple_of(b * BLOCK, BLOCK)
        at, keys = pl.ds(q0, BLOCK), pl.ds(q0, SPAN)
        k_place = q0 + lax.broadcasted_iota(jnp.int32, (SPAN, BLOCK), 0)
        q_place = q0 + WINDOW + lax.broadcasted_iota(jnp.int32, (SPAN, BLOCK), 1)
        seen = (k_place >= lo_ref[:, at]) & (k_place <= q_place)
        bias[...] = jnp.where(seen, 0.0, NEGATIVE)
        q_rows, g_rows = q_ref[at, :], g_ref[at, :]
        grads = []
        for h in range(heads):
            q_head = head_of(q_rows, h)
            g_head = head_of(g_rows, h)
            s = dot(kh[h, keys, :], q_head, ((1,), (1,))) + bias[...]
            p = jnp.exp(s - lse_ref[pl.ds(h, 1), at])
            dp = dot(vh[h, keys, :], g_head, ((1,), (1,)))
            inner = jnp.sum(p * dp, axis=0, keepdims=True)
            ds = (p * (dp - inner)).astype(bf16)
            dv[h, keys, :] += dot(p.astype(bf16), g_head, ((1,), (0,)))
            dk[h, keys, :] += dot(ds, q_head, ((1,), (0,)))
            grads.append(dot(kt[h * HD : (h + 1) * HD, keys], ds, ((1,), (0,))).T)
        grad = jnp.concatenate(grads, axis=1)
        part_ref[...] += jnp.sum(grad * q_rows.astype(f32), axis=0, keepdims=True)
        dq_ref[at, :] = (grad * sc_ref[...]).astype(bf16)
        return carry

    lax.fori_loop(0, rows // BLOCK, block, 0)
    for i in range(k_ref.shape[0] // BLOCK):
        at = pl.ds(i * BLOCK, BLOCK)
        both = [table[h, at, :HD] for table in (dk, dv) for h in range(heads)]
        dkv_ref[at, :] = jnp.concatenate(both, axis=1).astype(bf16)
        ht[:, at] = h_ref[at, :].T
    gw_q = dot(ht[:, WINDOW:], dq_ref[...], ((1,), (0,))).astype(bf16)
    gw_kv = dot(ht[...], dkv_ref[...], ((1,), (0,))).astype(bf16)
    outer, own, padded = send_ref.shape
    zeros = jnp.zeros((2 * outer * own, padded - 3 * cols), bf16)
    whole = jnp.concatenate([gw_q, gw_kv, zeros], axis=1)
    for low in range(2):

        @pl.when(at_ref[0] == low)
        def _():
            for i in range(2 * outer):
                to = keep_ref if i % 2 == low else send_ref
                to[i // 2] = whole[i * own : (i + 1) * own]


def rows_kernel(parts, at_ref, q_ref, kv_ref, w_ref, even_ref, odd_ref):
    cols, width = q_ref.shape[1], w_ref.shape[0]
    share = even_ref.shape[1]
    for f in range(parts):
        at = pl.multiple_of(at_ref[f], 16)
        here = pl.ds(pl.multiple_of(at + WINDOW, 16), share)
        to = odd_ref if f % 2 else even_ref
        grads = jnp.concatenate([q_ref[pl.ds(at, share), :], kv_ref[here, :]], axis=1)
        to[f // 2, :, width:] = dot(grads, w_ref[:, : 3 * cols], ((1,), (1,))).astype(bf16)
        to[f // 2, :, :width] = dot(
            kv_ref[pl.ds(at, share), :], w_ref[:, cols : 3 * cols], ((1,), (1,))
        ).astype(bf16)


def rows_kernel(parts, at_ref, q_ref, kv_ref, w_ref, even_ref, odd_ref):
    cols, width = q_ref.shape[1], w_ref.shape[0]
    share = even_ref.shape[1]
    for f in range(parts):
        at = pl.multiple_of(at_ref[f], 16)
        here = pl.ds(pl.multiple_of(at + WINDOW, 16), share)
        to = odd_ref if f % 2 else even_ref
        grads = jnp.concatenate([q_ref[pl.ds(at, share), :], kv_ref[here, :]], axis=1)
        to[f // 2, :, width:] = dot(grads, w_ref[:, : 3 * cols], ((1,), (1,))).astype(bf16)
        to[f // 2, :, :width] = dot(
            kv_ref[pl.ds(at, share), :], w_ref[:, cols : 3 * cols], ((1,), (1,))
        ).astype(bf16)


def share_kernel(counts, at_ref, *refs):
    peers = len(counts)
    ctx, refs = refs[:peers], refs[peers:]
    mats = [refs[sum(counts[:r]) : sum(counts[: r + 1])] for r in range(peers)]
    refs = refs[sum(counts) :]
    x_ref, cot_ref, gain_ref = refs[:3]
    outs = refs[3:]
    res_ref, gmid_ref, part_ref, rows_ref, even_ref, odd_ref = outs[:6]
    gctx = outs[6 : 6 + peers]
    w_out, w_in, w_back = outs[6 + peers :]
    cols = ctx[0].shape[1]
    for r, pieces in enumerate(mats):
        for i, (m, k) in enumerate((m, k) for m in pieces for k in range(m.shape[0])):
            at = pl.ds(pl.multiple_of(at_ref[i], 16), m.shape[1])
            for j, w in enumerate((w_out, w_in, w_back)):
                w[at, r * cols : (r + 1) * cols] = m[k, :, j * cols : (j + 1) * cols]
    gain = gain_ref[...]
    mixed = jnp.concatenate([c[...] for c in ctx], axis=1)
    mid = x_ref[...].astype(f32) + dot(mixed, w_out[...], ((1,), (1,)))
    factor = lax.rsqrt(jnp.mean(mid * mid, axis=-1, keepdims=True) + EPSILON)
    normed = mid * factor
    h2 = (normed * gain).astype(bf16)
    rows_ref[1] = h2
    cot = cot_ref[...]
    pre = dot(h2, w_in[...], ((1,), (0,)))
    g_hid = dot(cot, w_back[...], ((1,), (0,)))
    sig = 1.0 / (1.0 + jnp.exp(-pre))
    hidden = (pre * sig).astype(bf16)
    g_pre = (g_hid * sig * (1.0 + pre * (1.0 - sig))).astype(bf16)
    for r in range(peers):
        half, to = odd_ref if r % 2 else even_ref, slice(r // 2 * cols, (r // 2 + 1) * cols)
        half[0, :, to] = g_pre[:, r * cols : (r + 1) * cols]
        half[1, :, to] = hidden[:, r * cols : (r + 1) * cols]
    res_ref[...] = mid + dot(hidden, w_back[...], ((1,), (1,)))
    g_h2 = dot(g_pre, w_in[...], ((1,), (1,)))
    part_ref[...] = jnp.sum(g_h2 * normed, axis=0, keepdims=True)
    scaled = g_h2 * gain
    back = factor * (scaled - normed * jnp.mean(scaled * normed, axis=-1, keepdims=True))
    g_mid = cot.astype(f32) + back
    gmid_ref[...] = g_mid
    gm = g_mid.astype(bf16)
    rows_ref[0] = gm
    g_mixed = dot(gm, w_out[...], ((1,), (0,))).astype(bf16)
    for r, out in enumerate(gctx):
        out[...] = g_mixed[:, r * cols : (r + 1) * cols]


def share_grads_kernel(count, at_ref, *refs):
    ctx, ctx_far = refs[:count], refs[count]
    rows_ref, rows_far, even_ref, odd_far, cot_ref, cot_far = refs[count + 1 : count + 7]
    firsts, send_ref, keep_ref = refs[count + 7 : 2 * count + 7], *refs[2 * count + 7 :]
    lefts = [
        jnp.concatenate([one.T, two.T], axis=1)
        for one, two in (
            (rows_ref[0], rows_far[0]),
            (rows_ref[1], rows_far[1]),
            (cot_ref[...], cot_far[...]),
        )
    ]
    half, cols = firsts[0].shape[-1], ctx[0].shape[1]
    zeros = jnp.zeros((firsts[0].shape[0], 2 * half - 3 * cols), bf16)
    pairs, rows = send_ref.shape[1:3]
    for r in range(count):
        to = slice(r * cols, (r + 1) * cols)
        rights = (
            (ctx[r][...], ctx_far[:, to]),
            (even_ref[0, :, to], odd_far[0, :, to]),
            (even_ref[1, :, to], odd_far[1, :, to]),
        )
        parts = [
            dot(left, jnp.concatenate(right, axis=0), ((1,), (0,))).astype(bf16)
            for left, right in zip(lefts, rights)
        ]
        whole = jnp.concatenate([*parts, zeros], axis=1)
        firsts[r][...] = whole[:, :half]
        for bit, (zero, one) in enumerate(((keep_ref, send_ref), (send_ref, keep_ref))):

            @pl.when(at_ref[0] == bit)
            def _():
                for i in range(pairs):
                    zero[r, i] = whole[2 * i * rows : (2 * i + 1) * rows, half:]
                    one[r, i] = whole[(2 * i + 1) * rows : (2 * i + 2) * rows, half:]


def grads_kernel(keep_w, came_w, keep_m, came_m, qkv_ref, out_ref, mlp_ref, col_ref, row_ref):
    cols = out_ref.shape[1]
    col_ref[...] = jnp.zeros_like(col_ref)
    row_sums = []
    for i, (keep, came) in enumerate(((keep_w, came_w), (keep_m, came_m))):
        total = keep[...].astype(f32) + came[...].astype(f32)
        for j in range(3):
            grad = total[:, j * cols : (j + 1) * cols]
            if i == 0:
                qkv_ref[j] = grad
            elif j == 0:
                out_ref[...] = grad
            else:
                mlp_ref[j - 1] = grad
            square = grad * grad
            col_ref[3 * i + j : 3 * i + j + 1, :] = jnp.sum(square, axis=0, keepdims=True)
            row_sums.append(jnp.sum(square, axis=1, keepdims=True))
    zeros = jnp.zeros((row_sums[0].shape[0], LANES - 6), f32)
    row_ref[...] = jnp.concatenate([*row_sums, zeros], axis=1).T[:8, :]


def update_kernel(sizes, qkv_ref, out_ref, mlp_ref, col_ref, row_ref, cs_ref, rs_ref, cn_ref, rn_ref, up_ref, sq_ref):
    total_cols, width = sizes
    col_new = BETA_TWO * cs_ref[...] + (1.0 - BETA_TWO) * col_ref[:6, :] / width
    row_new = BETA_TWO * rs_ref[...] + (1.0 - BETA_TWO) * row_ref[:6, :] / total_cols
    cn_ref[...] = col_new
    rn_ref[...] = row_new
    rows = row_new.shape[1]
    row_cols = jnp.concatenate([row_new, jnp.ones((2, rows), f32)], axis=0).T
    sq_ref[...] = jnp.zeros_like(sq_ref)
    for i in range(6):
        grad = qkv_ref[i] if i < 3 else out_ref[...] if i == 3 else mlp_ref[i - 4]
        update = grad * lax.rsqrt(row_cols[:, i : i + 1] * col_new[i : i + 1, :])
        up_ref[i] = update
        sq_ref[i : i + 1, :] = jnp.sum(update * update, axis=0, keepdims=True)


def step_kernel(up_ref, step_ref, qkv_ref, out_ref, mlp_ref, qkv_new, out_new, mlp_new):
    for i in range(6):
        old, new = (qkv_ref, qkv_new) if i < 3 else (mlp_ref, mlp_new)
        change = step_ref[i : i + 1, :] * up_ref[i]
        if i == 3:
            out_new[...] = out_ref[...] - change
        else:
            new[i % 4] = old[i % 4] - change


def shards(
    tokens,
    cotangent,
    lengths,
    qkv,
    out_proj,
    mlp,
    gains,
    query_scale,
    row_second,
    col_second,
    gain_second,
    scale_second,
):
    n_tensor, n_seq = lax.axis_size("tensor"), lax.axis_size("seq")
    seq_index, ten_index = lax.axis_index("seq"), lax.axis_index("tensor")
    tok_dev, width = tokens.shape
    share = cotangent.shape[0]
    rows_own, cols_own = qkv.shape[1], qkv.shape[2]
    heads = cols_own // HD
    row_first = ten_index * share
    flips = list(range(n_tensor))
    sds = jax.ShapeDtypeStruct

    x_share = lax.dynamic_slice_in_dim(tokens, row_first, share, 0)

    padded = -(-3 * cols_own // 256) * 256
    fill = jnp.zeros((rows_own, padded - 3 * cols_own), f32)
    shard_m = jnp.concatenate([out_proj, mlp[0], mlp[1], fill], axis=1).astype(bf16)
    shard_qkv = jnp.concatenate([qkv[0], qkv[1], qkv[2], fill], axis=1).astype(bf16)
    near, far, flips_q = gather_groups(shard_qkv)
    rim_own = lax.ppermute(x_share, "seq", [(i, i + 1) for i in range(n_seq - 1)])
    rims = [rim_own] + [hop(rim_own, "tensor", f) for f in flips[2::2]]
    flips_rim = flips[::2] + flips[1::2]
    rims = rims + [hop(piece, "tensor", 1) for piece in rims]
    across = {f: {} for f in flips[2::2]}

    def send_across(g, pairs, *earlier):
        for f in across:
            across[f][g] = hop(after(pairs[g], *earlier), "tensor", f)
        return [across[f][g] for f in across]

    def second(f, pairs):
        if not f:
            send_across(0, pairs)
            return near[-1], far[1]
        return send_across(f, pairs, rims[: n_tensor // 2])

    pairs_m = gather_pairs(shard_m, (near[1], far[0]), second)
    for g in pairs_m:
        if g % 2:
            send_across(g, pairs_m, list(across[flips[2]].values())[-1])
    flips_m = list(pairs_m)
    mats = {0: [jnp.stack([pairs_m[g] for g in flips_m])]}
    mats[1] = [hop(mats[0][0], "tensor", 1)]
    for f in across:
        mats[f] = [across[f][g][None] for g in flips_m]
    low, outer = seq_index % 2, seq_index // 2
    spots_share = [(ten_index ^ f) * share for f in flips]
    spots_q = [(outer ^ f) * 2 * rows_own for f in flips_q]
    spots_rim = [(ten_index ^ f) * share for f in flips_rim]
    spots_m = [(outer ^ f) * 2 * rows_own for f in flips_m]

    places = seq_index * tok_dev + jnp.arange(tok_dev, dtype=jnp.int32)
    ends = jnp.cumsum(lengths[0])
    passed = ends[None, :] <= places[:, None]
    doc_start = jnp.max(jnp.where(passed, ends[None, :], 0), axis=1)
    lo = jnp.maximum(places - (WINDOW - 1), doc_start)
    lo = jnp.where(places >= ends[-1], places, lo)
    lo = (lo - (seq_index * tok_dev - WINDOW)).astype(jnp.int32)[None, :]

    factor = jax.nn.softplus(query_scale) * SCALE_ROOT
    scale_cols = jnp.tile(factor, heads)[None, :]
    table = WINDOW + tok_dev
    pair_flops = tok_dev * SPAN * cols_own * 2
    h_all, queries, key_rows, value_rows, context, log_totals, w_qkv = vmem_call(
        functools.partial(attend_kernel, heads, (len(near), len(rims))),
        (
            sds((table, width), bf16),
            sds((tok_dev, cols_own), bf16),
            sds((table, cols_own), bf16),
            sds((table, cols_own), bf16),
            sds((tok_dev, cols_own), bf16),
            sds((heads, tok_dev), f32),
            sds((width, padded), bf16),
        ),
        [
            pltpu.VMEM((heads, table, LANES), bf16),
            pltpu.VMEM((cols_own, table), bf16),
            pltpu.VMEM((SPAN, BLOCK), f32),
        ],
        2 * table * width * 3 * cols_own + 6 * pair_flops,
        44,
        jnp.stack([low, *spots_q, *spots_rim]),
        tokens,
        *rims,
        *near,
        *far,
        gains[:1],
        scale_cols,
        lo,
    )

    for f in flips[2::2]:
        mats[f + 1] = [hop(after(piece, context), "tensor", 1) for piece in mats[f]]

    def share_of(values, f):
        return lax.dynamic_slice_in_dim(values, (ten_index ^ f) * share, share, 0)

    ctx = [share_of(context, f) for f in flips]
    ctx = [ctx[0]] + [hop(ctx[f], "tensor", f) for f in flips[1:]]
    shape_share = (share, width)
    outs = vmem_call(
        functools.partial(share_kernel, [len(mats[f]) for f in flips]),
        (
            sds(shape_share, f32),
            sds(shape_share, f32),
            sds((1, width), f32),
            sds((2, share, width), bf16),
            sds((2, share, n_tensor // 2 * cols_own), bf16),
            sds((2, share, n_tensor // 2 * cols_own), bf16),
            *[sds((share, cols_own), bf16) for _ in flips],
        ),
        [pltpu.VMEM((width, width), bf16) for _ in range(3)],
        2 * 6 * share * width * width,
        44,
        jnp.stack(spots_m),
        *ctx,
        *[piece for f in flips for piece in mats[f]],
        x_share,
        cotangent,
        gains[1:],
    )
    result, grad_mid, gain_two_grad, rows_two, even, odd = outs[:6]
    gctx = outs[6:]
    gctx = [gctx[0]] + [hop(gctx[f], "tensor", f) for f in flips[1:]]

    n_even, half = n_tensor // 2, padded // 2
    halves = sds((n_even, n_seq // 4, 2 * rows_own, half), bf16)
    *firsts, send, keep = vmem_call(
        functools.partial(share_grads_kernel, n_even),
        (*[sds((width, half), bf16) for _ in range(n_even)], halves, halves),
        [],
        2 * 3 * share * width * width,
        44,
        (outer % 2)[None],
        *ctx[::2],
        hop(jnp.concatenate(ctx[1::2], axis=1), "tensor", 1),
        rows_two,
        hop(rows_two, "tensor", 1),
        even,
        hop(odd, "tensor", 1),
        cotangent,
        hop(cotangent, "tensor", 1),
    )
    came = [hop(part, "tensor", 2 * i) for i, part in enumerate(firsts) if i]
    turned = hop(send, "seq", 2)
    log_totals, _ = lax.optimization_barrier((log_totals, firsts + [send]))

    grad_q, grad_kv, scale_raw, *grad_w = vmem_call(
        functools.partial(attend_back_kernel, heads, n_tensor),
        (
            sds((tok_dev, cols_own), bf16),
            sds((table, 2 * cols_own), bf16),
            sds((1, cols_own), f32),
            *[sds((n_seq // 2, rows_own, padded), bf16) for _ in range(2)],
        ),
        [
            pltpu.VMEM((heads, table, LANES), bf16),
            pltpu.VMEM((heads, table, LANES), bf16),
            pltpu.VMEM((cols_own, table), bf16),
            pltpu.VMEM((width, table), bf16),
            pltpu.VMEM((tok_dev, cols_own), bf16),
            pltpu.VMEM((heads, table, LANES), f32),
            pltpu.VMEM((heads, table, LANES), f32),
            pltpu.VMEM((SPAN, BLOCK), f32),
        ],
        14 * pair_flops + 2 * table * width * 3 * cols_own,
        56,
        jnp.stack([low, *spots_share]),
        *gctx,
        queries,
        key_rows,
        value_rows,
        scale_cols,
        lo,
        log_totals,
        h_all,
    )
    scale_part = (
        jnp.sum((scale_raw / scale_cols).reshape(heads, HD), axis=0)
        * SCALE_ROOT
        * jax.nn.sigmoid(query_scale)
    )
    bits = n_seq.bit_length() - 1
    part_rows = sds((n_even, share, 2 * width), bf16)
    even_rows, odd_rows = vmem_call(
        functools.partial(rows_kernel, n_tensor),
        (part_rows, part_rows),
        [],
        2 * (tok_dev * 5 * cols_own) * width,
        44,
        jnp.stack(spots_share),
        grad_q,
        grad_kv,
        w_qkv,
    )
    turned_w = hop(grad_w[0], "seq", 1)
    from_core_rows = hop(odd_rows, "tensor", 1)

    first = firsts[0].astype(f32)
    for part in came:
        first = first + part.astype(f32)
    first = first.reshape(*[2] * bits, rows_own, half)
    send, keep_first = scatter_step(first, list(range(bits)), 1)
    second = keep.astype(f32) + turned.astype(f32)
    sends = [second[i].astype(bf16) for i in range(1, n_even)]
    came_first = hop(send, "seq", 2)
    far_second = [hop(part, "tensor", 2 * i + 2) for i, part in enumerate(sends)]
    from_core_rows = after(from_core_rows, far_second)
    sums = [even_rows[i].astype(f32) + from_core_rows[i].astype(f32) for i in range(n_even)]
    sum_sends = [part.astype(bf16) for part in sums[1:]]

    rest = [0, *range(2, bits)]
    first = keep_first + came_first.astype(f32)
    second = second[0]
    for part in far_second:
        second = second + part.astype(f32)
    second = second.reshape(*[2] * (bits - 1), rows_own, half)
    both = jnp.concatenate([first, second], axis=-1)
    far_rim = [hop(part[:, :width], "tensor", 2 * i + 2) for i, part in enumerate(sum_sends)]
    rim_one, grad_one = sums[0][:, :width], sums[0][:, width:]
    for part in far_rim:
        rim_one = rim_one + part.astype(f32)
    far_here = [
        hop(after(part[:, width:], far_rim), "tensor", 2 * i + 2)
        for i, part in enumerate(sum_sends)
    ]
    for part in far_here:
        grad_one = grad_one + part.astype(f32)
    high = list(range(1, bits))
    own_qkv = grad_w[1].astype(f32) + after(turned_w, sum_sends, came_first).astype(f32)
    own_qkv = own_qkv.reshape(*[2] * (bits - 1), *own_qkv.shape[1:])
    keep_m, came_m = scatter_seq(both, rest, rest[::-1])
    keep_w, came_w = scatter_seq(own_qkv, high, high, far_rim)
    back = lax.ppermute(rim_one.astype(bf16), "seq", [(i, i - 1) for i in range(1, n_seq)])
    grad_one = grad_one + back.astype(f32)
    came_w = after(came_w, back)
    x_part = x_share.astype(f32)
    factor_one = lax.rsqrt(jnp.mean(x_part * x_part, axis=-1, keepdims=True) + EPSILON)
    norm_one = x_part * factor_one
    gain_one_grad = jnp.sum(grad_one * norm_one, axis=0)
    scaled = grad_one * gains[0]
    tokens_grad = grad_mid + factor_one * (
        scaled - norm_one * jnp.mean(scaled * norm_one, axis=-1, keepdims=True)
    )

    total_cols = cols_own * n_tensor
    shape_w = (sds((3, rows_own, cols_own), f32), sds((rows_own, cols_own), f32))
    shape_w = (*shape_w, sds((2, rows_own, cols_own), f32))
    *grads, col_part, row_part = vmem_call(
        grads_kernel,
        (*shape_w, sds((8, cols_own), f32), sds((8, rows_own), f32)),
        [],
        1e9,
        32,
        keep_w,
        came_w,
        keep_m,
        came_m,
    )
    col_new, row_new, unscaled, unscaled_part = vmem_call(
        functools.partial(update_kernel, (total_cols, width)),
        (
            sds((6, cols_own), f32),
            sds((6, rows_own), f32),
            sds((6, rows_own, cols_own), f32),
            sds((6, cols_own), f32),
        ),
        [],
        1e9,
        32,
        *grads,
        summed(col_part, "seq"),
        summed(row_part, "tensor"),
        col_second,
        row_second,
    )

    gain_part = jnp.stack([gain_one_grad, gain_two_grad[0]])
    gain_part = gain_part.reshape(2, n_seq, rows_own).transpose(1, 0, 2).reshape(n_seq, 2 * rows_own)
    rest = jnp.concatenate(
        [
            scale_part,
            jnp.sum(unscaled_part, axis=1),
            jnp.sum(row_part[:6], axis=1),
            jnp.sum(row_second, axis=1) / n_tensor,
        ]
    )
    rest = jnp.broadcast_to(rest, (n_seq, HD + 18))
    last = jnp.concatenate([gain_part, rest], axis=1)
    size = -(-last.shape[1] // 1024) * 1024
    last = jnp.pad(last, ((0, 0), (0, size - last.shape[1]))).reshape(n_seq, 1, size // 128, 128)
    last = jnp.broadcast_to(last, (n_seq, n_tensor, size // 128, 128))
    last = last.reshape(n_seq * n_tensor, size // 128, 128)
    got = lax.all_to_all(last, ("seq", "tensor"), split_axis=0, concat_axis=0)
    gains_grad, scale_grad, unscaled_square, all_square, old_sums = unpacked(
        jnp.sum(got, axis=0), (2, rows_own), (HD,), (6,), (6,), (6,)
    )
    row_mean = (BETA_TWO * old_sums + (1.0 - BETA_TWO) * all_square / total_cols) / width
    update_rms = jnp.sqrt(row_mean * unscaled_square / (width * total_cols))
    step = STEP_RATE * jnp.sqrt(row_mean) / jnp.maximum(1.0, update_rms / CLIP_LEVEL)
    fresh = vmem_call(
        step_kernel,
        shape_w,
        [],
        1e9,
        32,
        unscaled,
        jnp.broadcast_to(step[:, None], (6, cols_own)),
        qkv,
        out_proj,
        mlp,
    )
    gains_own = lax.dynamic_slice_in_dim(gains, seq_index * rows_own, rows_own, 1)
    gain_second_new = BETA_TWO * gain_second + (1.0 - BETA_TWO) * gains_grad * gains_grad
    gains_new = gains_own - VECTOR_RATE * gains_grad * lax.rsqrt(gain_second_new)
    scale_second_new = BETA_TWO * scale_second + (1.0 - BETA_TWO) * scale_grad * scale_grad
    scale_new = query_scale - VECTOR_RATE * scale_grad * lax.rsqrt(scale_second_new)
    return (
        result,
        tokens_grad,
        *grads,
        gains_grad,
        scale_grad,
        *fresh,
        gains_new,
        scale_new,
        row_new,
        col_new,
        update_rms,
        gain_second_new,
        scale_second_new,
    )


def solution(mesh):
    return jax.shard_map(
        shards,
        mesh=mesh,
        in_specs=(
            P("seq", None),
            P(("seq", "tensor"), None),
            P(),
            P(None, "seq", "tensor"),
            P("seq", "tensor"),
            P(None, "seq", "tensor"),
            P(),
            P(),
            P(None, "seq"),
            P(None, "tensor"),
            P(None, "seq"),
            P(),
        ),
        out_specs=(
            P(("seq", "tensor"), None),
            P(("seq", "tensor"), None),
            P(None, "seq", "tensor"),
            P("seq", "tensor"),
            P(None, "seq", "tensor"),
            P(None, "seq"),
            P(),
            P(None, "seq", "tensor"),
            P("seq", "tensor"),
            P(None, "seq", "tensor"),
            P(None, "seq"),
            P(),
            P(None, "seq"),
            P(None, "tensor"),
            P(),
            P(None, "seq"),
            P(),
        ),
        check_vma=False,
    )
```

time: 508 us -> 353 us (0.69)
  local copies, waits for them, and re-layouts: 87 us -> 23.2 us
  other arithmetic: 74.4 us -> 30.8 us
  waiting for transfers between devices: 162 us -> 129 us
  Pallas kernels: 72.3 us -> 89.2 us
  starting transfers between devices: 91.6 us -> 75.2 us
  matrix products: 13.7 us -> 0 us
    ppermute x47 -> x49, waiting for transfers between devices: 149 us -> 124 us  [hop(): return lax.ppermute(value, axis, [(i, i ^ flip) for i in range(peers)])]
    dynamic_update_slice x15 -> x0, local copies, waits for them, and re-layouts: 21.3 us -> none  [put(): return lax.dynamic_update_slice_in_dim(table, piece, row, 0)]
    pallas_call x4 -> x8, Pallas kernels: 72.3 us -> 89.2 us  [vmem_call(): pl.pallas_call(body, out_shape=outs, in_specs=[scalars if a.ndim == 1 els...]
    dot_general x4 -> x0, matrix products: 13.7 us -> none  [dot(): lax.dot_general(left, right, (dims, ((), ())), preferred_element_type=f32)]
    ppermute x4 -> x0, local copies, waits for them, and re-layouts: 13.2 us -> none  [the longest x3 11.4 us: hop(): return lax.ppermute(value, axis, [(i, i ^ flip) for i in range(peers)])]
    convert_element_type x6 -> x3, other arithmetic: 14.1 us -> 2.57 us  [the longest x1 2.31 us: shards(): sum_sends = [part.astype(bf16) for part in sums[1:]]]
    all_to_all x2 -> x0, starting transfers between devices: 9.77 us -> none  [spread(): lax.all_to_all(jnp.broadcast_to(payload, (peers, *payload.shape)), axis,...]
    dot_general x1 -> x0, local copies, waits for them, and re-layouts: 8.38 us -> none  [dot(): lax.dot_general(left, right, (dims, ((), ())), preferred_element_type=f32)]
  transfers between devices with their start and end apart: 52 -> 52, of which waited for: 20 -> 24; matrix products, arithmetic and copies ran while one was open for 26% -> 9% of each run, Pallas kernels for 7% -> 22%
where the time goes in v2:
time: 353 us; the launch traced here: 349 us
  waiting for transfers between devices  129 us (37%)
  Pallas kernels  89.2 us (25%)
  starting transfers between devices  75.2 us (21%)
  other arithmetic  30.8 us (9%)
  local copies, waits for them, and re-layouts  23.2 us (7%)
    ppermute x49, waiting for transfers between devices, hop(): return lax.ppermute(value, axis, [(i, i ^ flip) for i in range(peers)])  124 us
    pallas_call x8, Pallas kernels, vmem_call(): pl.pallas_call(body, out_shape=outs, in_specs=[scalars if a.ndim == 1 els...  89.2 us
    ppermute x49, starting transfers between devices, hop(): return lax.ppermute(value, axis, [(i, i ^ flip) for i in range(peers)])  68.6 us
    unnamed x110, local copies, waits for them, and re-layouts  16.2 us
  transfers between devices with their start and end apart: 52, of which 24 were waited for; matrix products, arithmetic and copies ran while one was open for 9% of the time, Pallas kernels for 22%

profile of v2, /device:TPU:0, one launch (start us, length us, event | category | flops | bytes accessed | tf_op | source)
XLA Modules:
  0.0 348.6 jit_solution(10047248277370740956)
XLA Ops:
  3.4 4.1 %collective-permute-start.4 = (bf16[160,1024]{1,0:T(8,128)(2,1)S(1)}, bf16[160,1024]{1,0:T(8,128)(2,1)S(1)}, u32[]{:S(2)}, u32[]{:S(2)}) collective-permute-start(bf16[160,1024]{1,0:T(8,128)(2,1)S(1)} %get-tuple-element.167), channel_id=1, source_target_pairs={{0,16},{4,20},{8,24},{12,28},{16,0},{20,4},{24,8},{28,12},{1,17},{... | collective-permute-start | bytes 983048 | tf_op jit(solution)/shard_map/ppermute | solution.py:52
  7.6 1.6 collective-permute-start.6
  9.2 1.9 fusion.8
  11.1 2.4 collective-permute-start
  13.5 2.6 collective-permute-start.12
  16.1 6.1 %collective-permute-done.4 = bf16[160,1024]{1,0:T(8,128)(2,1)S(1)} collective-permute-done((bf16[160,1024]{1,0:T(8,128)(2,1)S(1)}, bf16[160,1024]{1,0:T(8,128)(2,1)S(1)}, u32[]{:S(2)}, u32[]{:S(2)}) %collective-permute-start.4) | collective-permute-done | bytes 327712 | tf_op jit(solution)/shard_map/ppermute | solution.py:52
  23.9 11.7 %collective-permute-start.5 = (bf16[2,160,1024]{2,1,0:T(8,128)(2,1)}, bf16[2,160,1024]{2,1,0:T(8,128)(2,1)S(1)}, u32[]{:S(2)}, u32[]{:S(2)}) collective-permute-start(bf16[2,160,1024]{2,1,0:T(8,128)(2,1)} %pad_maximum_fusion.1), channel_id=1, source_target_pairs={{0,8},{4,12},{8,0},{12,4},{16,24},{20,28},{24,16},{28,20},{1,9},{5... | collective-permute-start | bytes 1966088 | tf_op jit(solution)/shard_map/ppermute | solution.py:52
  36.4 1.9 collective-permute-start.14
  42.0 3.4 collective-permute-done.7.refs_10_
  45.5 2.7 collective-permute-done.5.refs_8_
  48.2 8.3 %collective-permute-start.15 = (bf16[320,1024]{1,0:T(8,128)(2,1)}, bf16[320,1024]{1,0:T(8,128)(2,1)}, u32[]{:S(2)}, u32[]{:S(2)}) collective-permute-start(bf16[320,1024]{1,0:T(8,128)(2,1)} %get-tuple-element.77), channel_id=1, source_target_pairs={{0,8},{4,12},{8,0},{12,4},{16,24},{20,28},{24,16},{28,20},{1,9},{5... | collective-permute-start | bytes 1966088 | tf_op jit(solution)/shard_map/ppermute | solution.py:52
  60.2 11.0 %collective-permute-done.15 = bf16[320,1024]{1,0:T(8,128)(2,1)} collective-permute-done((bf16[320,1024]{1,0:T(8,128)(2,1)}, bf16[320,1024]{1,0:T(8,128)(2,1)}, u32[]{:S(2)}, u32[]{:S(2)}) %collective-permute-start.15) | collective-permute-done | bytes 655392 | tf_op jit(solution)/shard_map/ppermute | solution.py:52
  71.2 3.5 %collective-permute-done.16 = bf16[320,1024]{1,0:T(8,128)(2,1)S(1)} collective-permute-done((bf16[320,1024]{1,0:T(8,128)(2,1)}, bf16[320,1024]{1,0:T(8,128)(2,1)S(1)}, u32[]{:S(2)}, u32[]{:S(2)}) %collective-permute-start.16) | collective-permute-done | bytes 655392 | tf_op jit(solution)/shard_map/ppermute | solution.py:52
  75.2 12.0 %collective-permute-start.17 = (bf16[320,1024]{1,0:T(8,128)(2,1)}, bf16[320,1024]{1,0:T(8,128)(2,1)S(1)}, u32[]{:S(2)}, u32[]{:S(2)}) collective-permute-start(bf16[320,1024]{1,0:T(8,128)(2,1)} %get-tuple-element.79), channel_id=1, source_target_pairs={{0,8},{4,12},{8,0},{12,4},{16,24},{20,28},{24,16},{28,20},{1,9},{5... | collective-permute-start | bytes 1966088 | tf_op jit(solution)/shard_map/ppermute | solution.py:52
  90.3 9.7 %collective-permute-done.17 = bf16[320,1024]{1,0:T(8,128)(2,1)S(1)} collective-permute-done((bf16[320,1024]{1,0:T(8,128)(2,1)}, bf16[320,1024]{1,0:T(8,128)(2,1)S(1)}, u32[]{:S(2)}, u32[]{:S(2)}) %collective-permute-start.17) | collective-permute-done | bytes 655392 | tf_op jit(solution)/shard_map/ppermute | solution.py:52
  100.6 1.9 pad_maximum_fusion.refs_4_
  102.6 1.9 collective-permute-done.8.refs_11_
  104.6 24.3 %shard_map.251 = (bf16[2048,1280]{1,0:T(8,128)(2,1)}, bf16[1024,320]{1,0:T(8,128)(2,1)S(1)}, bf16[2048,320]{1,0:T(8,128)(2,1)S(1)}, bf16[2048,320]{1,0:T(8,128)(...) custom-call(s32[9]{0:T(128)S(1)} %stack.88.refs_0_, ...), custom_call_target="tpu_custom_call" | custom-call | flops 80530636800 | bytes 19687716 | tf_op jit(solution)/shard_map/pallas_call | solution.py:39
  133.3 5.6 %collective-permute-done.10.refs_2_.refs_1_ = bf16[256,320]{1,0:T(8,128)(2,1)S(1)} collective-permute-done((bf16[256,320]{1,0:T(8,128)(2,1)S(1)}, bf16[256,320]{1,0:T(8,128)(2,1)S(1)}, u32[]{:S(2)}, u32[]{:S(2)}) %collective-permute-start.10) | collective-permute-done | bytes 163872 | tf_op jit(solution)/shard_map/ppermute | solution.py:52
  138.9 1.5 collective-permute-done.11.refs_3_
  141.6 1.6 collective-permute-done.24.refs_12_
  144.2 1.6 copy-done.53
  145.8 11.9 %shard_map.252 = (f32[256,1280]{1,0:T(8,128)}, f32[256,1280]{1,0:T(8,128)}, f32[1,1280]{1,0:T(1,128)S(1)}, bf16[2,256,1280]{2,1,0:T(8,128)(2,1)}, bf16[2,256,640...) custom-call(s32[4]{0:T(128)S(1)} %pad_add_fusion.at_ref, ...), custom_call_target="tpu_custom_call" | custom-call | flops 40265318400 | bytes 18360336 | tf_op jit(solution)/shard_map/pallas_call | solution.py:39
  162.8 2.0 collective-permute-done.32.refs_8_
  168.7 7.9 %shard_map.253 = (bf16[1280,512]{1,0:T(8,128)(2,1)S(1)}, bf16[1280,512]{1,0:T(8,128)(2,1)}, bf16[2,2,320,512]{3,2,1,0:T(8,128)(2,1)}, bf16[2,2,320,512]{3,2,1,0:T(8,128)(2,1)S(1)}) custom-call(s32[1]{0:T(128)} %bitcast.27.at_ref, bf16[256,320]{1,0:T(8,128)(2,1)S(1)} %get-tuple-element.149.refs_0_, ...), custom_call_target="tpu_custom_call" | custom-call | flops 20132659200 | bytes 11141124 | tf_op jit(solution)/shard_map/pallas_call | solution.py:39
  179.1 33.4 %shard_map.254 = (bf16[1024,320]{1,0:T(8,128)(2,1)}, bf16[2048,640]{1,0:T(8,128)(2,1)}, f32[1,320]{1,0:T(1,128)}, bf16[4,160,1024]{2,1,0:T(8,128)(2,1)}, bf16[4,160,1024]{2,1,0:T(8,128)(2,1)}) custom-call(s32[5]{0:T(128)} %stack.96.at_ref, bf16[256,320]{1,0:T(8,128)(2,1)} %copy-done.32, bf16[256,320]{1,0:T(8,128)(2,1)} %collective-permute-done.26.refs_1_, ...), custom_call_target="tpu_custom_call" | custom-call | flops 134217728000 | bytes 15096340 | tf_op jit(solution)/shard_map/pallas_call | solution.py:39
  212.5 1.7 copy-done.26
  215.4 8.2 %shard_map.255 = (bf16[2,256,2560]{2,1,0:T(8,128)(2,1)S(1)}, bf16[2,256,2560]{2,1,0:T(8,128)(2,1)}) custom-call(s32[4]{0:T(128)S(1)} %pad_add_fusion.1.at_ref, bf16[1024,320]{1,0:T(8,128)(2,1)S(1)} %copy-done.29, bf16[2048,640]{1,0:T(8,128)(2,1)S(1)} %copy-done.26, bf16[1280,1024]{1,0:T(8,128)(2,1)} %get-tuple-element.106.w_ref), custom_call_target="tpu_custom_call" | custom-call | flops 33554432000 | bytes 11141136 | tf_op jit(solution)/shard_map/pallas_call | solution.py:39
  223.7 1.7 convert_add_fusion.1
  226.8 1.7 convert_add_fusion.2
  233.1 10.7 %collective-permute-done.41 = bf16[2,2,160,512]{3,2,1,0:T(8,128)(2,1)} collective-permute-done((bf16[2,2,160,512]{3,2,1,0:T(8,128)(2,1)}, bf16[2,2,160,512]{3,2,1,0:T(8,128)(2,1)}, u32[]{:S(2)}, u32[]{:S(2)}) %collective-permute-start.41) | collective-permute-done | bytes 655392 | tf_op jit(solution)/shard_map/ppermute | solution.py:52
  243.8 1.7 bitcast_add_fusion
  245.6 2.4 collective-permute-done.35
  249.4 3.4 collective-permute-start.44
  252.8 2.3 fusion.9
  255.2 8.0 %collective-permute-done.39 = bf16[4,160,1024]{2,1,0:T(8,128)(2,1)} collective-permute-done((bf16[4,160,1024]{2,1,0:T(8,128)(2,1)}, bf16[4,160,1024]{2,1,0:T(8,128)(2,1)}, u32[]{:S(2)}, u32[]{:S(2)}) %collective-permute-start.39) | collective-permute-done | bytes 1310752 | tf_op jit(solution)/shard_map/ppermute | solution.py:52
  264.0 1.8 convert_add_fusion
  265.9 1.8 collective-permute-start.42
  267.7 13.4 %collective-permute-done.44 = bf16[2,160,1024]{2,1,0:T(8,128)(2,1)S(1)} collective-permute-done((bf16[2,160,1024]{2,1,0:T(8,128)(2,1)S(1)}, bf16[2,160,1024]{2,1,0:T(8,128)(2,1)S(1)}, u32[]{:S(2)}, u32[]{:S(2)}) %collective-permute-start.44) | collective-permute-done | bytes 655392 | tf_op jit(solution)/shard_map/ppermute | solution.py:52
  283.8 11.4 %collective-permute-done.42 = bf16[2,160,1024]{2,1,0:T(8,128)(2,1)S(1)} collective-permute-done((bf16[2,160,1024]{2,1,0:T(8,128)(2,1)S(1)}, bf16[2,160,1024]{2,1,0:T(8,128)(2,1)S(1)}, u32[]{:S(2)}, u32[]{:S(2)}) %collective-permute-start.42) | collective-permute-done | bytes 655392 | tf_op jit(solution)/shard_map/ppermute | solution.py:52
  295.5 1.5 collective-permute-start.43
  298.1 17.4 %collective-permute-done.43.came_w = bf16[160,1024]{1,0:T(8,128)(2,1)S(1)} collective-permute-done((bf16[160,1024]{1,0:T(8,128)(2,1)S(1)}, bf16[160,1024]{1,0:T(8,128)(2,1)S(1)}, u32[]{:S(2)}, u32[]{:S(2)}) %collective-permute-start.43) | collective-permute-done | bytes 327712 | tf_op jit(solution)/shard_map/ppermute | solution.py:52
  317.8 2.7 collective-permute-done.46
  321.8 2.5 collective-permute-done.47
  324.5 4.4 %collective-permute-done.48 = f32[8,320]{1,0:T(8,128)S(1)} collective-permute-done((f32[8,320]{1,0:T(8,128)S(1)}, f32[8,320]{1,0:T(8,128)S(1)}, u32[]{:S(2)}, u32[]{:S(2)}) %collective-permute-start.48) | collective-permute-done | bytes 10272 | tf_op jit(solution)/shard_map/ppermute | solution.py:52
  332.0 2.8 all-to-all-start
  334.9 3.8 %fusion.6 = f32[256,1280]{1,0:T(8,128)} fusion(f32[256,1280]{1,0:T(8,128)} %get-tuple-element.87, bf16[256,1280]{1,0:T(8,128)(2,1)S(1)} %get-tuple-element.141.refs_14_, f32[256]{0:T(256)S(1)} %broadcast_multiply_fusion, f32[1280]{0:T(1024)S(1)} %copy-done.43, f32[256]{0:T(256)S(1)} %add_rsqrt_fusion, bf16[256,1280]{1,0:T(8,128)(2,1)} %copy-done.40, ...), kind=kLoop, calls=%fused_computation.18 | loop fusion | flops 3604480 | bytes 5905408 | tf_op jit(solution)/shard_map/add | solution.py:689
  338.6 4.4 %all-to-all-done = f32[32,8,128]{2,1,0:T(8,128)S(1)} async-done(((f32[32,8,128]{2,1,0:T(8,128)}), f32[32,8,128]{2,1,0:T(8,128)S(1)}, u32[]{:S(2)}, u32[]{:S(2)}) %all-to-all-start) | async-done | bytes 131104 | tf_op jit(solution)/shard_map/all_to_all | solution.py:741
  (257 shorter events, 60.5 us)
Async XLA Ops:
  3.4 18.8 %collective-permute-start.4 = (bf16[160,1024]{1,0:T(8,128)(2,1)S(1)}, bf16[160,1024]{1,0:T(8,128)(2,1)S(1)}, u32[]{:S(2)}, u32[]{:S(2)}) collective-permute-start(bf16[160,1024]{1,0:T(8,128)(2,1)S(1)} %get-tuple-element.167), channel_id=1, source_target_pairs={{0,16},{4,20},{8,24},{12,28},{16,0},{20,4},{24,8},{28,12},{1,17},{... | collective-permute-start | bytes 983048 | tf_op jit(solution)/shard_map/ppermute | solution.py:52
  7.6 14.6 %collective-permute-start.6 = (bf16[1,160,1024]{2,1,0:T(8,128)(2,1)S(1)}, bf16[1,160,1024]{2,1,0:T(8,128)(2,1)S(1)}, u32[]{:S(2)}, u32[]{:S(2)}) collective-permute-start(bf16[1,160,1024]{2,1,0:T(8,128)(2,1)S(1)} %pad_maximum_fusion.4.refs_6_), channel_id=1, source_target_pairs={{0,4},{4,0},{8,12},{12,8},{16,20},{20,16},{24,28},{28,24},{1,5},{5... | collective-permute-start | bytes 983048 | tf_op jit(solution)/shard_map/ppermute | solution.py:52
  11.1 27.2 %collective-permute-start = (bf16[256,1280]{1,0:T(8,128)(2,1)S(1)}, bf16[256,1280]{1,0:T(8,128)(2,1)S(1)}, u32[]{:S(2)}, u32[]{:S(2)}) collective-permute-start(bf16[256,1280]{1,0:T(8,128)(2,1)S(1)} %get-tuple-element.141.refs_14_), channel_id=1, source_target_pairs={{0,4},{4,8},{8,12},{12,16},{16,20},{20,24},{24,28},{1,5},{5,9},{9,... | collective-permute-start | bytes 1966088 | tf_op jit(solution)/shard_map/ppermute | solution.py:467
  13.5 26.3 %collective-permute-start.12 = (bf16[160,1024]{1,0:T(8,128)(2,1)S(1)}, bf16[160,1024]{1,0:T(8,128)(2,1)}, u32[]{:S(2)}, u32[]{:S(2)}) collective-permute-start(bf16[160,1024]{1,0:T(8,128)(2,1)S(1)} %get-tuple-element.75), channel_id=1, source_target_pairs={{0,4},{4,0},{8,12},{12,8},{16,20},{20,16},{24,28},{28,24},{1,5},{5... | collective-permute-start | bytes 983048 | tf_op jit(solution)/shard_map/ppermute | solution.py:52
  23.0 13.4 %collective-permute-start.13 = (bf16[160,1024]{1,0:T(8,128)(2,1)S(1)}, bf16[160,1024]{1,0:T(8,128)(2,1)S(1)}, u32[]{:S(2)}, u32[]{:S(2)}) collective-permute-start(bf16[160,1024]{1,0:T(8,128)(2,1)S(1)} %get-tuple-element.75), channel_id=1, source_target_pairs={{0,16},{4,20},{8,24},{12,28},{16,0},{20,4},{24,8},{28,12},{1,17},{... | collective-permute-start | bytes 983048 | tf_op jit(solution)/shard_map/ppermute | solution.py:52
  23.9 24.2 %collective-permute-start.5 = (bf16[2,160,1024]{2,1,0:T(8,128)(2,1)}, bf16[2,160,1024]{2,1,0:T(8,128)(2,1)S(1)}, u32[]{:S(2)}, u32[]{:S(2)}) collective-permute-start(bf16[2,160,1024]{2,1,0:T(8,128)(2,1)} %pad_maximum_fusion.1), channel_id=1, source_target_pairs={{0,8},{4,12},{8,0},{12,4},{16,24},{20,28},{24,16},{28,20},{1,9},{5... | collective-permute-start | bytes 1966088 | tf_op jit(solution)/shard_map/ppermute | solution.py:52
  35.7 9.8 %collective-permute-start.7 = (bf16[1,160,1024]{2,1,0:T(8,128)(2,1)S(1)}, bf16[1,160,1024]{2,1,0:T(8,128)(2,1)S(1)}, u32[]{:S(2)}, u32[]{:S(2)}) collective-permute-start(bf16[1,160,1024]{2,1,0:T(8,128)(2,1)S(1)} %bitcast.82), channel_id=1, source_target_pairs={{0,4},{4,0},{8,12},{12,8},{16,20},{20,16},{24,28},{28,24},{1,5},{5... | collective-permute-start | bytes 983048 | tf_op jit(solution)/shard_map/ppermute | solution.py:52
  36.4 20.1 %collective-permute-start.14 = (bf16[160,1024]{1,0:T(8,128)(2,1)S(1)}, bf16[160,1024]{1,0:T(8,128)(2,1)S(1)}, u32[]{:S(2)}, u32[]{:S(2)}) collective-permute-start(bf16[160,1024]{1,0:T(8,128)(2,1)S(1)} %collective-permute-done.13), channel_id=1, source_target_pairs={{0,4},{4,0},{8,12},{12,8},{16,20},{20,16},{24,28},{28,24},{1,5},{5... | collective-permute-start | bytes 983048 | tf_op jit(solution)/shard_map/ppermute | solution.py:52
  38.3 19.5 %collective-permute-start.1 = (bf16[256,1280]{1,0:T(8,128)(2,1)S(1)}, bf16[256,1280]{1,0:T(8,128)(2,1)S(1)}, u32[]{:S(2)}, u32[]{:S(2)}) collective-permute-start(bf16[256,1280]{1,0:T(8,128)(2,1)S(1)} %collective-permute-done.refs_2_), channel_id=1, source_target_pairs={{0,2},{1,3},{2,0},{3,1},{4,6},{5,7},{6,4},{7,5},{8,10},{9,11},{10,... | collective-permute-start | bytes 1966088 | tf_op jit(solution)/shard_map/ppermute | solution.py:52
  48.2 23.0 %collective-permute-start.15 = (bf16[320,1024]{1,0:T(8,128)(2,1)}, bf16[320,1024]{1,0:T(8,128)(2,1)}, u32[]{:S(2)}, u32[]{:S(2)}) collective-permute-start(bf16[320,1024]{1,0:T(8,128)(2,1)} %get-tuple-element.77), channel_id=1, source_target_pairs={{0,8},{4,12},{8,0},{12,4},{16,24},{20,28},{24,16},{28,20},{1,9},{5... | collective-permute-start | bytes 1966088 | tf_op jit(solution)/shard_map/ppermute | solution.py:52
  58.7 16.0 %collective-permute-start.16 = (bf16[320,1024]{1,0:T(8,128)(2,1)}, bf16[320,1024]{1,0:T(8,128)(2,1)S(1)}, u32[]{:S(2)}, u32[]{:S(2)}) collective-permute-start(bf16[320,1024]{1,0:T(8,128)(2,1)} %get-tuple-element.79), channel_id=1, source_target_pairs={{0,2},{1,3},{2,0},{3,1},{4,6},{5,7},{6,4},{7,5},{8,10},{9,11},{10,... | collective-permute-start | bytes 1966088 | tf_op jit(solution)/shard_map/ppermute | solution.py:52
  74.7 15.1 %collective-permute-start.20 = (bf16[320,1024]{1,0:T(8,128)(2,1)}, bf16[320,1024]{1,0:T(8,128)(2,1)S(1)}, u32[]{:S(2)}, u32[]{:S(2)}) collective-permute-start(bf16[320,1024]{1,0:T(8,128)(2,1)} %collective-permute-done.15), channel_id=1, source_target_pairs={{0,2},{1,3},{2,0},{3,1},{4,6},{5,7},{6,4},{7,5},{8,10},{9,11},{10,... | collective-permute-start | bytes 1966088 | tf_op jit(solution)/shard_map/ppermute | solution.py:52
  75.2 24.8 %collective-permute-start.17 = (bf16[320,1024]{1,0:T(8,128)(2,1)}, bf16[320,1024]{1,0:T(8,128)(2,1)S(1)}, u32[]{:S(2)}, u32[]{:S(2)}) collective-permute-start(bf16[320,1024]{1,0:T(8,128)(2,1)} %get-tuple-element.79), channel_id=1, source_target_pairs={{0,8},{4,12},{8,0},{12,4},{16,24},{20,28},{24,16},{28,20},{1,9},{5... | collective-permute-start | bytes 1966088 | tf_op jit(solution)/shard_map/ppermute | solution.py:52
  87.3 15.2 %collective-permute-start.2 = (bf16[256,1280]{1,0:T(8,128)(2,1)S(1)}, bf16[256,1280]{1,0:T(8,128)(2,1)S(1)}, u32[]{:S(2)}, u32[]{:S(2)}) collective-permute-start(bf16[256,1280]{1,0:T(8,128)(2,1)S(1)} %collective-permute-done.refs_2_), channel_id=1, source_target_pairs={{0,1},{1,0},{2,3},{3,2},{4,5},{5,4},{6,7},{7,6},{8,9},{9,8},{10,11... | collective-permute-start | bytes 1966088 | tf_op jit(solution)/shard_map/ppermute | solution.py:52
  87.4 17.1 %collective-permute-start.8 = (bf16[2,160,1024]{2,1,0:T(8,128)(2,1)S(1)}, bf16[2,160,1024]{2,1,0:T(8,128)(2,1)S(1)}, u32[]{:S(2)}, u32[]{:S(2)}) collective-permute-start(bf16[2,160,1024]{2,1,0:T(8,128)(2,1)S(1)} %collective-permute-done.5.refs_8_), channel_id=1, source_target_pairs={{0,4},{4,0},{8,12},{12,8},{16,20},{20,16},{24,28},{28,24},{1,5},{5... | collective-permute-start | bytes 1966088 | tf_op jit(solution)/shard_map/ppermute | solution.py:52
  88.1 16.5 %collective-permute-start.3 = (bf16[256,1280]{1,0:T(8,128)(2,1)}, bf16[256,1280]{1,0:T(8,128)(2,1)S(1)}, u32[]{:S(2)}, u32[]{:S(2)}) collective-permute-start(bf16[256,1280]{1,0:T(8,128)(2,1)} %copy-done.11), channel_id=1, source_target_pairs={{0,1},{1,0},{2,3},{3,2},{4,5},{5,4},{6,7},{7,6},{8,9},{9,8},{10,11... | collective-permute-start | bytes 1966088 | tf_op jit(solution)/shard_map/ppermute | solution.py:52
  89.8 42.3 %collective-permute-start.19 = (bf16[320,1024]{1,0:T(8,128)(2,1)}, bf16[320,1024]{1,0:T(8,128)(2,1)S(1)}, u32[]{:S(2)}, u32[]{:S(2)}) collective-permute-start(bf16[320,1024]{1,0:T(8,128)(2,1)} %get-tuple-element.77), channel_id=1, source_target_pairs={{0,2},{1,3},{2,0},{3,1},{4,6},{5,7},{6,4},{7,5},{8,10},{9,11},{10,... | collective-permute-start | bytes 1966088 | tf_op jit(solution)/shard_map/ppermute | solution.py:52
  100.1 33.1 %collective-permute-start.21 = (bf16[320,1024]{1,0:T(8,128)(2,1)S(1)}, bf16[320,1024]{1,0:T(8,128)(2,1)S(1)}, u32[]{:S(2)}, u32[]{:S(2)}) collective-permute-start(bf16[320,1024]{1,0:T(8,128)(2,1)S(1)} %collective-permute-done.17), channel_id=1, source_target_pairs={{0,2},{1,3},{2,0},{3,1},{4,6},{5,7},{6,4},{7,5},{8,10},{9,11},{10,... | collective-permute-start | bytes 1966088 | tf_op jit(solution)/shard_map/ppermute | solution.py:52
  102.5 41.7 %collective-permute-start.18 = (bf16[4,320,1024]{2,1,0:T(8,128)(2,1)S(1)}, bf16[4,320,1024]{2,1,0:T(8,128)(2,1)S(1)}, u32[]{:S(2)}, u32[]{:S(2)}) collective-permute-start(bf16[4,320,1024]{2,1,0:T(8,128)(2,1)S(1)} %pad_maximum_fusion.refs_4_), channel_id=1, source_target_pairs={{0,1},{1,0},{2,3},{3,2},{4,5},{5,4},{6,7},{7,6},{8,9},{9,8},{10,11... | collective-permute-start | bytes 7864328 | tf_op jit(solution)/shard_map/ppermute | solution.py:52
  131.0 7.9 %collective-permute-start.10 = (bf16[256,320]{1,0:T(8,128)(2,1)S(1)}, bf16[256,320]{1,0:T(8,128)(2,1)S(1)}, u32[]{:S(2)}, u32[]{:S(2)}) collective-permute-start(bf16[256,320]{1,0:T(8,128)(2,1)S(1)} %get-tuple-element.147), channel_id=1, source_target_pairs={{0,2},{1,3},{2,0},{3,1},{4,6},{5,7},{6,4},{7,5},{8,10},{9,11},{10,... | collective-permute-start | bytes 491528 | tf_op jit(solution)/shard_map/ppermute | solution.py:52
  131.6 8.8 %collective-permute-start.11 = (bf16[256,320]{1,0:T(8,128)(2,1)S(1)}, bf16[256,320]{1,0:T(8,128)(2,1)S(1)}, u32[]{:S(2)}, u32[]{:S(2)}) collective-permute-start(bf16[256,320]{1,0:T(8,128)(2,1)S(1)} %get-tuple-element.146), channel_id=1, source_target_pairs={{0,3},{1,2},{2,1},{3,0},{4,7},{5,6},{6,5},{7,4},{8,11},{9,10},{10,... | collective-permute-start | bytes 491528 | tf_op jit(solution)/shard_map/ppermute | solution.py:52
  132.0 9.5 %collective-permute-start.9 = (bf16[256,320]{1,0:T(8,128)(2,1)S(1)}, bf16[256,320]{1,0:T(8,128)(2,1)S(1)}, u32[]{:S(2)}, u32[]{:S(2)}) collective-permute-start(bf16[256,320]{1,0:T(8,128)(2,1)S(1)} %get-tuple-element.148), channel_id=1, source_target_pairs={{0,1},{1,0},{2,3},{3,2},{4,5},{5,4},{6,7},{7,6},{8,9},{9,8},{10,11... | collective-permute-start | bytes 491528 | tf_op jit(solution)/shard_map/ppermute | solution.py:52
  133.2 8.4 %collective-permute-start.23 = (bf16[1,320,1024]{2,1,0:T(8,128)(2,1)S(1)}, bf16[1,320,1024]{2,1,0:T(8,128)(2,1)S(1)}, u32[]{:S(2)}, u32[]{:S(2)}) collective-permute-start(bf16[1,320,1024]{2,1,0:T(8,128)(2,1)S(1)} %bitcast.84), channel_id=1, source_target_pairs={{0,1},{1,0},{2,3},{3,2},{4,5},{5,4},{6,7},{7,6},{8,9},{9,8},{10,11... | collective-permute-start | bytes 1966088 | tf_op jit(solution)/shard_map/ppermute | solution.py:52
  159.2 7.2 %collective-permute-start.30 = (bf16[2,256,1280]{2,1,0:T(8,128)(2,1)}, bf16[2,256,1280]{2,1,0:T(8,128)(2,1)}, u32[]{:S(2)}, u32[]{:S(2)}) collective-permute-start(bf16[2,256,1280]{2,1,0:T(8,128)(2,1)} %get-tuple-element.96.refs_3_), channel_id=1, source_target_pairs={{0,1},{1,0},{2,3},{3,2},{4,5},{5,4},{6,7},{7,6},{8,9},{9,8},{10,11... | collective-permute-start | bytes 3932168 | tf_op jit(solution)/shard_map/ppermute | solution.py:52
  159.5 5.3 %collective-permute-start.32 = (bf16[256,1280]{1,0:T(8,128)(2,1)S(1)}, bf16[256,1280]{1,0:T(8,128)(2,1)S(1)}, u32[]{:S(2)}, u32[]{:S(2)}) collective-permute-start(bf16[256,1280]{1,0:T(8,128)(2,1)S(1)} %copy-done.10), channel_id=1, source_target_pairs={{0,1},{1,0},{2,3},{3,2},{4,5},{5,4},{6,7},{7,6},{8,9},{9,8},{10,11... | collective-permute-start | bytes 1966088 | tf_op jit(solution)/shard_map/ppermute | solution.py:52
  159.7 6.6 %collective-permute-start.31 = (bf16[2,256,640]{2,1,0:T(8,128)(2,1)S(1)}, bf16[2,256,640]{2,1,0:T(8,128)(2,1)}, u32[]{:S(2)}, u32[]{:S(2)}) collective-permute-start(bf16[2,256,640]{2,1,0:T(8,128)(2,1)S(1)} %get-tuple-element.98), channel_id=1, source_target_pairs={{0,1},{1,0},{2,3},{3,2},{4,5},{5,4},{6,7},{7,6},{8,9},{9,8},{10,11... | collective-permute-start | bytes 1966088 | tf_op jit(solution)/shard_map/ppermute | solution.py:52
  160.9 4.5 %collective-permute-start.29 = (bf16[256,640]{1,0:T(8,128)(2,1)}, bf16[256,640]{1,0:T(8,128)(2,1)S(1)}, u32[]{:S(2)}, u32[]{:S(2)}) collective-permute-start(bf16[256,640]{1,0:T(8,128)(2,1)} %pad_maximum_fusion.5), channel_id=1, source_target_pairs={{0,1},{1,0},{2,3},{3,2},{4,5},{5,4},{6,7},{7,6},{8,9},{9,8},{10,11... | collective-permute-start | bytes 983048 | tf_op jit(solution)/shard_map/ppermute | solution.py:52
  162.4 16.6 %collective-permute-start.26 = (bf16[256,320]{1,0:T(8,128)(2,1)}, bf16[256,320]{1,0:T(8,128)(2,1)}, u32[]{:S(2)}, u32[]{:S(2)}) collective-permute-start(bf16[256,320]{1,0:T(8,128)(2,1)} %copy-done.19), channel_id=1, source_target_pairs={{0,1},{1,0},{2,3},{3,2},{4,5},{5,4},{6,7},{7,6},{8,9},{9,8},{10,11... | collective-permute-start | bytes 491528 | tf_op jit(solution)/shard_map/ppermute | solution.py:52
  164.8 14.2 %collective-permute-start.27 = (bf16[256,320]{1,0:T(8,128)(2,1)}, bf16[256,320]{1,0:T(8,128)(2,1)}, u32[]{:S(2)}, u32[]{:S(2)}) collective-permute-start(bf16[256,320]{1,0:T(8,128)(2,1)} %copy-done.18), channel_id=1, source_target_pairs={{0,2},{1,3},{2,0},{3,1},{4,6},{5,7},{6,4},{7,5},{8,10},{9,11},{10,... | collective-permute-start | bytes 491528 | tf_op jit(solution)/shard_map/ppermute | solution.py:52
  165.4 13.7 %collective-permute-start.28 = (bf16[256,320]{1,0:T(8,128)(2,1)}, bf16[256,320]{1,0:T(8,128)(2,1)}, u32[]{:S(2)}, u32[]{:S(2)}) collective-permute-start(bf16[256,320]{1,0:T(8,128)(2,1)} %copy-done.17), channel_id=1, source_target_pairs={{0,3},{1,2},{2,1},{3,0},{4,7},{5,6},{6,5},{7,4},{8,11},{9,10},{10,... | collective-permute-start | bytes 491528 | tf_op jit(solution)/shard_map/ppermute | solution.py:52
  176.6 50.2 %collective-permute-start.34 = (bf16[2,2,320,512]{3,2,1,0:T(8,128)(2,1)}, bf16[2,2,320,512]{3,2,1,0:T(8,128)(2,1)}, u32[]{:S(2)}, u32[]{:S(2)}) collective-permute-start(bf16[2,2,320,512]{3,2,1,0:T(8,128)(2,1)} %get-tuple-element.101), channel_id=1, source_target_pairs={{0,8},{4,12},{8,0},{12,4},{16,24},{20,28},{24,16},{28,20},{1,9},{5... | collective-permute-start | bytes 3932168 | tf_op jit(solution)/shard_map/ppermute | solution.py:52
  177.6 46.1 %collective-permute-start.40 = (bf16[1280,512]{1,0:T(8,128)(2,1)}, bf16[1280,512]{1,0:T(8,128)(2,1)}, u32[]{:S(2)}, u32[]{:S(2)}) collective-permute-start(bf16[1280,512]{1,0:T(8,128)(2,1)} %get-tuple-element.100), channel_id=1, source_target_pairs={{0,2},{1,3},{2,0},{3,1},{4,6},{5,7},{6,4},{7,5},{8,10},{9,11},{10,... | collective-permute-start | bytes 3932168 | tf_op jit(solution)/shard_map/ppermute | solution.py:52
  223.6 29.2 %collective-permute-start.33 = (bf16[2,256,2560]{2,1,0:T(8,128)(2,1)}, bf16[2,256,2560]{2,1,0:T(8,128)(2,1)}, u32[]{:S(2)}, u32[]{:S(2)}) collective-permute-start(bf16[2,256,2560]{2,1,0:T(8,128)(2,1)} %get-tuple-element.108), channel_id=1, source_target_pairs={{0,1},{1,0},{2,3},{3,2},{4,5},{5,4},{6,7},{7,6},{8,9},{9,8},{10,11... | collective-permute-start | bytes 7864328 | tf_op jit(solution)/shard_map/ppermute | solution.py:52
  226.5 17.3 %collective-permute-start.41 = (bf16[2,2,160,512]{3,2,1,0:T(8,128)(2,1)}, bf16[2,2,160,512]{3,2,1,0:T(8,128)(2,1)}, u32[]{:S(2)}, u32[]{:S(2)}) collective-permute-start(bf16[2,2,160,512]{3,2,1,0:T(8,128)(2,1)} %fusion.18), channel_id=1, source_target_pairs={{0,8},{4,12},{8,0},{12,4},{16,24},{20,28},{24,16},{28,20},{1,9},{5... | collective-permute-start | bytes 1966088 | tf_op jit(solution)/shard_map/ppermute | solution.py:52
  230.9 17.1 %collective-permute-start.35 = (bf16[2,320,512]{2,1,0:T(8,128)(2,1)}, bf16[2,320,512]{2,1,0:T(8,128)(2,1)}, u32[]{:S(2)}, u32[]{:S(2)}) collective-permute-start(bf16[2,320,512]{2,1,0:T(8,128)(2,1)} %fusion.20), channel_id=1, source_target_pairs={{0,2},{1,3},{2,0},{3,1},{4,6},{5,7},{6,4},{7,5},{8,10},{9,11},{10,... | collective-permute-start | bytes 1966088 | tf_op jit(solution)/shard_map/ppermute | solution.py:52
  232.3 30.9 %collective-permute-start.39 = (bf16[4,160,1024]{2,1,0:T(8,128)(2,1)}, bf16[4,160,1024]{2,1,0:T(8,128)(2,1)}, u32[]{:S(2)}, u32[]{:S(2)}) collective-permute-start(bf16[4,160,1024]{2,1,0:T(8,128)(2,1)} %get-tuple-element.113), channel_id=1, source_target_pairs={{0,4},{4,0},{8,12},{12,8},{16,20},{20,16},{24,28},{28,24},{1,5},{5... | collective-permute-start | bytes 3932168 | tf_op jit(solution)/shard_map/ppermute | solution.py:52
  249.4 31.7 %collective-permute-start.44 = (bf16[2,160,1024]{2,1,0:T(8,128)(2,1)S(1)}, bf16[2,160,1024]{2,1,0:T(8,128)(2,1)S(1)}, u32[]{:S(2)}, u32[]{:S(2)}) collective-permute-start(bf16[2,160,1024]{2,1,0:T(8,128)(2,1)S(1)} %fusion.21), channel_id=1, source_target_pairs={{0,16},{4,20},{8,24},{12,28},{16,0},{20,4},{24,8},{28,12},{1,17},{... | collective-permute-start | bytes 1966088 | tf_op jit(solution)/shard_map/ppermute | solution.py:52
  263.3 19.1 %collective-permute-start.36 = (bf16[256,1280]{1,0:T(8,128)(2,1)S(1)}, bf16[256,1280]{1,0:T(8,128)(2,1)S(1)}, u32[]{:S(2)}, u32[]{:S(2)}) collective-permute-start(bf16[256,1280]{1,0:T(8,128)(2,1)S(1)} %get-tuple-element.145), channel_id=1, source_target_pairs={{0,2},{1,3},{2,0},{3,1},{4,6},{5,7},{6,4},{7,5},{8,10},{9,11},{10,... | collective-permute-start | bytes 1966088 | tf_op jit(solution)/shard_map/ppermute | solution.py:52
  265.9 29.3 %collective-permute-start.42 = (bf16[2,160,1024]{2,1,0:T(8,128)(2,1)S(1)}, bf16[2,160,1024]{2,1,0:T(8,128)(2,1)S(1)}, u32[]{:S(2)}, u32[]{:S(2)}) collective-permute-start(bf16[2,160,1024]{2,1,0:T(8,128)(2,1)S(1)} %fusion.19), channel_id=1, source_target_pairs={{0,8},{4,12},{8,0},{12,4},{16,24},{20,28},{24,16},{28,20},{1,9},{5... | collective-permute-start | bytes 1966088 | tf_op jit(solution)/shard_map/ppermute | solution.py:52
  281.4 34.2 %collective-permute-start.45 = (bf16[160,1024]{1,0:T(8,128)(2,1)S(1)}, bf16[160,1024]{1,0:T(8,128)(2,1)S(1)}, u32[]{:S(2)}, u32[]{:S(2)}) collective-permute-start(bf16[160,1024]{1,0:T(8,128)(2,1)S(1)} %fusion.23), channel_id=1, source_target_pairs={{0,4},{4,0},{8,12},{12,8},{16,20},{20,16},{24,28},{28,24},{1,5},{5... | collective-permute-start | bytes 983048 | tf_op jit(solution)/shard_map/ppermute | solution.py:52
  282.5 33.0 %collective-permute-start.38 = (bf16[256,1280]{1,0:T(8,128)(2,1)S(1)}, bf16[256,1280]{1,0:T(8,128)(2,1)S(1)}, u32[]{:S(2)}, u32[]{:S(2)}) collective-permute-start(bf16[256,1280]{1,0:T(8,128)(2,1)S(1)} %fusion.16), channel_id=1, source_target_pairs={{4,0},{8,4},{12,8},{16,12},{20,16},{24,20},{28,24},{5,1},{9,5},{13... | collective-permute-start | bytes 1966088 | tf_op jit(solution)/shard_map/ppermute | solution.py:681
  295.5 20.1 %collective-permute-start.43 = (bf16[160,1024]{1,0:T(8,128)(2,1)S(1)}, bf16[160,1024]{1,0:T(8,128)(2,1)S(1)}, u32[]{:S(2)}, u32[]{:S(2)}) collective-permute-start(bf16[160,1024]{1,0:T(8,128)(2,1)S(1)} %fusion.22), channel_id=1, source_target_pairs={{0,16},{4,20},{8,24},{12,28},{16,0},{20,4},{24,8},{28,12},{1,17},{... | collective-permute-start | bytes 983048 | tf_op jit(solution)/shard_map/ppermute | solution.py:52
  297.1 19.8 %collective-permute-start.37 = (bf16[256,1280]{1,0:T(8,128)(2,1)S(1)}, bf16[256,1280]{1,0:T(8,128)(2,1)S(1)}, u32[]{:S(2)}, u32[]{:S(2)}) collective-permute-start(bf16[256,1280]{1,0:T(8,128)(2,1)S(1)} %get-tuple-element.111), channel_id=1, source_target_pairs={{0,2},{1,3},{2,0},{3,1},{4,6},{5,7},{6,4},{7,5},{8,10},{9,11},{10,... | collective-permute-start | bytes 1966088 | tf_op jit(solution)/shard_map/ppermute | solution.py:52
  316.9 3.7 %collective-permute-start.49 = (f32[8,160]{1,0:T(8,128)S(1)}, f32[8,160]{1,0:T(8,128)S(1)}, u32[]{:S(2)}, u32[]{:S(2)}) collective-permute-start(f32[8,160]{1,0:T(8,128)S(1)} %get-tuple-element.123), channel_id=1, source_target_pairs={{0,1},{1,0},{2,3},{3,2},{4,5},{5,4},{6,7},{7,6},{8,9},{9,8},{10,11... | collective-permute-start | bytes 15368 | tf_op jit(solution)/shard_map/ppermute | solution.py:52
  316.9 3.7 %collective-permute-start.46 = (f32[8,320]{1,0:T(8,128)S(1)}, f32[8,320]{1,0:T(8,128)S(1)}, u32[]{:S(2)}, u32[]{:S(2)}) collective-permute-start(f32[8,320]{1,0:T(8,128)S(1)} %get-tuple-element.122), channel_id=1, source_target_pairs={{0,4},{4,0},{8,12},{12,8},{16,20},{20,16},{24,28},{28,24},{1,5},{5... | collective-permute-start | bytes 30728 | tf_op jit(solution)/shard_map/ppermute | solution.py:52
  320.6 3.9 %collective-permute-start.50 = (f32[8,160]{1,0:T(8,128)S(1)}, f32[8,160]{1,0:T(8,128)S(1)}, u32[]{:S(2)}, u32[]{:S(2)}) collective-permute-start(f32[8,160]{1,0:T(8,128)S(1)} %add.209), channel_id=1, source_target_pairs={{0,2},{1,3},{2,0},{3,1},{4,6},{5,7},{6,4},{7,5},{8,10},{9,11},{10,... | collective-permute-start | bytes 15368 | tf_op jit(solution)/shard_map/ppermute | solution.py:52
  324.3 4.6 %collective-permute-start.48 = (f32[8,320]{1,0:T(8,128)S(1)}, f32[8,320]{1,0:T(8,128)S(1)}, u32[]{:S(2)}, u32[]{:S(2)}) collective-permute-start(f32[8,320]{1,0:T(8,128)S(1)} %add.207), channel_id=1, source_target_pairs={{0,16},{4,20},{8,24},{12,28},{16,0},{20,4},{24,8},{28,12},{1,17},{... | collective-permute-start | bytes 30728 | tf_op jit(solution)/shard_map/ppermute | solution.py:52
  332.0 11.1 %all-to-all-start = ((f32[32,8,128]{2,1,0:T(8,128)}), f32[32,8,128]{2,1,0:T(8,128)S(1)}, u32[]{:S(2)}, u32[]{:S(2)}) async-start(f32[32,8,128]{2,1,0:T(8,128)} %bitcast.47), calls=%async_computation | async-start | bytes 262144 | tf_op jit(solution)/shard_map/all_to_all | solution.py:741
  (59 other events, 484.3 us)

commit v3 on v2

--- a/solution.py
+++ b/solution.py
@@ -32,15 +32,19 @@
     return lax.dot_general(left, right, (dims, ((), ())), preferred_element_type=f32)
 
 
-def vmem_call(body, outs, scratch, flops, limit, *args):
+def vmem_call(body, outs, scratch, flops, limit, *args, far_in=(), far_out=()):
     size = sum(math.prod(a.shape) * a.dtype.itemsize for a in (*args, *outs))
     space = pl.BlockSpec(memory_space=pltpu.VMEM)
     scalars = pl.BlockSpec(memory_space=pltpu.SMEM)
+    anywhere = pl.BlockSpec(memory_space=pl.ANY)
     return pl.pallas_call(
         body,
         out_shape=outs,
-        in_specs=[scalars if a.ndim == 1 else space for a in args],
-        out_specs=[space] * len(outs),
+        in_specs=[
+            scalars if a.ndim == 1 else anywhere if i in far_in else space
+            for i, a in enumerate(args)
+        ],
+        out_specs=[anywhere if i in far_out else space for i in range(len(outs))],
         scratch_shapes=scratch,
         compiler_params=pltpu.CompilerParams(vmem_limit_bytes=limit * MIB),
         cost_estimate=pl.CostEstimate(flops=8 * int(flops), bytes_accessed=size, transcendentals=0),
@@ -99,7 +103,7 @@
     left = list(left)
     for k in order:
         send, keep = scatter_step(total, left, k)
-        send = after(send, *earlier) if k == order[-1] else send
+        send = after(send, *earlier) if len(left) == 1 else send
         left.remove(k)
         came = hop(send, "seq", 1 << k)
         if left:
@@ -136,49 +140,81 @@
 
 
 def attend_kernel(heads, counts, *refs):
-    n_near, n_rim = counts
-    at_ref, tok_ref = refs[:2]
-    rims = refs[2 : 2 + n_rim]
-    near = refs[2 + n_rim : 2 + n_rim + n_near]
-    far = refs[2 + n_rim + n_near : 2 + n_rim + 2 * n_near]
-    gain_ref, sc_ref, lo_ref = refs[2 + n_rim + 2 * n_near : 5 + n_rim + 2 * n_near]
-    h_ref, q_ref, k_ref, v_ref, c_ref, lse_ref, w_ref, kh, vt, bias = refs[5 + n_rim + 2 * n_near :]
+    n_near, n_rim, n_parts = counts
+    refs = list(refs)
+
+    def take(n):
+        out = refs[:n]
+        del refs[:n]
+        return out
+
+    at_ref, tok_in = take(2)
+    rims, near, far = take(n_rim), take(n_near), take(n_near)
+    gain_ref, sc_ref, lo_ref = take(3)
+    h_out, q_out, k_out, v_out, w_out, lse_ref = take(6)
+    pieces = take(n_parts)
+    x_ref, h_ref, w_ref, q_ref, k_ref, v_ref, kh, vt, bias, c_ref = take(10)
+    stages, (in_sem, out_sem) = take(2 * n_near), take(2)
     cols = heads * HD
     rows = q_ref.shape[0]
 
-    low, spot = at_ref[0], 1
-    for one, two in zip(near, far):
+    arrive = []
+
+    def bring(source, target):
+        arrive.append(pltpu.make_async_copy(source, target, in_sem.at[len(arrive)]))
+        arrive[-1].start()
+        return arrive[-1]
+
+    weights = [bring(a, b) for a, b in zip((*near, *far), stages)]
+    own = bring(tok_in, x_ref.at[pl.ds(WINDOW, rows), :])
+    spot = 1 + sum(a.shape[0] for a in near)
+    rim_copies = []
+    for i, rim in enumerate(rims):
+        place = pl.multiple_of(at_ref[spot + i], 16)
+        rim_copies.append(bring(rim, x_ref.at[pl.ds(place, rim.shape[0]), :]))
+    spot += n_rim
+
+    leave = []
+
+    def send(source, target):
+        leave.append(pltpu.make_async_copy(source, target, out_sem.at[len(leave)]))
+        leave[-1].start()
+
+    for copy in weights:
+        copy.wait()
+    turn = 1
+    for one, two in zip(stages[:n_near], stages[n_near:]):
         for i in range(one.shape[0]):
-            at = pl.ds(pl.multiple_of(at_ref[spot], 16), 2 * one.shape[1])
-            spot += 1
-
-            @pl.when(low == 0)
+            at = pl.ds(pl.multiple_of(at_ref[turn], 16), 2 * one.shape[1])
+            turn += 1
+
+            @pl.when(at_ref[0] == 0)
             def _():
                 w_ref[at, :] = jnp.concatenate([one[i], two[i]], axis=0)
 
-            @pl.when(low == 1)
+            @pl.when(at_ref[0] == 1)
             def _():
                 w_ref[at, :] = jnp.concatenate([two[i], one[i]], axis=0)
 
-    def norm(values):
-        values = values.astype(f32)
+    send(w_ref, w_out)
+
+    blocks = h_ref.shape[0] // BLOCK
+    own.wait()
+    for j in range(blocks):
+        i = (j + WINDOW // BLOCK) % blocks
+        if i == 0:
+            for copy in rim_copies:
+                copy.wait()
+        at = slice(i * BLOCK, (i + 1) * BLOCK)
+        values = x_ref[at, :].astype(f32)
         factor = lax.rsqrt(jnp.mean(values * values, axis=-1, keepdims=True) + EPSILON)
-        return (values * factor * gain_ref[...]).astype(bf16)
-
-    for rim in rims:
-        share = rim.shape[0]
-        h_ref[pl.ds(pl.multiple_of(at_ref[spot], 16), share), :] = norm(rim[...])
-        spot += 1
-    for i in range(rows // BLOCK):
-        h_ref[WINDOW + i * BLOCK : WINDOW + (i + 1) * BLOCK, :] = norm(
-            tok_ref[i * BLOCK : (i + 1) * BLOCK, :]
-        )
-
-    for i in range(h_ref.shape[0] // BLOCK):
-        at = pl.ds(i * BLOCK, BLOCK)
-        proj = dot(h_ref[at, :], w_ref[:, : 3 * cols], ((1,), (0,)))
+        normed = (values * factor * gain_ref[...]).astype(bf16)
+        h_ref[at, :] = normed
+        proj = dot(normed, w_ref[:, : 3 * cols], ((1,), (0,)))
         if i * BLOCK >= WINDOW:
-            q_ref[pl.ds(i * BLOCK - WINDOW, BLOCK), :] = (proj[:, :cols] * sc_ref[...]).astype(bf16)
+            q_ref[i * BLOCK - WINDOW : (i + 1) * BLOCK - WINDOW, :] = (
+                proj[:, :cols] * sc_ref[...]
+            ).astype(bf16)
         k_rows = proj[:, cols : 2 * cols].astype(bf16)
         v_rows = proj[:, 2 * cols :].astype(bf16)
         k_ref[at, :] = k_rows
@@ -186,28 +222,45 @@
         vt[:, at] = v_rows.T
         for h in range(heads):
             kh[h, at, :] = head_of(k_rows, h)
-
-    def block(b, carry):
-        q0 = pl.multiple_of(b * BLOCK, BLOCK)
-        k_place = q0 + lax.broadcasted_iota(jnp.int32, (SPAN, BLOCK), 0)
-        q_place = q0 + WINDOW + lax.broadcasted_iota(jnp.int32, (SPAN, BLOCK), 1)
-        seen = (k_place >= lo_ref[:, pl.ds(q0, BLOCK)]) & (k_place <= q_place)
-        bias[...] = jnp.where(seen, 0.0, NEGATIVE)
-        q_rows = q_ref[pl.ds(q0, BLOCK), :]
-        mixed = []
-        for h in range(heads):
-            q_head = head_of(q_rows, h)
-            s = dot(kh[h, pl.ds(q0, SPAN), :], q_head, ((1,), (1,))) + bias[...]
-            top = jnp.max(s, axis=0, keepdims=True)
-            p = jnp.exp(s - top)
-            total = jnp.sum(p, axis=0, keepdims=True)
-            part = dot(vt[h * HD : (h + 1) * HD, pl.ds(q0, SPAN)], p.astype(bf16), ((1,), (0,)))
-            mixed.append((part / total).T)
-            lse_ref[pl.ds(h, 1), pl.ds(q0, BLOCK)] = top + jnp.log(total)
-        c_ref[pl.ds(q0, BLOCK), :] = jnp.concatenate(mixed, axis=1).astype(bf16)
-        return carry
-
-    lax.fori_loop(0, rows // BLOCK, block, 0)
+    for source, target in ((h_ref, h_out), (q_ref, q_out), (k_ref, k_out), (v_ref, v_out)):
+        send(source, target)
+
+    steps = [(b, h) for b in range(rows // BLOCK) for h in range(heads)]
+
+    def begin(b, h):
+        if h == 0:
+            fill_bias(bias, b, lo_ref)
+        keys = slice(b * BLOCK, b * BLOCK + SPAN)
+        q_head = head_of(q_ref[b * BLOCK : (b + 1) * BLOCK, :], h)
+        return dot(kh[h, keys, :], q_head, ((1,), (1,))) + bias[b % 2]
+
+    ready, mixed = begin(*steps[0]), []
+    for i, (b, h) in enumerate(steps):
+        s = ready
+        if i + 1 < len(steps):
+            ready = begin(*steps[i + 1])
+        at, keys = slice(b * BLOCK, (b + 1) * BLOCK), slice(b * BLOCK, b * BLOCK + SPAN)
+        top = jnp.max(s, axis=0, keepdims=True)
+        p = jnp.exp(s - top)
+        total = jnp.sum(p, axis=0, keepdims=True)
+        part = dot(vt[h * HD : (h + 1) * HD, keys], p.astype(bf16), ((1,), (0,)))
+        mixed.append((part / total).T)
+        lse_ref[h : h + 1, at] = top + jnp.log(total)
+        if h == heads - 1:
+            c_ref[at, :] = jnp.concatenate(mixed, axis=1).astype(bf16)
+            mixed = []
+    for i, piece in enumerate(pieces):
+        share = piece.shape[0]
+        piece[...] = c_ref[pl.ds(pl.multiple_of(at_ref[spot + i], 16), share), :]
+    for copy in leave:
+        copy.wait()
+
+
+def fill_bias(bias, b, lo_ref):
+    k_place = b * BLOCK + lax.broadcasted_iota(jnp.int32, (SPAN, BLOCK), 0)
+    q_place = b * BLOCK + WINDOW + lax.broadcasted_iota(jnp.int32, (SPAN, BLOCK), 1)
+    seen = (k_place >= lo_ref[:, b * BLOCK : (b + 1) * BLOCK]) & (k_place <= q_place)
+    bias[b % 2] = jnp.where(seen, 0.0, NEGATIVE)
 
 
 def attend_back_kernel(heads, n_parts, at_ref, *refs):
@@ -216,7 +269,9 @@
     outs = refs[n_parts + 7 :]
     dq_ref, dkv_ref, part_ref = outs[:3]
     send_ref, keep_ref = outs[3:5]
-    kh, vh, kt, ht, g_ref, dk, dv, bias = outs[5:]
+    kh, vh, kt, ht, g_ref, dk, dv, bias, h_rows, sem = outs[5:]
+    arrive = pltpu.make_async_copy(h_ref, h_rows, sem)
+    arrive.start()
     rows, cols = q_ref.shape
     for i, part in enumerate(parts):
         share = part.shape[0]
@@ -225,41 +280,45 @@
     for h in range(heads):
         kh[h] = head_of(k_ref[...], h)
         vh[h] = head_of(v_ref[...], h)
-    dk[...] = jnp.zeros_like(dk)
-    dv[...] = jnp.zeros_like(dv)
     part_ref[...] = jnp.zeros_like(part_ref)
 
-    def block(b, carry):
-        q0 = pl.multiple_of(b * BLOCK, BLOCK)
-        at, keys = pl.ds(q0, BLOCK), pl.ds(q0, SPAN)
-        k_place = q0 + lax.broadcasted_iota(jnp.int32, (SPAN, BLOCK), 0)
-        q_place = q0 + WINDOW + lax.broadcasted_iota(jnp.int32, (SPAN, BLOCK), 1)
-        seen = (k_place >= lo_ref[:, at]) & (k_place <= q_place)
-        bias[...] = jnp.where(seen, 0.0, NEGATIVE)
-        q_rows, g_rows = q_ref[at, :], g_ref[at, :]
-        grads = []
-        for h in range(heads):
-            q_head = head_of(q_rows, h)
-            g_head = head_of(g_rows, h)
-            s = dot(kh[h, keys, :], q_head, ((1,), (1,))) + bias[...]
-            p = jnp.exp(s - lse_ref[pl.ds(h, 1), at])
-            dp = dot(vh[h, keys, :], g_head, ((1,), (1,)))
-            inner = jnp.sum(p * dp, axis=0, keepdims=True)
-            ds = (p * (dp - inner)).astype(bf16)
-            dv[h, keys, :] += dot(p.astype(bf16), g_head, ((1,), (0,)))
-            dk[h, keys, :] += dot(ds, q_head, ((1,), (0,)))
-            grads.append(dot(kt[h * HD : (h + 1) * HD, keys], ds, ((1,), (0,))).T)
-        grad = jnp.concatenate(grads, axis=1)
-        part_ref[...] += jnp.sum(grad * q_rows.astype(f32), axis=0, keepdims=True)
-        dq_ref[at, :] = (grad * sc_ref[...]).astype(bf16)
-        return carry
-
-    lax.fori_loop(0, rows // BLOCK, block, 0)
+    steps = [(b, h) for b in range(rows // BLOCK) for h in range(heads)]
+
+    def begin(b, h):
+        if h == 0:
+            fill_bias(bias, b, lo_ref)
+        at, keys = slice(b * BLOCK, (b + 1) * BLOCK), slice(b * BLOCK, b * BLOCK + SPAN)
+        q_head, g_head = head_of(q_ref[at, :], h), head_of(g_ref[at, :], h)
+        s = dot(kh[h, keys, :], q_head, ((1,), (1,))) + bias[b % 2]
+        return s, dot(vh[h, keys, :], g_head, ((1,), (1,))), q_head, g_head
+
+    ready, grads = begin(*steps[0]), []
+    for i, (b, h) in enumerate(steps):
+        s, dp, q_head, g_head = ready
+        if i + 1 < len(steps):
+            ready = begin(*steps[i + 1])
+        at, keys = slice(b * BLOCK, (b + 1) * BLOCK), slice(b * BLOCK, b * BLOCK + SPAN)
+        p = jnp.exp(s - lse_ref[h : h + 1, at])
+        inner = jnp.sum(p * dp, axis=0, keepdims=True)
+        ds = (p * (dp - inner)).astype(bf16)
+        g_value, g_key = dot(p.astype(bf16), g_head, ((1,), (0,))), dot(ds, q_head, ((1,), (0,)))
+        for table, part in ((dv, g_value), (dk, g_key)):
+            if b:
+                table[h, b * BLOCK : b * BLOCK + WINDOW, :] += part[:WINDOW]
+                table[h, b * BLOCK + WINDOW : b * BLOCK + SPAN, :] = part[WINDOW:]
+            else:
+                table[h, keys, :] = part
+        grads.append(dot(kt[h * HD : (h + 1) * HD, keys], ds, ((1,), (0,))).T)
+        if h == heads - 1:
+            grad, grads = jnp.concatenate(grads, axis=1), []
+            part_ref[...] += jnp.sum(grad * q_ref[at, :].astype(f32), axis=0, keepdims=True)
+            dq_ref[at, :] = (grad * sc_ref[...]).astype(bf16)
+    arrive.wait()
     for i in range(k_ref.shape[0] // BLOCK):
         at = pl.ds(i * BLOCK, BLOCK)
         both = [table[h, at, :HD] for table in (dk, dv) for h in range(heads)]
         dkv_ref[at, :] = jnp.concatenate(both, axis=1).astype(bf16)
-        ht[:, at] = h_ref[at, :].T
+        ht[:, at] = h_rows[at, :].T
     gw_q = dot(ht[:, WINDOW:], dq_ref[...], ((1,), (0,))).astype(bf16)
     gw_kv = dot(ht[...], dkv_ref[...], ((1,), (0,))).astype(bf16)
     outer, own, padded = send_ref.shape
@@ -508,25 +567,37 @@
     scale_cols = jnp.tile(factor, heads)[None, :]
     table = WINDOW + tok_dev
     pair_flops = tok_dev * SPAN * cols_own * 2
-    h_all, queries, key_rows, value_rows, context, log_totals, w_qkv = vmem_call(
-        functools.partial(attend_kernel, heads, (len(near), len(rims))),
+    stages = [pltpu.VMEM(part.shape, bf16) for part in (*near, *far)]
+    n_in = len(stages) + 1 + len(rims)
+    h_all, queries, key_rows, value_rows, w_qkv, log_totals, *ctx = vmem_call(
+        functools.partial(attend_kernel, heads, (len(near), len(rims), n_tensor)),
         (
             sds((table, width), bf16),
             sds((tok_dev, cols_own), bf16),
             sds((table, cols_own), bf16),
             sds((table, cols_own), bf16),
-            sds((tok_dev, cols_own), bf16),
+            sds((width, padded), bf16),
             sds((heads, tok_dev), f32),
-            sds((width, padded), bf16),
+            *[sds((share, cols_own), bf16) for _ in flips],
         ),
         [
+            pltpu.VMEM((table, width), bf16),
+            pltpu.VMEM((table, width), bf16),
+            pltpu.VMEM((width, padded), bf16),
+            pltpu.VMEM((tok_dev, cols_own), bf16),
+            pltpu.VMEM((table, cols_own), bf16),
+            pltpu.VMEM((table, cols_own), bf16),
             pltpu.VMEM((heads, table, LANES), bf16),
             pltpu.VMEM((cols_own, table), bf16),
-            pltpu.VMEM((SPAN, BLOCK), f32),
+            pltpu.VMEM((2, SPAN, BLOCK), f32),
+            pltpu.VMEM((tok_dev, cols_own), bf16),
+            *stages,
+            pltpu.SemaphoreType.DMA((n_in,)),
+            pltpu.SemaphoreType.DMA((5,)),
         ],
         2 * table * width * 3 * cols_own + 6 * pair_flops,
-        44,
-        jnp.stack([low, *spots_q, *spots_rim]),
+        56,
+        jnp.stack([low, *spots_q, *spots_rim, *spots_share]),
         tokens,
         *rims,
         *near,
@@ -534,15 +605,12 @@
         gains[:1],
         scale_cols,
         lo,
-    )
-
+        far_in=range(1, 1 + n_in),
+        far_out=range(5),
+    )
     for f in flips[2::2]:
-        mats[f + 1] = [hop(after(piece, context), "tensor", 1) for piece in mats[f]]
-
-    def share_of(values, f):
-        return lax.dynamic_slice_in_dim(values, (ten_index ^ f) * share, share, 0)
-
-    ctx = [share_of(context, f) for f in flips]
+        mats[f + 1] = [hop(after(piece, log_totals), "tensor", 1) for piece in mats[f]]
+
     ctx = [ctx[0]] + [hop(ctx[f], "tensor", f) for f in flips[1:]]
     shape_share = (share, width)
     outs = vmem_call(
@@ -608,7 +676,9 @@
             pltpu.VMEM((tok_dev, cols_own), bf16),
             pltpu.VMEM((heads, table, LANES), f32),
             pltpu.VMEM((heads, table, LANES), f32),
-            pltpu.VMEM((SPAN, BLOCK), f32),
+            pltpu.VMEM((2, SPAN, BLOCK), f32),
+            pltpu.VMEM((table, width), bf16),
+            pltpu.SemaphoreType.DMA,
         ],
         14 * pair_flops + 2 * table * width * 3 * cols_own,
         56,
@@ -621,6 +691,7 @@
         lo,
         log_totals,
         h_all,
+        far_in=[n_tensor + 7],
     )
     scale_part = (
         jnp.sum((scale_raw / scale_cols).reshape(heads, HD), axis=0)
@@ -641,7 +712,6 @@
         w_qkv,
     )
     turned_w = hop(grad_w[0], "seq", 1)
-    from_core_rows = hop(odd_rows, "tensor", 1)
 
     first = firsts[0].astype(f32)
     for part in came:
@@ -652,17 +722,22 @@
     sends = [second[i].astype(bf16) for i in range(1, n_even)]
     came_first = hop(send, "seq", 2)
     far_second = [hop(part, "tensor", 2 * i + 2) for i, part in enumerate(sends)]
-    from_core_rows = after(from_core_rows, far_second)
+    from_core_rows = hop(after(odd_rows, turned_w, came_first, far_second), "tensor", 1)
     sums = [even_rows[i].astype(f32) + from_core_rows[i].astype(f32) for i in range(n_even)]
     sum_sends = [part.astype(bf16) for part in sums[1:]]
 
-    rest = [0, *range(2, bits)]
+    parts_m, rest = [], [0, *range(2, bits)]
     first = keep_first + came_first.astype(f32)
     second = second[0]
     for part in far_second:
         second = second + part.astype(f32)
     second = second.reshape(*[2] * (bits - 1), rows_own, half)
-    both = jnp.concatenate([first, second], axis=-1)
+    for part, left, order in (
+        (first, rest, rest),
+        (second, rest, rest[::-1]),
+    ):
+        parts_m.append(scatter_seq(part, left, order))
+    sum_sends = after(sum_sends, turned_w, far_second)
     far_rim = [hop(part[:, :width], "tensor", 2 * i + 2) for i, part in enumerate(sum_sends)]
     rim_one, grad_one = sums[0][:, :width], sums[0][:, width:]
     for part in far_rim:
@@ -674,13 +749,20 @@
     for part in far_here:
         grad_one = grad_one + part.astype(f32)
     high = list(range(1, bits))
-    own_qkv = grad_w[1].astype(f32) + after(turned_w, sum_sends, came_first).astype(f32)
+    own_qkv = grad_w[1].astype(f32) + turned_w.astype(f32)
     own_qkv = own_qkv.reshape(*[2] * (bits - 1), *own_qkv.shape[1:])
-    keep_m, came_m = scatter_seq(both, rest, rest[::-1])
-    keep_w, came_w = scatter_seq(own_qkv, high, high, far_rim)
-    back = lax.ppermute(rim_one.astype(bf16), "seq", [(i, i - 1) for i in range(1, n_seq)])
-    grad_one = grad_one + back.astype(f32)
-    came_w = after(came_w, back)
+    send, keep_w = scatter_step(own_qkv, high, 1)
+    came_w = hop(send, "seq", 2)
+    keep_m, came_m = (jnp.concatenate(part, axis=1) for part in zip(*parts_m))
+    if bits > 2:
+        own_qkv = keep_w.astype(f32) + came_w.astype(f32)
+        keep_w, came_w = scatter_seq(own_qkv, high[1:], high[1:])
+    cut = (width // 512) * 128
+    to_last = [(i, i - 1) for i in range(1, n_seq)]
+    rim_low = rim_one.astype(bf16)
+    back = [lax.ppermute(part, "seq", to_last) for part in (rim_low[:, :cut], rim_low[:, cut:])]
+    grad_one = grad_one + jnp.concatenate(back, axis=1).astype(f32)
+    came_w = after(came_w, back[0], far_here)
     x_part = x_share.astype(f32)
     factor_one = lax.rsqrt(jnp.mean(x_part * x_part, axis=-1, keepdims=True) + EPSILON)
     norm_one = x_part * factor_one
@@ -716,7 +798,7 @@
         1e9,
         32,
         *grads,
-        summed(col_part, "seq"),
+        after(summed(col_part, "seq"), back),
         summed(row_part, "tensor"),
         col_second,
         row_second,

time: 353 us -> 339 us (0.960)
  waiting for transfers between devices: 129 us -> 118 us
  starting transfers between devices: 75.2 us -> 84.7 us
  Pallas kernels: 89.2 us -> 80 us
    ppermute x49 -> x51, waiting for transfers between devices: 124 us -> 107 us  [hop(): return lax.ppermute(value, axis, [(i, i ^ flip) for i in range(peers)])]
    pallas_call x8, Pallas kernels: 89.2 us -> 80 us  [vmem_call(): pl.pallas_call(body, out_shape=outs, in_specs=[scalars if a.ndim == 1 els...]
    ppermute x1 -> x2, waiting for transfers between devices: 0.01 us -> 6.23 us  [shards(): lax.ppermute(part, 'seq', to_last)]
    ppermute x49 -> x51, starting transfers between devices: 68.6 us -> 74.8 us  [hop(): return lax.ppermute(value, axis, [(i, i ^ flip) for i in range(peers)])]
    unnamed x110 -> x112, local copies, waits for them, and re-layouts: 16.2 us -> 16.9 us
  transfers between devices with their start and end apart: 52 -> 55, of which waited for: 24 -> 25; matrix products, arithmetic and copies ran while one was open for 9% -> 8% of each run, Pallas kernels for 22% -> 19%
where the time goes in v3:
time: 339 us; the launch traced here: 335 us
  waiting for transfers between devices  118 us (35%)
  starting transfers between devices  84.7 us (25%)
  Pallas kernels  80 us (24%)
  other arithmetic  27.4 us (8%)
  local copies, waits for them, and re-layouts  23.9 us (7%)
    ppermute x51, waiting for transfers between devices, hop(): return lax.ppermute(value, axis, [(i, i ^ flip) for i in range(peers)])  107 us
    pallas_call x8, Pallas kernels, vmem_call(): pl.pallas_call(body, out_shape=outs, in_specs=[scalars if a.ndim == 1 els...  80 us
    ppermute x51, starting transfers between devices, hop(): return lax.ppermute(value, axis, [(i, i ^ flip) for i in range(peers)])  74.8 us
    unnamed x112, local copies, waits for them, and re-layouts  16.9 us
  transfers between devices with their start and end apart: 55, of which 25 were waited for; matrix products, arithmetic and copies ran while one was open for 8% of the time, Pallas kernels for 19%

profile of v3, /device:TPU:0, one launch (start us, length us, event | category | flops | bytes accessed | tf_op | source)
XLA Modules:
  0.0 335.4 jit_solution(895074292590223894)
XLA Ops:
  3.4 4.1 %collective-permute-start.4 = (bf16[160,1024]{1,0:T(8,128)(2,1)S(1)}, bf16[160,1024]{1,0:T(8,128)(2,1)S(1)}, u32[]{:S(2)}, u32[]{:S(2)}) collective-permute-start(bf16[160,1024]{1,0:T(8,128)(2,1)S(1)} %get-tuple-element.169), channel_id=1, source_target_pairs={{0,16},{4,20},{8,24},{12,28},{16,0},{20,4},{24,8},{28,12},{1,17},{... | collective-permute-start | bytes 983048 | tf_op jit(solution)/shard_map/ppermute | solution.py:56
  7.6 1.6 collective-permute-start.6
  10.5 3.3 collective-permute-start
  13.8 1.8 collective-permute-start.12
  15.5 6.7 %collective-permute-done.4 = bf16[160,1024]{1,0:T(8,128)(2,1)S(1)} collective-permute-done((bf16[160,1024]{1,0:T(8,128)(2,1)S(1)}, bf16[160,1024]{1,0:T(8,128)(2,1)S(1)}, u32[]{:S(2)}, u32[]{:S(2)}) %collective-permute-start.4) | collective-permute-done | bytes 327712 | tf_op jit(solution)/shard_map/ppermute | solution.py:56
  23.2 11.8 %collective-permute-start.5 = (bf16[2,160,1024]{2,1,0:T(8,128)(2,1)S(1)}, bf16[2,160,1024]{2,1,0:T(8,128)(2,1)}, u32[]{:S(2)}, u32[]{:S(2)}) collective-permute-start(bf16[2,160,1024]{2,1,0:T(8,128)(2,1)S(1)} %pad_maximum_fusion.1), channel_id=1, source_target_pairs={{0,8},{4,12},{8,0},{12,4},{16,24},{20,28},{24,16},{28,20},{1,9},{5... | collective-permute-start | bytes 1966088 | tf_op jit(solution)/shard_map/ppermute | solution.py:56
  34.9 1.6 collective-permute-done.13
  36.5 1.8 collective-permute-start.14
  38.3 1.5 collective-permute-start.1
  40.9 4.6 %collective-permute-done.7.refs_10_ = bf16[1,160,1024]{2,1,0:T(8,128)(2,1)S(1)} collective-permute-done((bf16[1,160,1024]{2,1,0:T(8,128)(2,1)S(1)}, bf16[1,160,1024]{2,1,0:T(8,128)(2,1)S(1)}, u32[]{:S(2)}, u32[]{:S(2)}) %collective-permute-start.7) | collective-permute-done | bytes 327712 | tf_op jit(solution)/shard_map/ppermute | solution.py:56
  45.5 1.9 collective-permute-done.5.refs_8_
  47.4 8.0 %collective-permute-start.15 = (bf16[320,1024]{1,0:T(8,128)(2,1)}, bf16[320,1024]{1,0:T(8,128)(2,1)}, u32[]{:S(2)}, u32[]{:S(2)}) collective-permute-start(bf16[320,1024]{1,0:T(8,128)(2,1)} %get-tuple-element.83), channel_id=1, source_target_pairs={{0,8},{4,12},{8,0},{12,4},{16,24},{20,28},{24,16},{28,20},{1,9},{5... | collective-permute-start | bytes 1966088 | tf_op jit(solution)/shard_map/ppermute | solution.py:56
  61.2 8.9 %collective-permute-done.15 = bf16[320,1024]{1,0:T(8,128)(2,1)} collective-permute-done((bf16[320,1024]{1,0:T(8,128)(2,1)}, bf16[320,1024]{1,0:T(8,128)(2,1)}, u32[]{:S(2)}, u32[]{:S(2)}) %collective-permute-start.15) | collective-permute-done | bytes 655392 | tf_op jit(solution)/shard_map/ppermute | solution.py:56
  70.1 4.5 %collective-permute-done.16 = bf16[320,1024]{1,0:T(8,128)(2,1)S(1)} collective-permute-done((bf16[320,1024]{1,0:T(8,128)(2,1)}, bf16[320,1024]{1,0:T(8,128)(2,1)S(1)}, u32[]{:S(2)}, u32[]{:S(2)}) %collective-permute-start.16) | collective-permute-done | bytes 655392 | tf_op jit(solution)/shard_map/ppermute | solution.py:56
  75.1 12.4 %collective-permute-start.17 = (bf16[320,1024]{1,0:T(8,128)(2,1)}, bf16[320,1024]{1,0:T(8,128)(2,1)S(1)}, u32[]{:S(2)}, u32[]{:S(2)}) collective-permute-start(bf16[320,1024]{1,0:T(8,128)(2,1)} %get-tuple-element.85), channel_id=1, source_target_pairs={{0,8},{4,12},{8,0},{12,4},{16,24},{20,28},{24,16},{28,20},{1,9},{5... | collective-permute-start | bytes 1966088 | tf_op jit(solution)/shard_map/ppermute | solution.py:56
  91.5 8.9 %collective-permute-done.17 = bf16[320,1024]{1,0:T(8,128)(2,1)S(1)} collective-permute-done((bf16[320,1024]{1,0:T(8,128)(2,1)}, bf16[320,1024]{1,0:T(8,128)(2,1)S(1)}, u32[]{:S(2)}, u32[]{:S(2)}) %collective-permute-start.17) | collective-permute-done | bytes 655392 | tf_op jit(solution)/shard_map/ppermute | solution.py:56
  100.8 1.6 pad_maximum_fusion.refs_4_
  102.6 2.4 collective-permute-done.8.refs_11_
  106.7 19.8 %shard_map.251 = (bf16[2048,1280]{1,0:T(8,128)(2,1)}, bf16[1024,320]{1,0:T(8,128)(2,1)}, bf16[2048,320]{1,0:T(8,128)(2,1)}, bf16[2048,320]{1,0:T(8,128)(2,1)}, b...) custom-call(s32[13]{0:T(128)} %stack.92.refs_0_, ...), custom_call_target="tpu_custom_call" | custom-call | flops 80530636800 | bytes 19687732 | tf_op jit(solution)/shard_map/pallas_call | solution.py:40
  128.8 5.8 %collective-permute-done.10.refs_2_.refs_1_ = bf16[256,320]{1,0:T(8,128)(2,1)S(1)} collective-permute-done((bf16[256,320]{1,0:T(8,128)(2,1)}, bf16[256,320]{1,0:T(8,128)(2,1)S(1)}, u32[]{:S(2)}, u32[]{:S(2)}) %collective-permute-start.10) | collective-permute-done | bytes 163872 | tf_op jit(solution)/shard_map/ppermute | solution.py:56
  134.6 1.5 collective-permute-done.11.refs_3_
  137.4 1.6 collective-permute-done.24.refs_12_
  140.9 12.6 %shard_map.252 = (f32[256,1280]{1,0:T(8,128)}, f32[256,1280]{1,0:T(8,128)}, f32[1,1280]{1,0:T(1,128)S(1)}, bf16[2,256,1280]{2,1,0:T(8,128)(2,1)}, bf16[2,256,640...) custom-call(s32[4]{0:T(128)S(1)} %pad_add_fusion.at_ref, ...), custom_call_target="tpu_custom_call" | custom-call | flops 40265318400 | bytes 18360336 | tf_op jit(solution)/shard_map/pallas_call | solution.py:40
  158.5 1.4 collective-permute-done.32.refs_8_
  166.7 6.1 %shard_map.253 = (bf16[1280,512]{1,0:T(8,128)(2,1)S(1)}, bf16[1280,512]{1,0:T(8,128)(2,1)S(1)}, bf16[2,2,320,512]{3,2,1,0:T(8,128)(2,1)S(1)}, bf16[2,2,320,512]{3,2,1,0:T(8,128)(2,1)S(1)}) custom-call(s32[1]{0:T(128)} %bitcast.27.at_ref, bf16[256,320]{1,0:T(8,128)(2,1)S(1)} %copy-done.21, bf16[256,320]{1,0:T(8,128)(2,1)S(1)} %collective-permute-done.10.refs_2_.refs_1_, ...), custom_call_target="tpu_custom_call" | custom-call | flops 20132659200 | bytes 11141124 | tf_op jit(solution)/shard_map/pallas_call | solution.py:40
  175.6 29.3 %shard_map.254 = (bf16[1024,320]{1,0:T(8,128)(2,1)}, bf16[2048,640]{1,0:T(8,128)(2,1)}, f32[1,320]{1,0:T(1,128)}, bf16[4,160,1024]{2,1,0:T(8,128)(2,1)}, bf16[4,160,1024]{2,1,0:T(8,128)(2,1)}) custom-call(s32[5]{0:T(128)} %stack.100.at_ref, bf16[256,320]{1,0:T(8,128)(2,1)} %copy-done.22, bf16[256,320]{1,0:T(8,128)(2,1)} %collective-permute-done.26.refs_1_, ...), custom_call_target="tpu_custom_call" | custom-call | flops 134217728000 | bytes 15096340 | tf_op jit(solution)/shard_map/pallas_call | solution.py:40
  205.9 1.7 convert_add_fusion.2
  209.0 1.9 convert_add_fusion.1
  212.7 8.5 %shard_map.255 = (bf16[2,256,2560]{2,1,0:T(8,128)(2,1)S(1)}, bf16[2,256,2560]{2,1,0:T(8,128)(2,1)}) custom-call(s32[4]{0:T(128)S(1)} %pad_add_fusion.1.at_ref, bf16[1024,320]{1,0:T(8,128)(2,1)S(1)} %copy-done.19, bf16[2048,640]{1,0:T(8,128)(2,1)S(1)} %copy-done.16, bf16[1280,1024]{1,0:T(8,128)(2,1)} %get-tuple-element.112.w_ref), custom_call_target="tpu_custom_call" | custom-call | flops 33554432000 | bytes 11141136 | tf_op jit(solution)/shard_map/pallas_call | solution.py:40
  221.2 14.9 %collective-permute-done.33 = bf16[4,160,1024]{2,1,0:T(8,128)(2,1)} collective-permute-done((bf16[4,160,1024]{2,1,0:T(8,128)(2,1)}, bf16[4,160,1024]{2,1,0:T(8,128)(2,1)}, u32[]{:S(2)}, u32[]{:S(2)}) %collective-permute-start.33) | collective-permute-done | bytes 1310752 | tf_op jit(solution)/shard_map/ppermute | solution.py:56
  238.0 2.4 convert_add_fusion
  243.0 3.4 %collective-permute-start.46 = (bf16[2,160,512]{2,1,0:T(8,128)(2,1)S(1)}, bf16[2,160,512]{2,1,0:T(8,128)(2,1)S(1)}, u32[]{:S(2)}, u32[]{:S(2)}) collective-permute-start(bf16[2,160,512]{2,1,0:T(8,128)(2,1)S(1)} %fusion.18), channel_id=1, source_target_pairs={{0,16},{4,20},{8,24},{12,28},{16,0},{20,4},{24,8},{28,12},{1,17},{... | collective-permute-start | bytes 983048 | tf_op jit(solution)/shard_map/ppermute | solution.py:56
  246.5 18.3 %collective-permute-done.43 = bf16[2,160,1024]{2,1,0:T(8,128)(2,1)S(1)} collective-permute-done((bf16[2,160,1024]{2,1,0:T(8,128)(2,1)S(1)}, bf16[2,160,1024]{2,1,0:T(8,128)(2,1)S(1)}, u32[]{:S(2)}, u32[]{:S(2)}) %collective-permute-start.43) | collective-permute-done | bytes 655392 | tf_op jit(solution)/shard_map/ppermute | solution.py:56
  265.1 1.8 collective-permute-start.44
  267.1 2.3 fusion.9
  272.7 12.9 %collective-permute-done.39 = bf16[256,1280]{1,0:T(8,128)(2,1)S(1)} collective-permute-done((bf16[256,1280]{1,0:T(8,128)(2,1)S(1)}, bf16[256,1280]{1,0:T(8,128)(2,1)S(1)}, u32[]{:S(2)}, u32[]{:S(2)}) %collective-permute-start.39) | collective-permute-done | bytes 655392 | tf_op jit(solution)/shard_map/ppermute | solution.py:56
  289.5 1.4 collective-permute-start.42
  291.0 3.8 %collective-permute-done.41 = bf16[256,256]{1,0:T(8,128)(2,1)S(1)} collective-permute-done((bf16[256,256]{1,0:T(8,128)(2,1)S(1)}, bf16[256,256]{1,0:T(8,128)(2,1)S(1)}, u32[]{:S(2)}, u32[]{:S(2)}) %collective-permute-start.41) | collective-permute-done | bytes 131104 | tf_op jit(solution)/shard_map/ppermute | solution.py:763
  294.8 6.0 %collective-permute-done.40 = bf16[256,1280]{1,0:T(8,128)(2,1)S(1)} collective-permute-done((bf16[256,1280]{1,0:T(8,128)(2,1)S(1)}, bf16[256,1280]{1,0:T(8,128)(2,1)S(1)}, u32[]{:S(2)}, u32[]{:S(2)}) %collective-permute-start.40) | collective-permute-done | bytes 655392 | tf_op jit(solution)/shard_map/ppermute | solution.py:56
  300.8 1.3 shard_map.256
  302.8 2.4 collective-permute-done.42
  306.0 2.3 collective-permute-start.50
  310.0 1.7 collective-permute-start.51
  312.1 2.5 collective-permute-done.51
  317.7 3.9 %all-to-all-start = ((f32[32,8,128]{2,1,0:T(8,128)}), f32[32,8,128]{2,1,0:T(8,128)S(1)}, u32[]{:S(2)}, u32[]{:S(2)}) async-start(f32[32,8,128]{2,1,0:T(8,128)} %bitcast.51), calls=%async_computation | async-start | bytes 262144 | tf_op jit(solution)/shard_map/all_to_all | solution.py:823
  321.6 3.7 %fusion.6 = f32[256,1280]{1,0:T(8,128)} fusion(f32[256,1280]{1,0:T(8,128)} %get-tuple-element.94, bf16[256,1280]{1,0:T(8,128)(2,1)S(1)} %get-tuple-element.147.refs_14_, f32[256]{0:T(256)S(1)} %broadcast_multiply_fusion, f32[1280]{0:T(1024)S(1)} %copy-done.37, f32[256]{0:T(256)S(1)} %copy-done.39, bf16[256,1024]{1,0:T(8,128)(2,1)} %copy-done.30, ...), kind=kLoop, calls=%fused_computation.14 | loop fusion | flops 4587520 | bytes 5905408 | tf_op jit(solution)/shard_map/add | solution.py:771
  325.3 4.5 %all-to-all-done = f32[32,8,128]{2,1,0:T(8,128)S(1)} async-done(((f32[32,8,128]{2,1,0:T(8,128)}), f32[32,8,128]{2,1,0:T(8,128)S(1)}, u32[]{:S(2)}, u32[]{:S(2)}) %all-to-all-start) | async-done | bytes 131104 | tf_op jit(solution)/shard_map/all_to_all | solution.py:823
  331.2 1.4 copy-done.15
  (272 shorter events, 65.3 us)
Async XLA Ops:
  3.4 18.8 %collective-permute-start.4 = (bf16[160,1024]{1,0:T(8,128)(2,1)S(1)}, bf16[160,1024]{1,0:T(8,128)(2,1)S(1)}, u32[]{:S(2)}, u32[]{:S(2)}) collective-permute-start(bf16[160,1024]{1,0:T(8,128)(2,1)S(1)} %get-tuple-element.169), channel_id=1, source_target_pairs={{0,16},{4,20},{8,24},{12,28},{16,0},{20,4},{24,8},{28,12},{1,17},{... | collective-permute-start | bytes 983048 | tf_op jit(solution)/shard_map/ppermute | solution.py:56
  7.6 14.6 %collective-permute-start.6 = (bf16[1,160,1024]{2,1,0:T(8,128)(2,1)S(1)}, bf16[1,160,1024]{2,1,0:T(8,128)(2,1)S(1)}, u32[]{:S(2)}, u32[]{:S(2)}) collective-permute-start(bf16[1,160,1024]{2,1,0:T(8,128)(2,1)S(1)} %pad_maximum_fusion.5.refs_6_), channel_id=1, source_target_pairs={{0,4},{4,0},{8,12},{12,8},{16,20},{20,16},{24,28},{28,24},{1,5},{5... | collective-permute-start | bytes 983048 | tf_op jit(solution)/shard_map/ppermute | solution.py:56
  10.5 27.8 %collective-permute-start = (bf16[256,1280]{1,0:T(8,128)(2,1)S(1)}, bf16[256,1280]{1,0:T(8,128)(2,1)}, u32[]{:S(2)}, u32[]{:S(2)}) collective-permute-start(bf16[256,1280]{1,0:T(8,128)(2,1)S(1)} %get-tuple-element.147.refs_14_), channel_id=1, source_target_pairs={{0,4},{4,8},{8,12},{12,16},{16,20},{20,24},{24,28},{1,5},{5,9},{9,... | collective-permute-start | bytes 1966088 | tf_op jit(solution)/shard_map/ppermute | solution.py:526
  13.8 26.0 %collective-permute-start.12 = (bf16[160,1024]{1,0:T(8,128)(2,1)S(1)}, bf16[160,1024]{1,0:T(8,128)(2,1)S(1)}, u32[]{:S(2)}, u32[]{:S(2)}) collective-permute-start(bf16[160,1024]{1,0:T(8,128)(2,1)S(1)} %get-tuple-element.81), channel_id=1, source_target_pairs={{0,4},{4,0},{8,12},{12,8},{16,20},{20,16},{24,28},{28,24},{1,5},{5... | collective-permute-start | bytes 983048 | tf_op jit(solution)/shard_map/ppermute | solution.py:56
  23.0 13.5 %collective-permute-start.13 = (bf16[160,1024]{1,0:T(8,128)(2,1)S(1)}, bf16[160,1024]{1,0:T(8,128)(2,1)}, u32[]{:S(2)}, u32[]{:S(2)}) collective-permute-start(bf16[160,1024]{1,0:T(8,128)(2,1)S(1)} %get-tuple-element.81), channel_id=1, source_target_pairs={{0,16},{4,20},{8,24},{12,28},{16,0},{20,4},{24,8},{28,12},{1,17},{... | collective-permute-start | bytes 983048 | tf_op jit(solution)/shard_map/ppermute | solution.py:56
  23.2 24.2 %collective-permute-start.5 = (bf16[2,160,1024]{2,1,0:T(8,128)(2,1)S(1)}, bf16[2,160,1024]{2,1,0:T(8,128)(2,1)}, u32[]{:S(2)}, u32[]{:S(2)}) collective-permute-start(bf16[2,160,1024]{2,1,0:T(8,128)(2,1)S(1)} %pad_maximum_fusion.1), channel_id=1, source_target_pairs={{0,8},{4,12},{8,0},{12,4},{16,24},{20,28},{24,16},{28,20},{1,9},{5... | collective-permute-start | bytes 1966088 | tf_op jit(solution)/shard_map/ppermute | solution.py:56
  34.9 10.5 %collective-permute-start.7 = (bf16[1,160,1024]{2,1,0:T(8,128)(2,1)S(1)}, bf16[1,160,1024]{2,1,0:T(8,128)(2,1)S(1)}, u32[]{:S(2)}, u32[]{:S(2)}) collective-permute-start(bf16[1,160,1024]{2,1,0:T(8,128)(2,1)S(1)} %bitcast.102), channel_id=1, source_target_pairs={{0,4},{4,0},{8,12},{12,8},{16,20},{20,16},{24,28},{28,24},{1,5},{5... | collective-permute-start | bytes 983048 | tf_op jit(solution)/shard_map/ppermute | solution.py:56
  36.5 18.9 %collective-permute-start.14 = (bf16[160,1024]{1,0:T(8,128)(2,1)}, bf16[160,1024]{1,0:T(8,128)(2,1)S(1)}, u32[]{:S(2)}, u32[]{:S(2)}) collective-permute-start(bf16[160,1024]{1,0:T(8,128)(2,1)} %collective-permute-done.13), channel_id=1, source_target_pairs={{0,4},{4,0},{8,12},{12,8},{16,20},{20,16},{24,28},{28,24},{1,5},{5... | collective-permute-start | bytes 983048 | tf_op jit(solution)/shard_map/ppermute | solution.py:56
  38.3 19.3 %collective-permute-start.1 = (bf16[256,1280]{1,0:T(8,128)(2,1)}, bf16[256,1280]{1,0:T(8,128)(2,1)S(1)}, u32[]{:S(2)}, u32[]{:S(2)}) collective-permute-start(bf16[256,1280]{1,0:T(8,128)(2,1)} %collective-permute-done.refs_2_), channel_id=1, source_target_pairs={{0,2},{1,3},{2,0},{3,1},{4,6},{5,7},{6,4},{7,5},{8,10},{9,11},{10,... | collective-permute-start | bytes 1966088 | tf_op jit(solution)/shard_map/ppermute | solution.py:56
  47.4 22.7 %collective-permute-start.15 = (bf16[320,1024]{1,0:T(8,128)(2,1)}, bf16[320,1024]{1,0:T(8,128)(2,1)}, u32[]{:S(2)}, u32[]{:S(2)}) collective-permute-start(bf16[320,1024]{1,0:T(8,128)(2,1)} %get-tuple-element.83), channel_id=1, source_target_pairs={{0,8},{4,12},{8,0},{12,4},{16,24},{20,28},{24,16},{28,20},{1,9},{5... | collective-permute-start | bytes 1966088 | tf_op jit(solution)/shard_map/ppermute | solution.py:56
  58.5 16.0 %collective-permute-start.16 = (bf16[320,1024]{1,0:T(8,128)(2,1)}, bf16[320,1024]{1,0:T(8,128)(2,1)S(1)}, u32[]{:S(2)}, u32[]{:S(2)}) collective-permute-start(bf16[320,1024]{1,0:T(8,128)(2,1)} %get-tuple-element.85), channel_id=1, source_target_pairs={{0,2},{1,3},{2,0},{3,1},{4,6},{5,7},{6,4},{7,5},{8,10},{9,11},{10,... | collective-permute-start | bytes 1966088 | tf_op jit(solution)/shard_map/ppermute | solution.py:56
  74.5 16.4 %collective-permute-start.20 = (bf16[320,1024]{1,0:T(8,128)(2,1)}, bf16[320,1024]{1,0:T(8,128)(2,1)S(1)}, u32[]{:S(2)}, u32[]{:S(2)}) collective-permute-start(bf16[320,1024]{1,0:T(8,128)(2,1)} %collective-permute-done.15), channel_id=1, source_target_pairs={{0,2},{1,3},{2,0},{3,1},{4,6},{5,7},{6,4},{7,5},{8,10},{9,11},{10,... | collective-permute-start | bytes 1966088 | tf_op jit(solution)/shard_map/ppermute | solution.py:56
  75.1 25.2 %collective-permute-start.17 = (bf16[320,1024]{1,0:T(8,128)(2,1)}, bf16[320,1024]{1,0:T(8,128)(2,1)S(1)}, u32[]{:S(2)}, u32[]{:S(2)}) collective-permute-start(bf16[320,1024]{1,0:T(8,128)(2,1)} %get-tuple-element.85), channel_id=1, source_target_pairs={{0,8},{4,12},{8,0},{12,4},{16,24},{20,28},{24,16},{28,20},{1,9},{5... | collective-permute-start | bytes 1966088 | tf_op jit(solution)/shard_map/ppermute | solution.py:56
  87.6 14.9 %collective-permute-start.2 = (bf16[256,1280]{1,0:T(8,128)(2,1)}, bf16[256,1280]{1,0:T(8,128)(2,1)S(1)}, u32[]{:S(2)}, u32[]{:S(2)}) collective-permute-start(bf16[256,1280]{1,0:T(8,128)(2,1)} %collective-permute-done.refs_2_), channel_id=1, source_target_pairs={{0,1},{1,0},{2,3},{3,2},{4,5},{5,4},{6,7},{7,6},{8,9},{9,8},{10,11... | collective-permute-start | bytes 1966088 | tf_op jit(solution)/shard_map/ppermute | solution.py:56
  87.6 17.4 %collective-permute-start.8 = (bf16[2,160,1024]{2,1,0:T(8,128)(2,1)}, bf16[2,160,1024]{2,1,0:T(8,128)(2,1)S(1)}, u32[]{:S(2)}, u32[]{:S(2)}) collective-permute-start(bf16[2,160,1024]{2,1,0:T(8,128)(2,1)} %collective-permute-done.5.refs_8_), channel_id=1, source_target_pairs={{0,4},{4,0},{8,12},{12,8},{16,20},{20,16},{24,28},{28,24},{1,5},{5... | collective-permute-start | bytes 1966088 | tf_op jit(solution)/shard_map/ppermute | solution.py:56
  88.3 16.7 %collective-permute-start.3 = (bf16[256,1280]{1,0:T(8,128)(2,1)}, bf16[256,1280]{1,0:T(8,128)(2,1)S(1)}, u32[]{:S(2)}, u32[]{:S(2)}) collective-permute-start(bf16[256,1280]{1,0:T(8,128)(2,1)} %copy-done.48), channel_id=1, source_target_pairs={{0,1},{1,0},{2,3},{3,2},{4,5},{5,4},{6,7},{7,6},{8,9},{9,8},{10,11... | collective-permute-start | bytes 1966088 | tf_op jit(solution)/shard_map/ppermute | solution.py:56
  90.9 36.7 %collective-permute-start.19 = (bf16[320,1024]{1,0:T(8,128)(2,1)}, bf16[320,1024]{1,0:T(8,128)(2,1)S(1)}, u32[]{:S(2)}, u32[]{:S(2)}) collective-permute-start(bf16[320,1024]{1,0:T(8,128)(2,1)} %get-tuple-element.83), channel_id=1, source_target_pairs={{0,2},{1,3},{2,0},{3,1},{4,6},{5,7},{6,4},{7,5},{8,10},{9,11},{10,... | collective-permute-start | bytes 1966088 | tf_op jit(solution)/shard_map/ppermute | solution.py:56
  100.3 28.4 %collective-permute-start.21 = (bf16[320,1024]{1,0:T(8,128)(2,1)S(1)}, bf16[320,1024]{1,0:T(8,128)(2,1)S(1)}, u32[]{:S(2)}, u32[]{:S(2)}) collective-permute-start(bf16[320,1024]{1,0:T(8,128)(2,1)S(1)} %collective-permute-done.17), channel_id=1, source_target_pairs={{0,2},{1,3},{2,0},{3,1},{4,6},{5,7},{6,4},{7,5},{8,10},{9,11},{10,... | collective-permute-start | bytes 1966088 | tf_op jit(solution)/shard_map/ppermute | solution.py:56
  102.5 37.5 %collective-permute-start.18 = (bf16[4,320,1024]{2,1,0:T(8,128)(2,1)S(1)}, bf16[4,320,1024]{2,1,0:T(8,128)(2,1)}, u32[]{:S(2)}, u32[]{:S(2)}) collective-permute-start(bf16[4,320,1024]{2,1,0:T(8,128)(2,1)S(1)} %pad_maximum_fusion.refs_4_), channel_id=1, source_target_pairs={{0,1},{1,0},{2,3},{3,2},{4,5},{5,4},{6,7},{7,6},{8,9},{9,8},{10,11... | collective-permute-start | bytes 7864328 | tf_op jit(solution)/shard_map/ppermute | solution.py:56
  126.5 8.1 %collective-permute-start.10 = (bf16[256,320]{1,0:T(8,128)(2,1)}, bf16[256,320]{1,0:T(8,128)(2,1)S(1)}, u32[]{:S(2)}, u32[]{:S(2)}) collective-permute-start(bf16[256,320]{1,0:T(8,128)(2,1)} %get-tuple-element.79), channel_id=1, source_target_pairs={{0,2},{1,3},{2,0},{3,1},{4,6},{5,7},{6,4},{7,5},{8,10},{9,11},{10,... | collective-permute-start | bytes 491528 | tf_op jit(solution)/shard_map/ppermute | solution.py:56
  127.1 9.0 %collective-permute-start.11 = (bf16[256,320]{1,0:T(8,128)(2,1)}, bf16[256,320]{1,0:T(8,128)(2,1)S(1)}, u32[]{:S(2)}, u32[]{:S(2)}) collective-permute-start(bf16[256,320]{1,0:T(8,128)(2,1)} %get-tuple-element.80), channel_id=1, source_target_pairs={{0,3},{1,2},{2,1},{3,0},{4,7},{5,6},{6,5},{7,4},{8,11},{9,10},{10,... | collective-permute-start | bytes 491528 | tf_op jit(solution)/shard_map/ppermute | solution.py:56
  127.6 9.7 %collective-permute-start.9 = (bf16[256,320]{1,0:T(8,128)(2,1)}, bf16[256,320]{1,0:T(8,128)(2,1)S(1)}, u32[]{:S(2)}, u32[]{:S(2)}) collective-permute-start(bf16[256,320]{1,0:T(8,128)(2,1)} %get-tuple-element.78), channel_id=1, source_target_pairs={{0,1},{1,0},{2,3},{3,2},{4,5},{5,4},{6,7},{7,6},{8,9},{9,8},{10,11... | collective-permute-start | bytes 491528 | tf_op jit(solution)/shard_map/ppermute | solution.py:56
  128.8 8.6 %collective-permute-start.23 = (bf16[1,320,1024]{2,1,0:T(8,128)(2,1)S(1)}, bf16[1,320,1024]{2,1,0:T(8,128)(2,1)S(1)}, u32[]{:S(2)}, u32[]{:S(2)}) collective-permute-start(bf16[1,320,1024]{2,1,0:T(8,128)(2,1)S(1)} %bitcast.83), channel_id=1, source_target_pairs={{0,1},{1,0},{2,3},{3,2},{4,5},{5,4},{6,7},{7,6},{8,9},{9,8},{10,11... | collective-permute-start | bytes 1966088 | tf_op jit(solution)/shard_map/ppermute | solution.py:56
  155.0 7.2 %collective-permute-start.30 = (bf16[2,256,1280]{2,1,0:T(8,128)(2,1)}, bf16[2,256,1280]{2,1,0:T(8,128)(2,1)}, u32[]{:S(2)}, u32[]{:S(2)}) collective-permute-start(bf16[2,256,1280]{2,1,0:T(8,128)(2,1)} %get-tuple-element.102.refs_3_), channel_id=1, source_target_pairs={{0,1},{1,0},{2,3},{3,2},{4,5},{5,4},{6,7},{7,6},{8,9},{9,8},{10,11... | collective-permute-start | bytes 3932168 | tf_op jit(solution)/shard_map/ppermute | solution.py:56
  155.4 4.5 %collective-permute-start.32 = (bf16[256,1280]{1,0:T(8,128)(2,1)S(1)}, bf16[256,1280]{1,0:T(8,128)(2,1)S(1)}, u32[]{:S(2)}, u32[]{:S(2)}) collective-permute-start(bf16[256,1280]{1,0:T(8,128)(2,1)S(1)} %copy-done.7), channel_id=1, source_target_pairs={{0,1},{1,0},{2,3},{3,2},{4,5},{5,4},{6,7},{7,6},{8,9},{9,8},{10,11... | collective-permute-start | bytes 1966088 | tf_op jit(solution)/shard_map/ppermute | solution.py:56
  155.6 5.9 %collective-permute-start.31 = (bf16[2,256,640]{2,1,0:T(8,128)(2,1)}, bf16[2,256,640]{2,1,0:T(8,128)(2,1)S(1)}, u32[]{:S(2)}, u32[]{:S(2)}) collective-permute-start(bf16[2,256,640]{2,1,0:T(8,128)(2,1)} %get-tuple-element.104), channel_id=1, source_target_pairs={{0,1},{1,0},{2,3},{3,2},{4,5},{5,4},{6,7},{7,6},{8,9},{9,8},{10,11... | collective-permute-start | bytes 1966088 | tf_op jit(solution)/shard_map/ppermute | solution.py:56
  158.1 16.7 %collective-permute-start.26 = (bf16[256,320]{1,0:T(8,128)(2,1)}, bf16[256,320]{1,0:T(8,128)(2,1)}, u32[]{:S(2)}, u32[]{:S(2)}) collective-permute-start(bf16[256,320]{1,0:T(8,128)(2,1)} %get-tuple-element.96), channel_id=1, source_target_pairs={{0,1},{1,0},{2,3},{3,2},{4,5},{5,4},{6,7},{7,6},{8,9},{9,8},{10,11... | collective-permute-start | bytes 491528 | tf_op jit(solution)/shard_map/ppermute | solution.py:56
  160.0 14.9 %collective-permute-start.27 = (bf16[256,320]{1,0:T(8,128)(2,1)}, bf16[256,320]{1,0:T(8,128)(2,1)}, u32[]{:S(2)}, u32[]{:S(2)}) collective-permute-start(bf16[256,320]{1,0:T(8,128)(2,1)} %get-tuple-element.97), channel_id=1, source_target_pairs={{0,2},{1,3},{2,0},{3,1},{4,6},{5,7},{6,4},{7,5},{8,10},{9,11},{10,... | collective-permute-start | bytes 491528 | tf_op jit(solution)/shard_map/ppermute | solution.py:56
  160.7 14.2 %collective-permute-start.28 = (bf16[256,320]{1,0:T(8,128)(2,1)}, bf16[256,320]{1,0:T(8,128)(2,1)S(1)}, u32[]{:S(2)}, u32[]{:S(2)}) collective-permute-start(bf16[256,320]{1,0:T(8,128)(2,1)} %get-tuple-element.98), channel_id=1, source_target_pairs={{0,3},{1,2},{2,1},{3,0},{4,7},{5,6},{6,5},{7,4},{8,11},{9,10},{10,... | collective-permute-start | bytes 491528 | tf_op jit(solution)/shard_map/ppermute | solution.py:56
  172.9 33.0 %collective-permute-start.34 = (bf16[1280,512]{1,0:T(8,128)(2,1)S(1)}, bf16[1280,512]{1,0:T(8,128)(2,1)}, u32[]{:S(2)}, u32[]{:S(2)}) collective-permute-start(bf16[1280,512]{1,0:T(8,128)(2,1)S(1)} %get-tuple-element.106), channel_id=1, source_target_pairs={{0,2},{1,3},{2,0},{3,1},{4,6},{5,7},{6,4},{7,5},{8,10},{9,11},{10,... | collective-permute-start | bytes 3932168 | tf_op jit(solution)/shard_map/ppermute | solution.py:56
  174.1 34.6 %collective-permute-start.36 = (bf16[2,2,320,512]{3,2,1,0:T(8,128)(2,1)S(1)}, bf16[2,2,320,512]{3,2,1,0:T(8,128)(2,1)}, u32[]{:S(2)}, u32[]{:S(2)}) collective-permute-start(bf16[2,2,320,512]{3,2,1,0:T(8,128)(2,1)S(1)} %get-tuple-element.107), channel_id=1, source_target_pairs={{0,8},{4,12},{8,0},{12,4},{16,24},{20,28},{24,16},{28,20},{1,9},{5... | collective-permute-start | bytes 3932168 | tf_op jit(solution)/shard_map/ppermute | solution.py:56
  204.9 31.1 %collective-permute-start.33 = (bf16[4,160,1024]{2,1,0:T(8,128)(2,1)}, bf16[4,160,1024]{2,1,0:T(8,128)(2,1)}, u32[]{:S(2)}, u32[]{:S(2)}) collective-permute-start(bf16[4,160,1024]{2,1,0:T(8,128)(2,1)} %get-tuple-element.115), channel_id=1, source_target_pairs={{0,4},{4,0},{8,12},{12,8},{16,20},{20,16},{24,28},{28,24},{1,5},{5... | collective-permute-start | bytes 3932168 | tf_op jit(solution)/shard_map/ppermute | solution.py:56
  207.7 28.3 %collective-permute-start.35 = (bf16[2,2,160,512]{3,2,0,1:T(8,128)(2,1)S(1)}, bf16[2,2,160,512]{3,2,0,1:T(8,128)(2,1)S(1)}, u32[]{:S(2)}, u32[]{:S(2)}) collective-permute-start(bf16[2,2,160,512]{3,2,0,1:T(8,128)(2,1)S(1)} %fusion.13), channel_id=1, source_target_pairs={{0,8},{4,12},{8,0},{12,4},{16,24},{20,28},{24,16},{28,20},{1,9},{5... | collective-permute-start | bytes 1966088 | tf_op jit(solution)/shard_map/ppermute | solution.py:56
  211.0 25.0 %collective-permute-start.37 = (bf16[2,320,512]{2,1,0:T(8,128)(2,1)S(1)}, bf16[2,320,512]{2,1,0:T(8,128)(2,1)S(1)}, u32[]{:S(2)}, u32[]{:S(2)}) collective-permute-start(bf16[2,320,512]{2,1,0:T(8,128)(2,1)S(1)} %fusion.15), channel_id=1, source_target_pairs={{0,2},{1,3},{2,0},{3,1},{4,6},{5,7},{6,4},{7,5},{8,10},{9,11},{10,... | collective-permute-start | bytes 1966088 | tf_op jit(solution)/shard_map/ppermute | solution.py:56
  237.7 29.4 %collective-permute-start.38 = (bf16[2,256,2560]{2,1,0:T(8,128)(2,1)}, bf16[2,256,2560]{2,1,0:T(8,128)(2,1)}, u32[]{:S(2)}, u32[]{:S(2)}) collective-permute-start(bf16[2,256,2560]{2,1,0:T(8,128)(2,1)} %get-tuple-element.117), channel_id=1, source_target_pairs={{0,1},{1,0},{2,3},{3,2},{4,5},{5,4},{6,7},{7,6},{8,9},{9,8},{10,11... | collective-permute-start | bytes 7864328 | tf_op jit(solution)/shard_map/ppermute | solution.py:56
  240.5 24.2 %collective-permute-start.43 = (bf16[2,160,1024]{2,1,0:T(8,128)(2,1)S(1)}, bf16[2,160,1024]{2,1,0:T(8,128)(2,1)S(1)}, u32[]{:S(2)}, u32[]{:S(2)}) collective-permute-start(bf16[2,160,1024]{2,1,0:T(8,128)(2,1)S(1)} %fusion.14), channel_id=1, source_target_pairs={{0,8},{4,12},{8,0},{12,4},{16,24},{20,28},{24,16},{28,20},{1,9},{5... | collective-permute-start | bytes 1966088 | tf_op jit(solution)/shard_map/ppermute | solution.py:56
  241.8 25.2 %collective-permute-start.45 = (bf16[2,160,512]{2,1,0:T(8,128)(2,1)S(1)}, bf16[2,160,512]{2,1,0:T(8,128)(2,1)S(1)}, u32[]{:S(2)}, u32[]{:S(2)}) collective-permute-start(bf16[2,160,512]{2,1,0:T(8,128)(2,1)S(1)} %fusion.17), channel_id=1, source_target_pairs={{0,4},{4,0},{8,12},{12,8},{16,20},{20,16},{24,28},{28,24},{1,5},{5... | collective-permute-start | bytes 983048 | tf_op jit(solution)/shard_map/ppermute | solution.py:56
  243.0 28.5 %collective-permute-start.46 = (bf16[2,160,512]{2,1,0:T(8,128)(2,1)S(1)}, bf16[2,160,512]{2,1,0:T(8,128)(2,1)S(1)}, u32[]{:S(2)}, u32[]{:S(2)}) collective-permute-start(bf16[2,160,512]{2,1,0:T(8,128)(2,1)S(1)} %fusion.18), channel_id=1, source_target_pairs={{0,16},{4,20},{8,24},{12,28},{16,0},{20,4},{24,8},{28,12},{1,17},{... | collective-permute-start | bytes 983048 | tf_op jit(solution)/shard_map/ppermute | solution.py:56
  265.1 25.9 %collective-permute-start.44 = (bf16[160,1024]{1,0:T(8,128)(2,1)S(1)}, bf16[160,1024]{1,0:T(8,128)(2,1)S(1)}, u32[]{:S(2)}, u32[]{:S(2)}) collective-permute-start(bf16[160,1024]{1,0:T(8,128)(2,1)S(1)} %fusion.16), channel_id=1, source_target_pairs={{0,16},{4,20},{8,24},{12,28},{16,0},{20,4},{24,8},{28,12},{1,17},{... | collective-permute-start | bytes 983048 | tf_op jit(solution)/shard_map/ppermute | solution.py:56
  269.5 16.1 %collective-permute-start.39 = (bf16[256,1280]{1,0:T(8,128)(2,1)S(1)}, bf16[256,1280]{1,0:T(8,128)(2,1)S(1)}, u32[]{:S(2)}, u32[]{:S(2)}) collective-permute-start(bf16[256,1280]{1,0:T(8,128)(2,1)S(1)} %get-tuple-element.151), channel_id=1, source_target_pairs={{0,2},{1,3},{2,0},{3,1},{4,6},{5,7},{6,4},{7,5},{8,10},{9,11},{10,... | collective-permute-start | bytes 1966088 | tf_op jit(solution)/shard_map/ppermute | solution.py:56
  270.8 18.6 %collective-permute-start.47 = (bf16[160,512]{1,0:T(8,128)(2,1)S(1)}, bf16[160,512]{1,0:T(8,128)(2,1)S(1)}, u32[]{:S(2)}, u32[]{:S(2)}) collective-permute-start(bf16[160,512]{1,0:T(8,128)(2,1)S(1)} %fusion.19), channel_id=1, source_target_pairs={{0,16},{4,20},{8,24},{12,28},{16,0},{20,4},{24,8},{28,12},{1,17},{... | collective-permute-start | bytes 491528 | tf_op jit(solution)/shard_map/ppermute | solution.py:56
  271.7 17.7 %collective-permute-start.48 = (bf16[160,512]{1,0:T(8,128)(2,1)S(1)}, bf16[160,512]{1,0:T(8,128)(2,1)S(1)}, u32[]{:S(2)}, u32[]{:S(2)}) collective-permute-start(bf16[160,512]{1,0:T(8,128)(2,1)S(1)} %fusion.20), channel_id=1, source_target_pairs={{0,4},{4,0},{8,12},{12,8},{16,20},{20,16},{24,28},{28,24},{1,5},{5... | collective-permute-start | bytes 491528 | tf_op jit(solution)/shard_map/ppermute | solution.py:56
  285.6 15.2 %collective-permute-start.40 = (bf16[256,1280]{1,0:T(8,128)(2,1)S(1)}, bf16[256,1280]{1,0:T(8,128)(2,1)S(1)}, u32[]{:S(2)}, u32[]{:S(2)}) collective-permute-start(bf16[256,1280]{1,0:T(8,128)(2,1)S(1)} %get-tuple-element.119), channel_id=1, source_target_pairs={{0,2},{1,3},{2,0},{3,1},{4,6},{5,7},{6,4},{7,5},{8,10},{9,11},{10,... | collective-permute-start | bytes 1966088 | tf_op jit(solution)/shard_map/ppermute | solution.py:56
  287.1 7.8 %collective-permute-start.41 = (bf16[256,256]{1,0:T(8,128)(2,1)S(1)}, bf16[256,256]{1,0:T(8,128)(2,1)S(1)}, u32[]{:S(2)}, u32[]{:S(2)}) collective-permute-start(bf16[256,256]{1,0:T(8,128)(2,1)S(1)} %slice.116), channel_id=1, source_target_pairs={{4,0},{8,4},{12,8},{16,12},{20,16},{24,20},{28,24},{5,1},{9,5},{13... | collective-permute-start | bytes 393224 | tf_op jit(solution)/shard_map/ppermute | solution.py:763
  289.5 15.6 %collective-permute-start.42 = (bf16[256,1024]{1,0:T(8,128)(2,1)S(1)}, bf16[256,1024]{1,0:T(8,128)(2,1)S(1)}, u32[]{:S(2)}, u32[]{:S(2)}) collective-permute-start(bf16[256,1024]{1,0:T(8,128)(2,1)S(1)} %slice.117), channel_id=1, source_target_pairs={{4,0},{8,4},{12,8},{16,12},{20,16},{24,20},{28,24},{5,1},{9,5},{13... | collective-permute-start | bytes 1572872 | tf_op jit(solution)/shard_map/ppermute | solution.py:763
  302.1 6.2 %collective-permute-start.52 = (f32[8,160]{1,0:T(8,128)S(1)}, f32[8,160]{1,0:T(8,128)S(1)}, u32[]{:S(2)}, u32[]{:S(2)}) collective-permute-start(f32[8,160]{1,0:T(8,128)S(1)} %get-tuple-element.129), channel_id=1, source_target_pairs={{0,1},{1,0},{2,3},{3,2},{4,5},{5,4},{6,7},{7,6},{8,9},{9,8},{10,11... | collective-permute-start | bytes 15368 | tf_op jit(solution)/shard_map/ppermute | solution.py:56
  310.0 4.6 %collective-permute-start.51 = (f32[8,320]{1,0:T(8,128)S(1)}, f32[8,320]{1,0:T(8,128)S(1)}, u32[]{:S(2)}, u32[]{:S(2)}) collective-permute-start(f32[8,320]{1,0:T(8,128)S(1)} %add.204), channel_id=1, source_target_pairs={{0,16},{4,20},{8,24},{12,28},{16,0},{20,4},{24,8},{28,12},{1,17},{... | collective-permute-start | bytes 30728 | tf_op jit(solution)/shard_map/ppermute | solution.py:56
  317.7 12.1 %all-to-all-start = ((f32[32,8,128]{2,1,0:T(8,128)}), f32[32,8,128]{2,1,0:T(8,128)S(1)}, u32[]{:S(2)}, u32[]{:S(2)}) async-start(f32[32,8,128]{2,1,0:T(8,128)} %bitcast.51), calls=%async_computation | async-start | bytes 262144 | tf_op jit(solution)/shard_map/all_to_all | solution.py:823
  (63 other events, 490.9 us)

commit v4 on v3

--- a/solution.py
+++ b/solution.py
@@ -64,17 +64,17 @@
     return lax.dynamic_update_slice_in_dim(table, piece, row, 0)
 
 
-def pair_up(piece):
-    other = hop(piece, "seq", 1)
+def in_order(piece, other):
     low = lax.axis_index("seq") % 2 == 0
     return jnp.concatenate([jnp.where(low, piece, other), jnp.where(low, other, piece)], axis=0)
 
 
-def gather_pairs(shard, first, second):
+def gather_pairs(shard, other, first, second):
     peers = lax.axis_size("seq")
-    pairs = {}
-    for f in range(0, peers // 2, 2):
-        pairs[f] = pair_up(after(hop(after(shard, first), "seq", 2 * f), first) if f else shard)
+    pairs = {0: in_order(shard, other)}
+    for f in range(2, peers // 2, 2):
+        piece = after(hop(after(shard, first), "seq", 2 * f), first)
+        pairs[f] = in_order(piece, hop(piece, "seq", 1))
     for f in range(0, peers // 2, 2):
         pairs[f + 1] = hop(after(pairs[f], second(f, pairs)), "seq", 2)
     return pairs
@@ -534,13 +534,17 @@
             across[f][g] = hop(after(pairs[g], *earlier), "tensor", f)
         return [across[f][g] for f in across]
 
+    other_m = hop(after(shard_m, far[0]), "seq", 1)
+    own_across = {f: hop(shard_m, "tensor", f) for f in across}
+
     def second(f, pairs):
         if not f:
-            send_across(0, pairs)
+            for g in across:
+                across[g][0] = in_order(own_across[g], hop(other_m, "tensor", g))
             return near[-1], far[1]
         return send_across(f, pairs, rims[: n_tensor // 2])
 
-    pairs_m = gather_pairs(shard_m, (near[1], far[0]), second)
+    pairs_m = gather_pairs(shard_m, other_m, (near[1], far[0], list(own_across.values())), second)
     for g in pairs_m:
         if g % 2:
             send_across(g, pairs_m, list(across[flips[2]].values())[-1])

time: 339 us -> 336 us (level)
  starting transfers between devices: 84.7 us -> 77.8 us
  waiting for transfers between devices: 118 us -> 123 us
    ppermute x51 -> x52, starting transfers between devices: 74.8 us -> 68 us  [hop(): return lax.ppermute(value, axis, [(i, i ^ flip) for i in range(peers)])]
    ppermute x51 -> x52, waiting for transfers between devices: 107 us -> 112 us  [hop(): return lax.ppermute(value, axis, [(i, i ^ flip) for i in range(peers)])]
  transfers between devices with their start and end apart: 55 -> 56, of which waited for: 25 -> 24; matrix products, arithmetic and copies ran while one was open for 8% -> 9% of each run, Pallas kernels for 19% -> 20%
where the time goes in v4:
time: 336 us; the launch traced here: 332 us
  waiting for transfers between devices  123 us (37%)
  Pallas kernels  80 us (24%)
  starting transfers between devices  77.8 us (23%)
  other arithmetic  27.6 us (8%)
  local copies, waits for them, and re-layouts  22.1 us (7%)
    ppermute x52, waiting for transfers between devices, hop(): return lax.ppermute(value, axis, [(i, i ^ flip) for i in range(peers)])  112 us
    pallas_call x8, Pallas kernels, vmem_call(): pl.pallas_call(body, out_shape=outs, in_specs=[scalars if a.ndim == 1 els...  80 us
    ppermute x52, starting transfers between devices, hop(): return lax.ppermute(value, axis, [(i, i ^ flip) for i in range(peers)])  68 us
    unnamed x112, local copies, waits for them, and re-layouts  15.1 us
  transfers between devices with their start and end apart: 56, of which 24 were waited for; matrix products, arithmetic and copies ran while one was open for 9% of the time, Pallas kernels for 20%

profile of v4, /device:TPU:0, one launch (start us, length us, event | category | flops | bytes accessed | tf_op | source)
XLA Modules:
  0.0 332.3 jit_solution(16911501615427494850)
XLA Ops:
  2.1 3.0 collective-permute-start.6
  5.6 2.7 collective-permute-start.4
  8.3 1.5 collective-permute-start.13
  11.0 3.3 collective-permute-start
  14.3 1.7 collective-permute-start.12
  16.1 6.7 %collective-permute-done.4 = bf16[160,1024]{1,0:T(8,128)(2,1)S(1)} collective-permute-done((bf16[160,1024]{1,0:T(8,128)(2,1)S(1)}, bf16[160,1024]{1,0:T(8,128)(2,1)S(1)}, u32[]{:S(2)}, u32[]{:S(2)}) %collective-permute-start.4) | collective-permute-done | bytes 327712 | tf_op jit(solution)/shard_map/ppermute | solution.py:56
  23.0 4.1 %collective-permute-start.5 = (bf16[2,160,1024]{2,1,0:T(8,128)(2,1)S(1)}, bf16[2,160,1024]{2,1,0:T(8,128)(2,1)}, u32[]{:S(2)}, u32[]{:S(2)}) collective-permute-start(bf16[2,160,1024]{2,1,0:T(8,128)(2,1)S(1)} %pad_maximum_fusion.1), channel_id=1, source_target_pairs={{0,8},{4,12},{8,0},{12,4},{16,24},{20,28},{24,16},{28,20},{1,9},{5... | collective-permute-start | bytes 1966088 | tf_op jit(solution)/shard_map/ppermute | solution.py:56
  27.7 11.8 %collective-permute-done.14 = bf16[160,1024]{1,0:T(8,128)(2,1)} collective-permute-done((bf16[160,1024]{1,0:T(8,128)(2,1)S(1)}, bf16[160,1024]{1,0:T(8,128)(2,1)}, u32[]{:S(2)}, u32[]{:S(2)}) %collective-permute-start.14) | collective-permute-done | bytes 327712 | tf_op jit(solution)/shard_map/ppermute | solution.py:56
  40.0 1.5 collective-permute-start.1
  43.3 3.5 %collective-permute-done.5.refs_8_ = bf16[2,160,1024]{2,1,0:T(8,128)(2,1)} collective-permute-done((bf16[2,160,1024]{2,1,0:T(8,128)(2,1)S(1)}, bf16[2,160,1024]{2,1,0:T(8,128)(2,1)}, u32[]{:S(2)}, u32[]{:S(2)}) %collective-permute-start.5) | collective-permute-done | bytes 655392 | tf_op jit(solution)/shard_map/ppermute | solution.py:56
  46.8 8.7 %collective-permute-start.16 = (bf16[320,1024]{1,0:T(8,128)(2,1)}, bf16[320,1024]{1,0:T(8,128)(2,1)}, u32[]{:S(2)}, u32[]{:S(2)}) collective-permute-start(bf16[320,1024]{1,0:T(8,128)(2,1)} %get-tuple-element.85), channel_id=1, source_target_pairs={{0,8},{4,12},{8,0},{12,4},{16,24},{20,28},{24,16},{28,20},{1,9},{5... | collective-permute-start | bytes 1966088 | tf_op jit(solution)/shard_map/ppermute | solution.py:56
  61.3 8.9 %collective-permute-done.16 = bf16[320,1024]{1,0:T(8,128)(2,1)} collective-permute-done((bf16[320,1024]{1,0:T(8,128)(2,1)}, bf16[320,1024]{1,0:T(8,128)(2,1)}, u32[]{:S(2)}, u32[]{:S(2)}) %collective-permute-start.16) | collective-permute-done | bytes 655392 | tf_op jit(solution)/shard_map/ppermute | solution.py:56
  70.2 4.5 %collective-permute-done.17 = bf16[320,1024]{1,0:T(8,128)(2,1)S(1)} collective-permute-done((bf16[320,1024]{1,0:T(8,128)(2,1)}, bf16[320,1024]{1,0:T(8,128)(2,1)S(1)}, u32[]{:S(2)}, u32[]{:S(2)}) %collective-permute-start.17) | collective-permute-done | bytes 655392 | tf_op jit(solution)/shard_map/ppermute | solution.py:56
  75.2 11.7 %collective-permute-start.18 = (bf16[320,1024]{1,0:T(8,128)(2,1)}, bf16[320,1024]{1,0:T(8,128)(2,1)S(1)}, u32[]{:S(2)}, u32[]{:S(2)}) collective-permute-start(bf16[320,1024]{1,0:T(8,128)(2,1)} %get-tuple-element.87), channel_id=1, source_target_pairs={{0,8},{4,12},{8,0},{12,4},{16,24},{20,28},{24,16},{28,20},{1,9},{5... | collective-permute-start | bytes 1966088 | tf_op jit(solution)/shard_map/ppermute | solution.py:56
  90.9 8.9 %collective-permute-done.18 = bf16[320,1024]{1,0:T(8,128)(2,1)S(1)} collective-permute-done((bf16[320,1024]{1,0:T(8,128)(2,1)}, bf16[320,1024]{1,0:T(8,128)(2,1)S(1)}, u32[]{:S(2)}, u32[]{:S(2)}) %collective-permute-start.18) | collective-permute-done | bytes 655392 | tf_op jit(solution)/shard_map/ppermute | solution.py:56
  100.3 1.6 pad_maximum_fusion.refs_4_
  102.0 2.5 collective-permute-done.8.refs_11_
  104.5 19.8 %shard_map.251 = (bf16[2048,1280]{1,0:T(8,128)(2,1)}, bf16[1024,320]{1,0:T(8,128)(2,1)}, bf16[2048,320]{1,0:T(8,128)(2,1)}, bf16[2048,320]{1,0:T(8,128)(2,1)}, b...) custom-call(s32[13]{0:T(128)} %stack.92.refs_0_, ...), custom_call_target="tpu_custom_call" | custom-call | flops 80530636800 | bytes 19687732 | tf_op jit(solution)/shard_map/pallas_call | solution.py:40
  128.6 3.8 %collective-permute-done.10.refs_2_.refs_1_ = bf16[256,320]{1,0:T(8,128)(2,1)S(1)} collective-permute-done((bf16[256,320]{1,0:T(8,128)(2,1)}, bf16[256,320]{1,0:T(8,128)(2,1)S(1)}, u32[]{:S(2)}, u32[]{:S(2)}) %collective-permute-start.10) | collective-permute-done | bytes 163872 | tf_op jit(solution)/shard_map/ppermute | solution.py:56
  132.5 1.5 collective-permute-done.11.refs_3_
  135.2 1.6 collective-permute-done.25.refs_12_
  137.8 12.6 %shard_map.252 = (f32[256,1280]{1,0:T(8,128)}, f32[256,1280]{1,0:T(8,128)}, f32[1,1280]{1,0:T(1,128)S(1)}, bf16[2,256,1280]{2,1,0:T(8,128)(2,1)}, bf16[2,256,640...) custom-call(s32[4]{0:T(128)S(1)} %pad_add_fusion.at_ref, ...), custom_call_target="tpu_custom_call" | custom-call | flops 40265318400 | bytes 18360336 | tf_op jit(solution)/shard_map/pallas_call | solution.py:40
  155.5 1.4 collective-permute-done.33.refs_8_
  163.7 6.1 %shard_map.253 = (bf16[1280,512]{1,0:T(8,128)(2,1)S(1)}, bf16[1280,512]{1,0:T(8,128)(2,1)S(1)}, bf16[2,2,320,512]{3,2,1,0:T(8,128)(2,1)S(1)}, bf16[2,2,320,512]{3,2,1,0:T(8,128)(2,1)S(1)}) custom-call(s32[1]{0:T(128)} %bitcast.27.at_ref, bf16[256,320]{1,0:T(8,128)(2,1)S(1)} %copy-done.22, bf16[256,320]{1,0:T(8,128)(2,1)S(1)} %collective-permute-done.10.refs_2_.refs_1_, ...), custom_call_target="tpu_custom_call" | custom-call | flops 20132659200 | bytes 11141124 | tf_op jit(solution)/shard_map/pallas_call | solution.py:40
  172.6 29.3 %shard_map.254 = (bf16[1024,320]{1,0:T(8,128)(2,1)}, bf16[2048,640]{1,0:T(8,128)(2,1)}, f32[1,320]{1,0:T(1,128)}, bf16[4,160,1024]{2,1,0:T(8,128)(2,1)}, bf16[4,160,1024]{2,1,0:T(8,128)(2,1)}) custom-call(s32[5]{0:T(128)} %stack.100.at_ref, bf16[256,320]{1,0:T(8,128)(2,1)} %copy-done.23, bf16[256,320]{1,0:T(8,128)(2,1)} %collective-permute-done.27.refs_1_, ...), custom_call_target="tpu_custom_call" | custom-call | flops 134217728000 | bytes 15096340 | tf_op jit(solution)/shard_map/pallas_call | solution.py:40
  202.9 1.7 convert_add_fusion.2
  206.1 1.9 convert_add_fusion.1
  209.8 8.5 %shard_map.255 = (bf16[2,256,2560]{2,1,0:T(8,128)(2,1)S(1)}, bf16[2,256,2560]{2,1,0:T(8,128)(2,1)}) custom-call(s32[4]{0:T(128)S(1)} %pad_add_fusion.1.at_ref, bf16[1024,320]{1,0:T(8,128)(2,1)S(1)} %copy-done.20, bf16[2048,640]{1,0:T(8,128)(2,1)S(1)} %copy-done.17, bf16[1280,1024]{1,0:T(8,128)(2,1)} %get-tuple-element.114.w_ref), custom_call_target="tpu_custom_call" | custom-call | flops 33554432000 | bytes 11141136 | tf_op jit(solution)/shard_map/pallas_call | solution.py:40
  218.2 14.8 %collective-permute-done.34 = bf16[4,160,1024]{2,1,0:T(8,128)(2,1)} collective-permute-done((bf16[4,160,1024]{2,1,0:T(8,128)(2,1)}, bf16[4,160,1024]{2,1,0:T(8,128)(2,1)}, u32[]{:S(2)}, u32[]{:S(2)}) %collective-permute-start.34) | collective-permute-done | bytes 1310752 | tf_op jit(solution)/shard_map/ppermute | solution.py:56
  235.0 2.4 convert_add_fusion
  240.0 3.4 %collective-permute-start.47 = (bf16[2,160,512]{2,1,0:T(8,128)(2,1)S(1)}, bf16[2,160,512]{2,1,0:T(8,128)(2,1)S(1)}, u32[]{:S(2)}, u32[]{:S(2)}) collective-permute-start(bf16[2,160,512]{2,1,0:T(8,128)(2,1)S(1)} %fusion.18), channel_id=1, source_target_pairs={{0,16},{4,20},{8,24},{12,28},{16,0},{20,4},{24,8},{28,12},{1,17},{... | collective-permute-start | bytes 983048 | tf_op jit(solution)/shard_map/ppermute | solution.py:56
  243.4 18.3 %collective-permute-done.44 = bf16[2,160,1024]{2,1,0:T(8,128)(2,1)S(1)} collective-permute-done((bf16[2,160,1024]{2,1,0:T(8,128)(2,1)S(1)}, bf16[2,160,1024]{2,1,0:T(8,128)(2,1)S(1)}, u32[]{:S(2)}, u32[]{:S(2)}) %collective-permute-start.44) | collective-permute-done | bytes 655392 | tf_op jit(solution)/shard_map/ppermute | solution.py:56
  262.0 1.8 collective-permute-start.45
  264.0 2.3 fusion.9
  269.7 12.9 %collective-permute-done.40 = bf16[256,1280]{1,0:T(8,128)(2,1)S(1)} collective-permute-done((bf16[256,1280]{1,0:T(8,128)(2,1)S(1)}, bf16[256,1280]{1,0:T(8,128)(2,1)S(1)}, u32[]{:S(2)}, u32[]{:S(2)}) %collective-permute-start.40) | collective-permute-done | bytes 655392 | tf_op jit(solution)/shard_map/ppermute | solution.py:56
  286.5 1.4 collective-permute-start.43
  287.9 3.9 %collective-permute-done.42 = bf16[256,256]{1,0:T(8,128)(2,1)S(1)} collective-permute-done((bf16[256,256]{1,0:T(8,128)(2,1)S(1)}, bf16[256,256]{1,0:T(8,128)(2,1)S(1)}, u32[]{:S(2)}, u32[]{:S(2)}) %collective-permute-start.42) | collective-permute-done | bytes 131104 | tf_op jit(solution)/shard_map/ppermute | solution.py:767
  291.8 5.9 %collective-permute-done.41 = bf16[256,1280]{1,0:T(8,128)(2,1)S(1)} collective-permute-done((bf16[256,1280]{1,0:T(8,128)(2,1)S(1)}, bf16[256,1280]{1,0:T(8,128)(2,1)S(1)}, u32[]{:S(2)}, u32[]{:S(2)}) %collective-permute-start.41) | collective-permute-done | bytes 655392 | tf_op jit(solution)/shard_map/ppermute | solution.py:56
  297.8 1.3 shard_map.256
  299.7 2.4 collective-permute-done.43
  303.0 2.3 collective-permute-start.51
  307.0 1.7 collective-permute-start.52
  309.0 2.5 collective-permute-done.52
  314.7 3.9 %all-to-all-start = ((f32[32,8,128]{2,1,0:T(8,128)}), f32[32,8,128]{2,1,0:T(8,128)S(1)}, u32[]{:S(2)}, u32[]{:S(2)}) async-start(f32[32,8,128]{2,1,0:T(8,128)} %bitcast.51), calls=%async_computation | async-start | bytes 262144 | tf_op jit(solution)/shard_map/all_to_all | solution.py:827
  318.6 3.7 %fusion.6 = f32[256,1280]{1,0:T(8,128)} fusion(f32[256,1280]{1,0:T(8,128)} %get-tuple-element.96, bf16[256,1280]{1,0:T(8,128)(2,1)S(1)} %get-tuple-element.149.refs_14_, f32[256]{0:T(256)S(1)} %broadcast_multiply_fusion, f32[1280]{0:T(1024)S(1)} %copy-done.41, f32[256]{0:T(256)S(1)} %copy-done.43, bf16[256,1024]{1,0:T(8,128)(2,1)} %copy-done.31, ...), kind=kLoop, calls=%fused_computation.14 | loop fusion | flops 4587520 | bytes 5905408 | tf_op jit(solution)/shard_map/add | solution.py:775
  322.3 4.5 %all-to-all-done = f32[32,8,128]{2,1,0:T(8,128)S(1)} async-done(((f32[32,8,128]{2,1,0:T(8,128)}), f32[32,8,128]{2,1,0:T(8,128)S(1)}, u32[]{:S(2)}, u32[]{:S(2)}) %all-to-all-start) | async-done | bytes 131104 | tf_op jit(solution)/shard_map/all_to_all | solution.py:827
  328.2 1.4 copy-done.16
  330.8 1.3 fusion.23
  (276 shorter events, 63.5 us)
Async XLA Ops:
  2.1 12.2 %collective-permute-start.6 = (bf16[1,160,1024]{2,1,0:T(8,128)(2,1)S(1)}, bf16[1,160,1024]{2,1,0:T(8,128)(2,1)}, u32[]{:S(2)}, u32[]{:S(2)}) collective-permute-start(bf16[1,160,1024]{2,1,0:T(8,128)(2,1)S(1)} %pad_maximum_fusion.5.refs_6_), channel_id=1, source_target_pairs={{0,4},{4,0},{8,12},{12,8},{16,20},{20,16},{24,28},{28,24},{1,5},{5... | collective-permute-start | bytes 983048 | tf_op jit(solution)/shard_map/ppermute | solution.py:56
  5.6 17.2 %collective-permute-start.4 = (bf16[160,1024]{1,0:T(8,128)(2,1)S(1)}, bf16[160,1024]{1,0:T(8,128)(2,1)S(1)}, u32[]{:S(2)}, u32[]{:S(2)}) collective-permute-start(bf16[160,1024]{1,0:T(8,128)(2,1)S(1)} %get-tuple-element.173), channel_id=1, source_target_pairs={{0,16},{4,20},{8,24},{12,28},{16,0},{20,4},{24,8},{28,12},{1,17},{... | collective-permute-start | bytes 983048 | tf_op jit(solution)/shard_map/ppermute | solution.py:56
  8.3 14.5 %collective-permute-start.13 = (bf16[160,1024]{1,0:T(8,128)(2,1)S(1)}, bf16[160,1024]{1,0:T(8,128)(2,1)S(1)}, u32[]{:S(2)}, u32[]{:S(2)}) collective-permute-start(bf16[160,1024]{1,0:T(8,128)(2,1)S(1)} %get-tuple-element.82), channel_id=1, source_target_pairs={{0,2},{1,3},{2,0},{3,1},{4,6},{5,7},{6,4},{7,5},{8,10},{9,11},{10,... | collective-permute-start | bytes 983048 | tf_op jit(solution)/shard_map/ppermute | solution.py:56
  11.0 29.0 %collective-permute-start = (bf16[256,1280]{1,0:T(8,128)(2,1)S(1)}, bf16[256,1280]{1,0:T(8,128)(2,1)}, u32[]{:S(2)}, u32[]{:S(2)}) collective-permute-start(bf16[256,1280]{1,0:T(8,128)(2,1)S(1)} %get-tuple-element.149.refs_14_), channel_id=1, source_target_pairs={{0,4},{4,8},{8,12},{12,16},{16,20},{20,24},{24,28},{1,5},{5,9},{9,... | collective-permute-start | bytes 1966088 | tf_op jit(solution)/shard_map/ppermute | solution.py:526
  14.3 27.2 %collective-permute-start.12 = (bf16[160,1024]{1,0:T(8,128)(2,1)S(1)}, bf16[160,1024]{1,0:T(8,128)(2,1)S(1)}, u32[]{:S(2)}, u32[]{:S(2)}) collective-permute-start(bf16[160,1024]{1,0:T(8,128)(2,1)S(1)} %get-tuple-element.82), channel_id=1, source_target_pairs={{0,4},{4,0},{8,12},{12,8},{16,20},{20,16},{24,28},{28,24},{1,5},{5... | collective-permute-start | bytes 983048 | tf_op jit(solution)/shard_map/ppermute | solution.py:56
  22.8 16.8 %collective-permute-start.14 = (bf16[160,1024]{1,0:T(8,128)(2,1)S(1)}, bf16[160,1024]{1,0:T(8,128)(2,1)}, u32[]{:S(2)}, u32[]{:S(2)}) collective-permute-start(bf16[160,1024]{1,0:T(8,128)(2,1)S(1)} %get-tuple-element.82), channel_id=1, source_target_pairs={{0,16},{4,20},{8,24},{12,28},{16,0},{20,4},{24,8},{28,12},{1,17},{... | collective-permute-start | bytes 983048 | tf_op jit(solution)/shard_map/ppermute | solution.py:56
  23.0 23.8 %collective-permute-start.5 = (bf16[2,160,1024]{2,1,0:T(8,128)(2,1)S(1)}, bf16[2,160,1024]{2,1,0:T(8,128)(2,1)}, u32[]{:S(2)}, u32[]{:S(2)}) collective-permute-start(bf16[2,160,1024]{2,1,0:T(8,128)(2,1)S(1)} %pad_maximum_fusion.1), channel_id=1, source_target_pairs={{0,8},{4,12},{8,0},{12,4},{16,24},{20,28},{24,16},{28,20},{1,9},{5... | collective-permute-start | bytes 1966088 | tf_op jit(solution)/shard_map/ppermute | solution.py:56
  27.1 16.2 %collective-permute-start.7 = (bf16[1,160,1024]{2,1,0:T(8,128)(2,1)S(1)}, bf16[1,160,1024]{2,1,0:T(8,128)(2,1)S(1)}, u32[]{:S(2)}, u32[]{:S(2)}) collective-permute-start(bf16[1,160,1024]{2,1,0:T(8,128)(2,1)S(1)} %bitcast.101), channel_id=1, source_target_pairs={{0,4},{4,0},{8,12},{12,8},{16,20},{20,16},{24,28},{28,24},{1,5},{5... | collective-permute-start | bytes 983048 | tf_op jit(solution)/shard_map/ppermute | solution.py:56
  39.5 16.0 %collective-permute-start.15 = (bf16[160,1024]{1,0:T(8,128)(2,1)}, bf16[160,1024]{1,0:T(8,128)(2,1)S(1)}, u32[]{:S(2)}, u32[]{:S(2)}) collective-permute-start(bf16[160,1024]{1,0:T(8,128)(2,1)} %collective-permute-done.14), channel_id=1, source_target_pairs={{0,4},{4,0},{8,12},{12,8},{16,20},{20,16},{24,28},{28,24},{1,5},{5... | collective-permute-start | bytes 983048 | tf_op jit(solution)/shard_map/ppermute | solution.py:56
  40.0 17.8 %collective-permute-start.1 = (bf16[256,1280]{1,0:T(8,128)(2,1)}, bf16[256,1280]{1,0:T(8,128)(2,1)S(1)}, u32[]{:S(2)}, u32[]{:S(2)}) collective-permute-start(bf16[256,1280]{1,0:T(8,128)(2,1)} %collective-permute-done.refs_2_), channel_id=1, source_target_pairs={{0,2},{1,3},{2,0},{3,1},{4,6},{5,7},{6,4},{7,5},{8,10},{9,11},{10,... | collective-permute-start | bytes 1966088 | tf_op jit(solution)/shard_map/ppermute | solution.py:56
  46.8 23.3 %collective-permute-start.16 = (bf16[320,1024]{1,0:T(8,128)(2,1)}, bf16[320,1024]{1,0:T(8,128)(2,1)}, u32[]{:S(2)}, u32[]{:S(2)}) collective-permute-start(bf16[320,1024]{1,0:T(8,128)(2,1)} %get-tuple-element.85), channel_id=1, source_target_pairs={{0,8},{4,12},{8,0},{12,4},{16,24},{20,28},{24,16},{28,20},{1,9},{5... | collective-permute-start | bytes 1966088 | tf_op jit(solution)/shard_map/ppermute | solution.py:56
  58.6 16.0 %collective-permute-start.17 = (bf16[320,1024]{1,0:T(8,128)(2,1)}, bf16[320,1024]{1,0:T(8,128)(2,1)S(1)}, u32[]{:S(2)}, u32[]{:S(2)}) collective-permute-start(bf16[320,1024]{1,0:T(8,128)(2,1)} %get-tuple-element.87), channel_id=1, source_target_pairs={{0,2},{1,3},{2,0},{3,1},{4,6},{5,7},{6,4},{7,5},{8,10},{9,11},{10,... | collective-permute-start | bytes 1966088 | tf_op jit(solution)/shard_map/ppermute | solution.py:56
  74.6 15.7 %collective-permute-start.21 = (bf16[320,1024]{1,0:T(8,128)(2,1)}, bf16[320,1024]{1,0:T(8,128)(2,1)S(1)}, u32[]{:S(2)}, u32[]{:S(2)}) collective-permute-start(bf16[320,1024]{1,0:T(8,128)(2,1)} %collective-permute-done.16), channel_id=1, source_target_pairs={{0,2},{1,3},{2,0},{3,1},{4,6},{5,7},{6,4},{7,5},{8,10},{9,11},{10,... | collective-permute-start | bytes 1966088 | tf_op jit(solution)/shard_map/ppermute | solution.py:56
  75.2 24.6 %collective-permute-start.18 = (bf16[320,1024]{1,0:T(8,128)(2,1)}, bf16[320,1024]{1,0:T(8,128)(2,1)S(1)}, u32[]{:S(2)}, u32[]{:S(2)}) collective-permute-start(bf16[320,1024]{1,0:T(8,128)(2,1)} %get-tuple-element.87), channel_id=1, source_target_pairs={{0,8},{4,12},{8,0},{12,4},{16,24},{20,28},{24,16},{28,20},{1,9},{5... | collective-permute-start | bytes 1966088 | tf_op jit(solution)/shard_map/ppermute | solution.py:56
  87.0 14.9 %collective-permute-start.2 = (bf16[256,1280]{1,0:T(8,128)(2,1)}, bf16[256,1280]{1,0:T(8,128)(2,1)}, u32[]{:S(2)}, u32[]{:S(2)}) collective-permute-start(bf16[256,1280]{1,0:T(8,128)(2,1)} %collective-permute-done.refs_2_), channel_id=1, source_target_pairs={{0,1},{1,0},{2,3},{3,2},{4,5},{5,4},{6,7},{7,6},{8,9},{9,8},{10,11... | collective-permute-start | bytes 1966088 | tf_op jit(solution)/shard_map/ppermute | solution.py:56
  87.1 17.5 %collective-permute-start.8 = (bf16[2,160,1024]{2,1,0:T(8,128)(2,1)}, bf16[2,160,1024]{2,1,0:T(8,128)(2,1)}, u32[]{:S(2)}, u32[]{:S(2)}) collective-permute-start(bf16[2,160,1024]{2,1,0:T(8,128)(2,1)} %collective-permute-done.5.refs_8_), channel_id=1, source_target_pairs={{0,4},{4,0},{8,12},{12,8},{16,20},{20,16},{24,28},{28,24},{1,5},{5... | collective-permute-start | bytes 1966088 | tf_op jit(solution)/shard_map/ppermute | solution.py:56
  87.7 16.8 %collective-permute-start.3 = (bf16[256,1280]{1,0:T(8,128)(2,1)}, bf16[256,1280]{1,0:T(8,128)(2,1)}, u32[]{:S(2)}, u32[]{:S(2)}) collective-permute-start(bf16[256,1280]{1,0:T(8,128)(2,1)} %copy-done.52), channel_id=1, source_target_pairs={{0,1},{1,0},{2,3},{3,2},{4,5},{5,4},{6,7},{7,6},{8,9},{9,8},{10,11... | collective-permute-start | bytes 1966088 | tf_op jit(solution)/shard_map/ppermute | solution.py:56
  90.4 35.1 %collective-permute-start.20 = (bf16[160,1024]{1,0:T(8,128)(2,1)}, bf16[160,1024]{1,0:T(8,128)(2,1)S(1)}, u32[]{:S(2)}, u32[]{:S(2)}) collective-permute-start(bf16[160,1024]{1,0:T(8,128)(2,1)} %copy-done.39), channel_id=1, source_target_pairs={{0,2},{1,3},{2,0},{3,1},{4,6},{5,7},{6,4},{7,5},{8,10},{9,11},{10,... | collective-permute-start | bytes 983048 | tf_op jit(solution)/shard_map/ppermute | solution.py:56
  99.7 28.7 %collective-permute-start.22 = (bf16[320,1024]{1,0:T(8,128)(2,1)S(1)}, bf16[320,1024]{1,0:T(8,128)(2,1)S(1)}, u32[]{:S(2)}, u32[]{:S(2)}) collective-permute-start(bf16[320,1024]{1,0:T(8,128)(2,1)S(1)} %collective-permute-done.18), channel_id=1, source_target_pairs={{0,2},{1,3},{2,0},{3,1},{4,6},{5,7},{6,4},{7,5},{8,10},{9,11},{10,... | collective-permute-start | bytes 1966088 | tf_op jit(solution)/shard_map/ppermute | solution.py:56
  101.9 35.9 %collective-permute-start.19 = (bf16[4,320,1024]{2,1,0:T(8,128)(2,1)S(1)}, bf16[4,320,1024]{2,1,0:T(8,128)(2,1)}, u32[]{:S(2)}, u32[]{:S(2)}) collective-permute-start(bf16[4,320,1024]{2,1,0:T(8,128)(2,1)S(1)} %pad_maximum_fusion.refs_4_), channel_id=1, source_target_pairs={{0,1},{1,0},{2,3},{3,2},{4,5},{5,4},{6,7},{7,6},{8,9},{9,8},{10,11... | collective-permute-start | bytes 7864328 | tf_op jit(solution)/shard_map/ppermute | solution.py:56
  124.4 8.1 %collective-permute-start.10 = (bf16[256,320]{1,0:T(8,128)(2,1)}, bf16[256,320]{1,0:T(8,128)(2,1)S(1)}, u32[]{:S(2)}, u32[]{:S(2)}) collective-permute-start(bf16[256,320]{1,0:T(8,128)(2,1)} %get-tuple-element.80), channel_id=1, source_target_pairs={{0,2},{1,3},{2,0},{3,1},{4,6},{5,7},{6,4},{7,5},{8,10},{9,11},{10,... | collective-permute-start | bytes 491528 | tf_op jit(solution)/shard_map/ppermute | solution.py:56
  125.0 9.0 %collective-permute-start.11 = (bf16[256,320]{1,0:T(8,128)(2,1)}, bf16[256,320]{1,0:T(8,128)(2,1)S(1)}, u32[]{:S(2)}, u32[]{:S(2)}) collective-permute-start(bf16[256,320]{1,0:T(8,128)(2,1)} %get-tuple-element.81), channel_id=1, source_target_pairs={{0,3},{1,2},{2,1},{3,0},{4,7},{5,6},{6,5},{7,4},{8,11},{9,10},{10,... | collective-permute-start | bytes 491528 | tf_op jit(solution)/shard_map/ppermute | solution.py:56
  126.2 9.0 %collective-permute-start.9 = (bf16[256,320]{1,0:T(8,128)(2,1)}, bf16[256,320]{1,0:T(8,128)(2,1)S(1)}, u32[]{:S(2)}, u32[]{:S(2)}) collective-permute-start(bf16[256,320]{1,0:T(8,128)(2,1)} %get-tuple-element.79), channel_id=1, source_target_pairs={{0,1},{1,0},{2,3},{3,2},{4,5},{5,4},{6,7},{7,6},{8,9},{9,8},{10,11... | collective-permute-start | bytes 491528 | tf_op jit(solution)/shard_map/ppermute | solution.py:56
  128.5 6.7 %collective-permute-start.24 = (bf16[1,320,1024]{2,1,0:T(8,128)(2,1)S(1)}, bf16[1,320,1024]{2,1,0:T(8,128)(2,1)S(1)}, u32[]{:S(2)}, u32[]{:S(2)}) collective-permute-start(bf16[1,320,1024]{2,1,0:T(8,128)(2,1)S(1)} %bitcast.84), channel_id=1, source_target_pairs={{0,1},{1,0},{2,3},{3,2},{4,5},{5,4},{6,7},{7,6},{8,9},{9,8},{10,11... | collective-permute-start | bytes 1966088 | tf_op jit(solution)/shard_map/ppermute | solution.py:56
  152.0 7.2 %collective-permute-start.31 = (bf16[2,256,1280]{2,1,0:T(8,128)(2,1)}, bf16[2,256,1280]{2,1,0:T(8,128)(2,1)}, u32[]{:S(2)}, u32[]{:S(2)}) collective-permute-start(bf16[2,256,1280]{2,1,0:T(8,128)(2,1)} %get-tuple-element.104.refs_3_), channel_id=1, source_target_pairs={{0,1},{1,0},{2,3},{3,2},{4,5},{5,4},{6,7},{7,6},{8,9},{9,8},{10,11... | collective-permute-start | bytes 3932168 | tf_op jit(solution)/shard_map/ppermute | solution.py:56
  152.5 5.9 %collective-permute-start.32 = (bf16[2,256,640]{2,1,0:T(8,128)(2,1)}, bf16[2,256,640]{2,1,0:T(8,128)(2,1)S(1)}, u32[]{:S(2)}, u32[]{:S(2)}) collective-permute-start(bf16[2,256,640]{2,1,0:T(8,128)(2,1)} %get-tuple-element.106), channel_id=1, source_target_pairs={{0,1},{1,0},{2,3},{3,2},{4,5},{5,4},{6,7},{7,6},{8,9},{9,8},{10,11... | collective-permute-start | bytes 1966088 | tf_op jit(solution)/shard_map/ppermute | solution.py:56
  155.1 16.8 %collective-permute-start.27 = (bf16[256,320]{1,0:T(8,128)(2,1)}, bf16[256,320]{1,0:T(8,128)(2,1)}, u32[]{:S(2)}, u32[]{:S(2)}) collective-permute-start(bf16[256,320]{1,0:T(8,128)(2,1)} %get-tuple-element.98), channel_id=1, source_target_pairs={{0,1},{1,0},{2,3},{3,2},{4,5},{5,4},{6,7},{7,6},{8,9},{9,8},{10,11... | collective-permute-start | bytes 491528 | tf_op jit(solution)/shard_map/ppermute | solution.py:56
  156.9 15.0 %collective-permute-start.28 = (bf16[256,320]{1,0:T(8,128)(2,1)}, bf16[256,320]{1,0:T(8,128)(2,1)}, u32[]{:S(2)}, u32[]{:S(2)}) collective-permute-start(bf16[256,320]{1,0:T(8,128)(2,1)} %get-tuple-element.99), channel_id=1, source_target_pairs={{0,2},{1,3},{2,0},{3,1},{4,6},{5,7},{6,4},{7,5},{8,10},{9,11},{10,... | collective-permute-start | bytes 491528 | tf_op jit(solution)/shard_map/ppermute | solution.py:56
  157.6 14.3 %collective-permute-start.29 = (bf16[256,320]{1,0:T(8,128)(2,1)}, bf16[256,320]{1,0:T(8,128)(2,1)S(1)}, u32[]{:S(2)}, u32[]{:S(2)}) collective-permute-start(bf16[256,320]{1,0:T(8,128)(2,1)} %get-tuple-element.100), channel_id=1, source_target_pairs={{0,3},{1,2},{2,1},{3,0},{4,7},{5,6},{6,5},{7,4},{8,11},{9,10},{10,... | collective-permute-start | bytes 491528 | tf_op jit(solution)/shard_map/ppermute | solution.py:56
  169.8 33.1 %collective-permute-start.35 = (bf16[1280,512]{1,0:T(8,128)(2,1)S(1)}, bf16[1280,512]{1,0:T(8,128)(2,1)}, u32[]{:S(2)}, u32[]{:S(2)}) collective-permute-start(bf16[1280,512]{1,0:T(8,128)(2,1)S(1)} %get-tuple-element.108), channel_id=1, source_target_pairs={{0,2},{1,3},{2,0},{3,1},{4,6},{5,7},{6,4},{7,5},{8,10},{9,11},{10,... | collective-permute-start | bytes 3932168 | tf_op jit(solution)/shard_map/ppermute | solution.py:56
  171.1 34.6 %collective-permute-start.37 = (bf16[2,2,320,512]{3,2,1,0:T(8,128)(2,1)S(1)}, bf16[2,2,320,512]{3,2,1,0:T(8,128)(2,1)}, u32[]{:S(2)}, u32[]{:S(2)}) collective-permute-start(bf16[2,2,320,512]{3,2,1,0:T(8,128)(2,1)S(1)} %get-tuple-element.109), channel_id=1, source_target_pairs={{0,8},{4,12},{8,0},{12,4},{16,24},{20,28},{24,16},{28,20},{1,9},{5... | collective-permute-start | bytes 3932168 | tf_op jit(solution)/shard_map/ppermute | solution.py:56
  201.9 31.0 %collective-permute-start.34 = (bf16[4,160,1024]{2,1,0:T(8,128)(2,1)}, bf16[4,160,1024]{2,1,0:T(8,128)(2,1)}, u32[]{:S(2)}, u32[]{:S(2)}) collective-permute-start(bf16[4,160,1024]{2,1,0:T(8,128)(2,1)} %get-tuple-element.117), channel_id=1, source_target_pairs={{0,4},{4,0},{8,12},{12,8},{16,20},{20,16},{24,28},{28,24},{1,5},{5... | collective-permute-start | bytes 3932168 | tf_op jit(solution)/shard_map/ppermute | solution.py:56
  204.8 28.2 %collective-permute-start.36 = (bf16[2,2,160,512]{3,2,0,1:T(8,128)(2,1)S(1)}, bf16[2,2,160,512]{3,2,0,1:T(8,128)(2,1)S(1)}, u32[]{:S(2)}, u32[]{:S(2)}) collective-permute-start(bf16[2,2,160,512]{3,2,0,1:T(8,128)(2,1)S(1)} %fusion.13), channel_id=1, source_target_pairs={{0,8},{4,12},{8,0},{12,4},{16,24},{20,28},{24,16},{28,20},{1,9},{5... | collective-permute-start | bytes 1966088 | tf_op jit(solution)/shard_map/ppermute | solution.py:56
  208.1 24.9 %collective-permute-start.38 = (bf16[2,320,512]{2,1,0:T(8,128)(2,1)S(1)}, bf16[2,320,512]{2,1,0:T(8,128)(2,1)S(1)}, u32[]{:S(2)}, u32[]{:S(2)}) collective-permute-start(bf16[2,320,512]{2,1,0:T(8,128)(2,1)S(1)} %fusion.15), channel_id=1, source_target_pairs={{0,2},{1,3},{2,0},{3,1},{4,6},{5,7},{6,4},{7,5},{8,10},{9,11},{10,... | collective-permute-start | bytes 1966088 | tf_op jit(solution)/shard_map/ppermute | solution.py:56
  234.7 29.4 %collective-permute-start.39 = (bf16[2,256,2560]{2,1,0:T(8,128)(2,1)}, bf16[2,256,2560]{2,1,0:T(8,128)(2,1)}, u32[]{:S(2)}, u32[]{:S(2)}) collective-permute-start(bf16[2,256,2560]{2,1,0:T(8,128)(2,1)} %get-tuple-element.119), channel_id=1, source_target_pairs={{0,1},{1,0},{2,3},{3,2},{4,5},{5,4},{6,7},{7,6},{8,9},{9,8},{10,11... | collective-permute-start | bytes 7864328 | tf_op jit(solution)/shard_map/ppermute | solution.py:56
  237.5 24.2 %collective-permute-start.44 = (bf16[2,160,1024]{2,1,0:T(8,128)(2,1)S(1)}, bf16[2,160,1024]{2,1,0:T(8,128)(2,1)S(1)}, u32[]{:S(2)}, u32[]{:S(2)}) collective-permute-start(bf16[2,160,1024]{2,1,0:T(8,128)(2,1)S(1)} %fusion.14), channel_id=1, source_target_pairs={{0,8},{4,12},{8,0},{12,4},{16,24},{20,28},{24,16},{28,20},{1,9},{5... | collective-permute-start | bytes 1966088 | tf_op jit(solution)/shard_map/ppermute | solution.py:56
  238.7 25.2 %collective-permute-start.46 = (bf16[2,160,512]{2,1,0:T(8,128)(2,1)S(1)}, bf16[2,160,512]{2,1,0:T(8,128)(2,1)S(1)}, u32[]{:S(2)}, u32[]{:S(2)}) collective-permute-start(bf16[2,160,512]{2,1,0:T(8,128)(2,1)S(1)} %fusion.17), channel_id=1, source_target_pairs={{0,4},{4,0},{8,12},{12,8},{16,20},{20,16},{24,28},{28,24},{1,5},{5... | collective-permute-start | bytes 983048 | tf_op jit(solution)/shard_map/ppermute | solution.py:56
  240.0 28.5 %collective-permute-start.47 = (bf16[2,160,512]{2,1,0:T(8,128)(2,1)S(1)}, bf16[2,160,512]{2,1,0:T(8,128)(2,1)S(1)}, u32[]{:S(2)}, u32[]{:S(2)}) collective-permute-start(bf16[2,160,512]{2,1,0:T(8,128)(2,1)S(1)} %fusion.18), channel_id=1, source_target_pairs={{0,16},{4,20},{8,24},{12,28},{16,0},{20,4},{24,8},{28,12},{1,17},{... | collective-permute-start | bytes 983048 | tf_op jit(solution)/shard_map/ppermute | solution.py:56
  262.0 25.9 %collective-permute-start.45 = (bf16[160,1024]{1,0:T(8,128)(2,1)S(1)}, bf16[160,1024]{1,0:T(8,128)(2,1)S(1)}, u32[]{:S(2)}, u32[]{:S(2)}) collective-permute-start(bf16[160,1024]{1,0:T(8,128)(2,1)S(1)} %fusion.16), channel_id=1, source_target_pairs={{0,16},{4,20},{8,24},{12,28},{16,0},{20,4},{24,8},{28,12},{1,17},{... | collective-permute-start | bytes 983048 | tf_op jit(solution)/shard_map/ppermute | solution.py:56
  266.4 16.1 %collective-permute-start.40 = (bf16[256,1280]{1,0:T(8,128)(2,1)S(1)}, bf16[256,1280]{1,0:T(8,128)(2,1)S(1)}, u32[]{:S(2)}, u32[]{:S(2)}) collective-permute-start(bf16[256,1280]{1,0:T(8,128)(2,1)S(1)} %get-tuple-element.153), channel_id=1, source_target_pairs={{0,2},{1,3},{2,0},{3,1},{4,6},{5,7},{6,4},{7,5},{8,10},{9,11},{10,... | collective-permute-start | bytes 1966088 | tf_op jit(solution)/shard_map/ppermute | solution.py:56
  267.8 18.6 %collective-permute-start.48 = (bf16[160,512]{1,0:T(8,128)(2,1)S(1)}, bf16[160,512]{1,0:T(8,128)(2,1)S(1)}, u32[]{:S(2)}, u32[]{:S(2)}) collective-permute-start(bf16[160,512]{1,0:T(8,128)(2,1)S(1)} %fusion.19), channel_id=1, source_target_pairs={{0,16},{4,20},{8,24},{12,28},{16,0},{20,4},{24,8},{28,12},{1,17},{... | collective-permute-start | bytes 491528 | tf_op jit(solution)/shard_map/ppermute | solution.py:56
  268.6 17.7 %collective-permute-start.49 = (bf16[160,512]{1,0:T(8,128)(2,1)S(1)}, bf16[160,512]{1,0:T(8,128)(2,1)S(1)}, u32[]{:S(2)}, u32[]{:S(2)}) collective-permute-start(bf16[160,512]{1,0:T(8,128)(2,1)S(1)} %fusion.20), channel_id=1, source_target_pairs={{0,4},{4,0},{8,12},{12,8},{16,20},{20,16},{24,28},{28,24},{1,5},{5... | collective-permute-start | bytes 491528 | tf_op jit(solution)/shard_map/ppermute | solution.py:56
  282.6 15.2 %collective-permute-start.41 = (bf16[256,1280]{1,0:T(8,128)(2,1)S(1)}, bf16[256,1280]{1,0:T(8,128)(2,1)S(1)}, u32[]{:S(2)}, u32[]{:S(2)}) collective-permute-start(bf16[256,1280]{1,0:T(8,128)(2,1)S(1)} %get-tuple-element.121), channel_id=1, source_target_pairs={{0,2},{1,3},{2,0},{3,1},{4,6},{5,7},{6,4},{7,5},{8,10},{9,11},{10,... | collective-permute-start | bytes 1966088 | tf_op jit(solution)/shard_map/ppermute | solution.py:56
  284.0 7.8 %collective-permute-start.42 = (bf16[256,256]{1,0:T(8,128)(2,1)S(1)}, bf16[256,256]{1,0:T(8,128)(2,1)S(1)}, u32[]{:S(2)}, u32[]{:S(2)}) collective-permute-start(bf16[256,256]{1,0:T(8,128)(2,1)S(1)} %slice.116), channel_id=1, source_target_pairs={{4,0},{8,4},{12,8},{16,12},{20,16},{24,20},{28,24},{5,1},{9,5},{13... | collective-permute-start | bytes 393224 | tf_op jit(solution)/shard_map/ppermute | solution.py:767
  286.5 15.6 %collective-permute-start.43 = (bf16[256,1024]{1,0:T(8,128)(2,1)S(1)}, bf16[256,1024]{1,0:T(8,128)(2,1)S(1)}, u32[]{:S(2)}, u32[]{:S(2)}) collective-permute-start(bf16[256,1024]{1,0:T(8,128)(2,1)S(1)} %slice.117), channel_id=1, source_target_pairs={{4,0},{8,4},{12,8},{16,12},{20,16},{24,20},{28,24},{5,1},{9,5},{13... | collective-permute-start | bytes 1572872 | tf_op jit(solution)/shard_map/ppermute | solution.py:767
  299.1 6.2 %collective-permute-start.53 = (f32[8,160]{1,0:T(8,128)S(1)}, f32[8,160]{1,0:T(8,128)S(1)}, u32[]{:S(2)}, u32[]{:S(2)}) collective-permute-start(f32[8,160]{1,0:T(8,128)S(1)} %get-tuple-element.131), channel_id=1, source_target_pairs={{0,1},{1,0},{2,3},{3,2},{4,5},{5,4},{6,7},{7,6},{8,9},{9,8},{10,11... | collective-permute-start | bytes 15368 | tf_op jit(solution)/shard_map/ppermute | solution.py:56
  307.0 4.6 %collective-permute-start.52 = (f32[8,320]{1,0:T(8,128)S(1)}, f32[8,320]{1,0:T(8,128)S(1)}, u32[]{:S(2)}, u32[]{:S(2)}) collective-permute-start(f32[8,320]{1,0:T(8,128)S(1)} %add.205), channel_id=1, source_target_pairs={{0,16},{4,20},{8,24},{12,28},{16,0},{20,4},{24,8},{28,12},{1,17},{... | collective-permute-start | bytes 30728 | tf_op jit(solution)/shard_map/ppermute | solution.py:56
  314.7 12.1 %all-to-all-start = ((f32[32,8,128]{2,1,0:T(8,128)}), f32[32,8,128]{2,1,0:T(8,128)S(1)}, u32[]{:S(2)}, u32[]{:S(2)}) async-start(f32[32,8,128]{2,1,0:T(8,128)} %bitcast.51), calls=%async_computation | async-start | bytes 262144 | tf_op jit(solution)/shard_map/all_to_all | solution.py:827
  (64 other events, 495.2 us)

commit v5 on v4

--- a/solution.py
+++ b/solution.py
@@ -466,7 +466,7 @@
     row_ref[...] = jnp.concatenate([*row_sums, zeros], axis=1).T[:8, :]
 
 
-def update_kernel(sizes, qkv_ref, out_ref, mlp_ref, col_ref, row_ref, cs_ref, rs_ref, cn_ref, rn_ref, up_ref, sq_ref):
+def update_kernel(sizes, qkv_ref, out_ref, mlp_ref, col_ref, row_ref, cs_ref, rs_ref, cn_ref, rn_ref, sq_ref):
     total_cols, width = sizes
     col_new = BETA_TWO * cs_ref[...] + (1.0 - BETA_TWO) * col_ref[:6, :] / width
     row_new = BETA_TWO * rs_ref[...] + (1.0 - BETA_TWO) * row_ref[:6, :] / total_cols
@@ -478,14 +478,17 @@
     for i in range(6):
         grad = qkv_ref[i] if i < 3 else out_ref[...] if i == 3 else mlp_ref[i - 4]
         update = grad * lax.rsqrt(row_cols[:, i : i + 1] * col_new[i : i + 1, :])
-        up_ref[i] = update
         sq_ref[i : i + 1, :] = jnp.sum(update * update, axis=0, keepdims=True)
 
 
-def step_kernel(up_ref, step_ref, qkv_ref, out_ref, mlp_ref, qkv_new, out_new, mlp_new):
+def step_kernel(step_ref, cn_ref, rn_ref, g_qkv, g_out, g_mlp, qkv_ref, out_ref, mlp_ref, qkv_new, out_new, mlp_new):
+    rows = rn_ref.shape[1]
+    row_cols = jnp.concatenate([rn_ref[...], jnp.ones((2, rows), f32)], axis=0).T
     for i in range(6):
+        grad = g_qkv[i] if i < 3 else g_out[...] if i == 3 else g_mlp[i - 4]
+        update = grad * lax.rsqrt(row_cols[:, i : i + 1] * cn_ref[i : i + 1, :])
+        change = step_ref[i : i + 1, :] * update
         old, new = (qkv_ref, qkv_new) if i < 3 else (mlp_ref, mlp_new)
-        change = step_ref[i : i + 1, :] * up_ref[i]
         if i == 3:
             out_new[...] = out_ref[...] - change
         else:
@@ -790,12 +793,11 @@
         keep_m,
         came_m,
     )
-    col_new, row_new, unscaled, unscaled_part = vmem_call(
+    col_new, row_new, unscaled_part = vmem_call(
         functools.partial(update_kernel, (total_cols, width)),
         (
             sds((6, cols_own), f32),
             sds((6, rows_own), f32),
-            sds((6, rows_own, cols_own), f32),
             sds((6, cols_own), f32),
         ),
         [],
@@ -837,8 +839,10 @@
         [],
         1e9,
         32,
-        unscaled,
         jnp.broadcast_to(step[:, None], (6, cols_own)),
+        col_new,
+        row_new,
+        *grads,
         qkv,
         out_proj,
         mlp,

time: 336 us -> 336 us (level)
    unnamed x112 -> x114, local copies, waits for them, and re-layouts: 15.1 us -> 13.5 us
where the time goes in v5:
time: 336 us; the launch traced here: 332 us
  waiting for transfers between devices  123 us (37%)
  Pallas kernels  80.2 us (24%)
  starting transfers between devices  78 us (23%)
  other arithmetic  28.5 us (8%)
  local copies, waits for them, and re-layouts  20.5 us (6%)
    ppermute x52, waiting for transfers between devices, hop(): return lax.ppermute(value, axis, [(i, i ^ flip) for i in range(peers)])  112 us
    pallas_call x8, Pallas kernels, vmem_call(): pl.pallas_call(body, out_shape=outs, in_specs=[scalars if a.ndim == 1 els...  80.2 us
    ppermute x52, starting transfers between devices, hop(): return lax.ppermute(value, axis, [(i, i ^ flip) for i in range(peers)])  68 us
    unnamed x114, local copies, waits for them, and re-layouts  13.5 us
  transfers between devices with their start and end apart: 56, of which 24 were waited for; matrix products, arithmetic and copies ran while one was open for 9% of the time, Pallas kernels for 20%

profile of v5, /device:TPU:0, one launch (start us, length us, event | category | flops | bytes accessed | tf_op | source)
XLA Modules:
  0.0 332.0 jit_solution(8019240264744081241)
XLA Ops:
  2.1 3.0 collective-permute-start.6
  5.6 2.7 collective-permute-start.4
  8.3 1.5 collective-permute-start.13
  11.0 3.3 collective-permute-start
  14.3 1.7 collective-permute-start.12
  16.1 6.7 %collective-permute-done.4 = bf16[160,1024]{1,0:T(8,128)(2,1)S(1)} collective-permute-done((bf16[160,1024]{1,0:T(8,128)(2,1)S(1)}, bf16[160,1024]{1,0:T(8,128)(2,1)S(1)}, u32[]{:S(2)}, u32[]{:S(2)}) %collective-permute-start.4) | collective-permute-done | bytes 327712 | tf_op jit(solution)/shard_map/ppermute | solution.py:56
  23.0 4.1 %collective-permute-start.5 = (bf16[2,160,1024]{2,1,0:T(8,128)(2,1)S(1)}, bf16[2,160,1024]{2,1,0:T(8,128)(2,1)}, u32[]{:S(2)}, u32[]{:S(2)}) collective-permute-start(bf16[2,160,1024]{2,1,0:T(8,128)(2,1)S(1)} %pad_maximum_fusion.1), channel_id=1, source_target_pairs={{0,8},{4,12},{8,0},{12,4},{16,24},{20,28},{24,16},{28,20},{1,9},{5... | collective-permute-start | bytes 1966088 | tf_op jit(solution)/shard_map/ppermute | solution.py:56
  27.7 11.8 %collective-permute-done.14 = bf16[160,1024]{1,0:T(8,128)(2,1)} collective-permute-done((bf16[160,1024]{1,0:T(8,128)(2,1)S(1)}, bf16[160,1024]{1,0:T(8,128)(2,1)}, u32[]{:S(2)}, u32[]{:S(2)}) %collective-permute-start.14) | collective-permute-done | bytes 327712 | tf_op jit(solution)/shard_map/ppermute | solution.py:56
  40.0 1.5 collective-permute-start.1
  43.3 3.5 %collective-permute-done.5.refs_8_ = bf16[2,160,1024]{2,1,0:T(8,128)(2,1)} collective-permute-done((bf16[2,160,1024]{2,1,0:T(8,128)(2,1)S(1)}, bf16[2,160,1024]{2,1,0:T(8,128)(2,1)}, u32[]{:S(2)}, u32[]{:S(2)}) %collective-permute-start.5) | collective-permute-done | bytes 655392 | tf_op jit(solution)/shard_map/ppermute | solution.py:56
  46.8 8.7 %collective-permute-start.16 = (bf16[320,1024]{1,0:T(8,128)(2,1)}, bf16[320,1024]{1,0:T(8,128)(2,1)}, u32[]{:S(2)}, u32[]{:S(2)}) collective-permute-start(bf16[320,1024]{1,0:T(8,128)(2,1)} %get-tuple-element.84), channel_id=1, source_target_pairs={{0,8},{4,12},{8,0},{12,4},{16,24},{20,28},{24,16},{28,20},{1,9},{5... | collective-permute-start | bytes 1966088 | tf_op jit(solution)/shard_map/ppermute | solution.py:56
  61.2 8.9 %collective-permute-done.16 = bf16[320,1024]{1,0:T(8,128)(2,1)} collective-permute-done((bf16[320,1024]{1,0:T(8,128)(2,1)}, bf16[320,1024]{1,0:T(8,128)(2,1)}, u32[]{:S(2)}, u32[]{:S(2)}) %collective-permute-start.16) | collective-permute-done | bytes 655392 | tf_op jit(solution)/shard_map/ppermute | solution.py:56
  70.2 4.5 %collective-permute-done.17 = bf16[320,1024]{1,0:T(8,128)(2,1)S(1)} collective-permute-done((bf16[320,1024]{1,0:T(8,128)(2,1)}, bf16[320,1024]{1,0:T(8,128)(2,1)S(1)}, u32[]{:S(2)}, u32[]{:S(2)}) %collective-permute-start.17) | collective-permute-done | bytes 655392 | tf_op jit(solution)/shard_map/ppermute | solution.py:56
  75.2 11.7 %collective-permute-start.18 = (bf16[320,1024]{1,0:T(8,128)(2,1)}, bf16[320,1024]{1,0:T(8,128)(2,1)S(1)}, u32[]{:S(2)}, u32[]{:S(2)}) collective-permute-start(bf16[320,1024]{1,0:T(8,128)(2,1)} %get-tuple-element.86), channel_id=1, source_target_pairs={{0,8},{4,12},{8,0},{12,4},{16,24},{20,28},{24,16},{28,20},{1,9},{5... | collective-permute-start | bytes 1966088 | tf_op jit(solution)/shard_map/ppermute | solution.py:56
  90.9 8.9 %collective-permute-done.18 = bf16[320,1024]{1,0:T(8,128)(2,1)S(1)} collective-permute-done((bf16[320,1024]{1,0:T(8,128)(2,1)}, bf16[320,1024]{1,0:T(8,128)(2,1)S(1)}, u32[]{:S(2)}, u32[]{:S(2)}) %collective-permute-start.18) | collective-permute-done | bytes 655392 | tf_op jit(solution)/shard_map/ppermute | solution.py:56
  100.3 1.6 pad_maximum_fusion.refs_4_
  102.0 2.5 collective-permute-done.8.refs_11_
  104.5 19.8 %shard_map.251 = (bf16[2048,1280]{1,0:T(8,128)(2,1)}, bf16[1024,320]{1,0:T(8,128)(2,1)}, bf16[2048,320]{1,0:T(8,128)(2,1)}, bf16[2048,320]{1,0:T(8,128)(2,1)}, b...) custom-call(s32[13]{0:T(128)} %stack.92.refs_0_, ...), custom_call_target="tpu_custom_call" | custom-call | flops 80530636800 | bytes 19687732 | tf_op jit(solution)/shard_map/pallas_call | solution.py:40
  128.6 3.8 %collective-permute-done.10.refs_2_.refs_1_ = bf16[256,320]{1,0:T(8,128)(2,1)S(1)} collective-permute-done((bf16[256,320]{1,0:T(8,128)(2,1)}, bf16[256,320]{1,0:T(8,128)(2,1)S(1)}, u32[]{:S(2)}, u32[]{:S(2)}) %collective-permute-start.10) | collective-permute-done | bytes 163872 | tf_op jit(solution)/shard_map/ppermute | solution.py:56
  132.5 1.5 collective-permute-done.11.refs_3_
  135.2 1.6 collective-permute-done.25.refs_12_
  137.8 12.6 %shard_map.252 = (f32[256,1280]{1,0:T(8,128)}, f32[256,1280]{1,0:T(8,128)}, f32[1,1280]{1,0:T(1,128)S(1)}, bf16[2,256,1280]{2,1,0:T(8,128)(2,1)}, bf16[2,256,640...) custom-call(s32[4]{0:T(128)S(1)} %pad_add_fusion.at_ref, ...), custom_call_target="tpu_custom_call" | custom-call | flops 40265318400 | bytes 18360336 | tf_op jit(solution)/shard_map/pallas_call | solution.py:40
  155.5 1.4 collective-permute-done.33.refs_8_
  163.6 6.2 %shard_map.253 = (bf16[1280,512]{1,0:T(8,128)(2,1)S(1)}, bf16[1280,512]{1,0:T(8,128)(2,1)S(1)}, bf16[2,2,320,512]{3,2,1,0:T(8,128)(2,1)S(1)}, bf16[2,2,320,512]{3,2,1,0:T(8,128)(2,1)S(1)}) custom-call(s32[1]{0:T(128)} %bitcast.27.at_ref, bf16[256,320]{1,0:T(8,128)(2,1)S(1)} %copy-done.23, bf16[256,320]{1,0:T(8,128)(2,1)S(1)} %collective-permute-done.10.refs_2_.refs_1_, ...), custom_call_target="tpu_custom_call" | custom-call | flops 20132659200 | bytes 11141124 | tf_op jit(solution)/shard_map/pallas_call | solution.py:40
  172.6 29.3 %shard_map.254 = (bf16[1024,320]{1,0:T(8,128)(2,1)}, bf16[2048,640]{1,0:T(8,128)(2,1)}, f32[1,320]{1,0:T(1,128)}, bf16[4,160,1024]{2,1,0:T(8,128)(2,1)}, bf16[4,160,1024]{2,1,0:T(8,128)(2,1)}) custom-call(s32[5]{0:T(128)} %stack.100.at_ref, bf16[256,320]{1,0:T(8,128)(2,1)} %copy-done.24, bf16[256,320]{1,0:T(8,128)(2,1)} %collective-permute-done.27.refs_1_, ...), custom_call_target="tpu_custom_call" | custom-call | flops 134217728000 | bytes 15096340 | tf_op jit(solution)/shard_map/pallas_call | solution.py:40
  202.9 1.7 convert_add_fusion.2
  206.1 1.9 convert_add_fusion.1
  209.8 8.5 %shard_map.255 = (bf16[2,256,2560]{2,1,0:T(8,128)(2,1)S(1)}, bf16[2,256,2560]{2,1,0:T(8,128)(2,1)}) custom-call(s32[4]{0:T(128)S(1)} %pad_add_fusion.1.at_ref, bf16[1024,320]{1,0:T(8,128)(2,1)S(1)} %copy-done.21, bf16[2048,640]{1,0:T(8,128)(2,1)S(1)} %copy-done.18, bf16[1280,1024]{1,0:T(8,128)(2,1)} %get-tuple-element.113.w_ref), custom_call_target="tpu_custom_call" | custom-call | flops 33554432000 | bytes 11141136 | tf_op jit(solution)/shard_map/pallas_call | solution.py:40
  218.2 14.8 %collective-permute-done.34 = bf16[4,160,1024]{2,1,0:T(8,128)(2,1)} collective-permute-done((bf16[4,160,1024]{2,1,0:T(8,128)(2,1)}, bf16[4,160,1024]{2,1,0:T(8,128)(2,1)}, u32[]{:S(2)}, u32[]{:S(2)}) %collective-permute-start.34) | collective-permute-done | bytes 1310752 | tf_op jit(solution)/shard_map/ppermute | solution.py:56
  234.9 2.4 convert_add_fusion
  240.0 3.4 %collective-permute-start.47 = (bf16[2,160,512]{2,1,0:T(8,128)(2,1)S(1)}, bf16[2,160,512]{2,1,0:T(8,128)(2,1)S(1)}, u32[]{:S(2)}, u32[]{:S(2)}) collective-permute-start(bf16[2,160,512]{2,1,0:T(8,128)(2,1)S(1)} %fusion.18), channel_id=1, source_target_pairs={{0,16},{4,20},{8,24},{12,28},{16,0},{20,4},{24,8},{28,12},{1,17},{... | collective-permute-start | bytes 983048 | tf_op jit(solution)/shard_map/ppermute | solution.py:56
  243.4 18.3 %collective-permute-done.44 = bf16[2,160,1024]{2,1,0:T(8,128)(2,1)S(1)} collective-permute-done((bf16[2,160,1024]{2,1,0:T(8,128)(2,1)S(1)}, bf16[2,160,1024]{2,1,0:T(8,128)(2,1)S(1)}, u32[]{:S(2)}, u32[]{:S(2)}) %collective-permute-start.44) | collective-permute-done | bytes 655392 | tf_op jit(solution)/shard_map/ppermute | solution.py:56
  262.0 1.8 collective-permute-start.45
  264.0 2.3 fusion.9
  266.4 1.3 collective-permute-start.40
  269.7 12.9 %collective-permute-done.40 = bf16[256,1280]{1,0:T(8,128)(2,1)S(1)} collective-permute-done((bf16[256,1280]{1,0:T(8,128)(2,1)S(1)}, bf16[256,1280]{1,0:T(8,128)(2,1)S(1)}, u32[]{:S(2)}, u32[]{:S(2)}) %collective-permute-start.40) | collective-permute-done | bytes 655392 | tf_op jit(solution)/shard_map/ppermute | solution.py:56
  286.5 1.4 collective-permute-start.43
  287.9 3.9 %collective-permute-done.42 = bf16[256,256]{1,0:T(8,128)(2,1)S(1)} collective-permute-done((bf16[256,256]{1,0:T(8,128)(2,1)S(1)}, bf16[256,256]{1,0:T(8,128)(2,1)S(1)}, u32[]{:S(2)}, u32[]{:S(2)}) %collective-permute-start.42) | collective-permute-done | bytes 131104 | tf_op jit(solution)/shard_map/ppermute | solution.py:770
  291.8 5.9 %collective-permute-done.41 = bf16[256,1280]{1,0:T(8,128)(2,1)S(1)} collective-permute-done((bf16[256,1280]{1,0:T(8,128)(2,1)S(1)}, bf16[256,1280]{1,0:T(8,128)(2,1)S(1)}, u32[]{:S(2)}, u32[]{:S(2)}) %collective-permute-start.41) | collective-permute-done | bytes 655392 | tf_op jit(solution)/shard_map/ppermute | solution.py:56
  299.7 2.4 collective-permute-done.43
  303.0 2.3 collective-permute-start.51
  305.3 1.3 collective-permute-start.54
  306.9 1.7 collective-permute-start.52
  309.0 2.5 collective-permute-done.52
  313.5 4.0 %all-to-all-start = ((f32[32,8,128]{2,1,0:T(8,128)}), f32[32,8,128]{2,1,0:T(8,128)}, u32[]{:S(2)}, u32[]{:S(2)}) async-start(f32[32,8,128]{2,1,0:T(8,128)} %bitcast.51), calls=%async_computation | async-start | bytes 262144 | tf_op jit(solution)/shard_map/all_to_all | solution.py:829
  317.6 3.7 %fusion.6 = f32[256,1280]{1,0:T(8,128)} fusion(f32[256,1280]{1,0:T(8,128)} %get-tuple-element.95, bf16[256,1280]{1,0:T(8,128)(2,1)S(1)} %get-tuple-element.147.refs_14_, f32[256]{0:T(256)S(1)} %broadcast_multiply_fusion, f32[1280]{0:T(1024)S(1)} %copy-done.42, f32[256]{0:T(256)S(1)} %copy-done.44, bf16[256,1024]{1,0:T(8,128)(2,1)} %copy-done.32, ...), kind=kLoop, calls=%fused_computation.14 | loop fusion | flops 4587520 | bytes 5905408 | tf_op jit(solution)/shard_map/add | solution.py:778
  321.4 4.4 %all-to-all-done = f32[32,8,128]{2,1,0:T(8,128)} async-done(((f32[32,8,128]{2,1,0:T(8,128)}), f32[32,8,128]{2,1,0:T(8,128)}, u32[]{:S(2)}, u32[]{:S(2)}) %all-to-all-start) | async-done | bytes 131104 | tf_op jit(solution)/shard_map/all_to_all | solution.py:829
  329.0 1.5 shard_map.258
  (278 shorter events, 62.9 us)
Async XLA Ops:
  2.1 12.2 %collective-permute-start.6 = (bf16[1,160,1024]{2,1,0:T(8,128)(2,1)S(1)}, bf16[1,160,1024]{2,1,0:T(8,128)(2,1)}, u32[]{:S(2)}, u32[]{:S(2)}) collective-permute-start(bf16[1,160,1024]{2,1,0:T(8,128)(2,1)S(1)} %pad_maximum_fusion.5.refs_6_), channel_id=1, source_target_pairs={{0,4},{4,0},{8,12},{12,8},{16,20},{20,16},{24,28},{28,24},{1,5},{5... | collective-permute-start | bytes 983048 | tf_op jit(solution)/shard_map/ppermute | solution.py:56
  5.6 17.2 %collective-permute-start.4 = (bf16[160,1024]{1,0:T(8,128)(2,1)S(1)}, bf16[160,1024]{1,0:T(8,128)(2,1)S(1)}, u32[]{:S(2)}, u32[]{:S(2)}) collective-permute-start(bf16[160,1024]{1,0:T(8,128)(2,1)S(1)} %get-tuple-element.171), channel_id=1, source_target_pairs={{0,16},{4,20},{8,24},{12,28},{16,0},{20,4},{24,8},{28,12},{1,17},{... | collective-permute-start | bytes 983048 | tf_op jit(solution)/shard_map/ppermute | solution.py:56
  8.3 14.5 %collective-permute-start.13 = (bf16[160,1024]{1,0:T(8,128)(2,1)S(1)}, bf16[160,1024]{1,0:T(8,128)(2,1)S(1)}, u32[]{:S(2)}, u32[]{:S(2)}) collective-permute-start(bf16[160,1024]{1,0:T(8,128)(2,1)S(1)} %get-tuple-element.81), channel_id=1, source_target_pairs={{0,2},{1,3},{2,0},{3,1},{4,6},{5,7},{6,4},{7,5},{8,10},{9,11},{10,... | collective-permute-start | bytes 983048 | tf_op jit(solution)/shard_map/ppermute | solution.py:56
  11.0 29.0 %collective-permute-start = (bf16[256,1280]{1,0:T(8,128)(2,1)S(1)}, bf16[256,1280]{1,0:T(8,128)(2,1)}, u32[]{:S(2)}, u32[]{:S(2)}) collective-permute-start(bf16[256,1280]{1,0:T(8,128)(2,1)S(1)} %get-tuple-element.147.refs_14_), channel_id=1, source_target_pairs={{0,4},{4,8},{8,12},{12,16},{16,20},{20,24},{24,28},{1,5},{5,9},{9,... | collective-permute-start | bytes 1966088 | tf_op jit(solution)/shard_map/ppermute | solution.py:529
  14.3 27.2 %collective-permute-start.12 = (bf16[160,1024]{1,0:T(8,128)(2,1)S(1)}, bf16[160,1024]{1,0:T(8,128)(2,1)S(1)}, u32[]{:S(2)}, u32[]{:S(2)}) collective-permute-start(bf16[160,1024]{1,0:T(8,128)(2,1)S(1)} %get-tuple-element.81), channel_id=1, source_target_pairs={{0,4},{4,0},{8,12},{12,8},{16,20},{20,16},{24,28},{28,24},{1,5},{5... | collective-permute-start | bytes 983048 | tf_op jit(solution)/shard_map/ppermute | solution.py:56
  22.8 16.8 %collective-permute-start.14 = (bf16[160,1024]{1,0:T(8,128)(2,1)S(1)}, bf16[160,1024]{1,0:T(8,128)(2,1)}, u32[]{:S(2)}, u32[]{:S(2)}) collective-permute-start(bf16[160,1024]{1,0:T(8,128)(2,1)S(1)} %get-tuple-element.81), channel_id=1, source_target_pairs={{0,16},{4,20},{8,24},{12,28},{16,0},{20,4},{24,8},{28,12},{1,17},{... | collective-permute-start | bytes 983048 | tf_op jit(solution)/shard_map/ppermute | solution.py:56
  23.0 23.8 %collective-permute-start.5 = (bf16[2,160,1024]{2,1,0:T(8,128)(2,1)S(1)}, bf16[2,160,1024]{2,1,0:T(8,128)(2,1)}, u32[]{:S(2)}, u32[]{:S(2)}) collective-permute-start(bf16[2,160,1024]{2,1,0:T(8,128)(2,1)S(1)} %pad_maximum_fusion.1), channel_id=1, source_target_pairs={{0,8},{4,12},{8,0},{12,4},{16,24},{20,28},{24,16},{28,20},{1,9},{5... | collective-permute-start | bytes 1966088 | tf_op jit(solution)/shard_map/ppermute | solution.py:56
  27.1 16.2 %collective-permute-start.7 = (bf16[1,160,1024]{2,1,0:T(8,128)(2,1)S(1)}, bf16[1,160,1024]{2,1,0:T(8,128)(2,1)S(1)}, u32[]{:S(2)}, u32[]{:S(2)}) collective-permute-start(bf16[1,160,1024]{2,1,0:T(8,128)(2,1)S(1)} %bitcast.101), channel_id=1, source_target_pairs={{0,4},{4,0},{8,12},{12,8},{16,20},{20,16},{24,28},{28,24},{1,5},{5... | collective-permute-start | bytes 983048 | tf_op jit(solution)/shard_map/ppermute | solution.py:56
  39.5 16.0 %collective-permute-start.15 = (bf16[160,1024]{1,0:T(8,128)(2,1)}, bf16[160,1024]{1,0:T(8,128)(2,1)S(1)}, u32[]{:S(2)}, u32[]{:S(2)}) collective-permute-start(bf16[160,1024]{1,0:T(8,128)(2,1)} %collective-permute-done.14), channel_id=1, source_target_pairs={{0,4},{4,0},{8,12},{12,8},{16,20},{20,16},{24,28},{28,24},{1,5},{5... | collective-permute-start | bytes 983048 | tf_op jit(solution)/shard_map/ppermute | solution.py:56
  40.0 17.8 %collective-permute-start.1 = (bf16[256,1280]{1,0:T(8,128)(2,1)}, bf16[256,1280]{1,0:T(8,128)(2,1)S(1)}, u32[]{:S(2)}, u32[]{:S(2)}) collective-permute-start(bf16[256,1280]{1,0:T(8,128)(2,1)} %collective-permute-done.refs_2_), channel_id=1, source_target_pairs={{0,2},{1,3},{2,0},{3,1},{4,6},{5,7},{6,4},{7,5},{8,10},{9,11},{10,... | collective-permute-start | bytes 1966088 | tf_op jit(solution)/shard_map/ppermute | solution.py:56
  46.8 23.3 %collective-permute-start.16 = (bf16[320,1024]{1,0:T(8,128)(2,1)}, bf16[320,1024]{1,0:T(8,128)(2,1)}, u32[]{:S(2)}, u32[]{:S(2)}) collective-permute-start(bf16[320,1024]{1,0:T(8,128)(2,1)} %get-tuple-element.84), channel_id=1, source_target_pairs={{0,8},{4,12},{8,0},{12,4},{16,24},{20,28},{24,16},{28,20},{1,9},{5... | collective-permute-start | bytes 1966088 | tf_op jit(solution)/shard_map/ppermute | solution.py:56
  58.6 16.0 %collective-permute-start.17 = (bf16[320,1024]{1,0:T(8,128)(2,1)}, bf16[320,1024]{1,0:T(8,128)(2,1)S(1)}, u32[]{:S(2)}, u32[]{:S(2)}) collective-permute-start(bf16[320,1024]{1,0:T(8,128)(2,1)} %get-tuple-element.86), channel_id=1, source_target_pairs={{0,2},{1,3},{2,0},{3,1},{4,6},{5,7},{6,4},{7,5},{8,10},{9,11},{10,... | collective-permute-start | bytes 1966088 | tf_op jit(solution)/shard_map/ppermute | solution.py:56
  74.6 15.7 %collective-permute-start.21 = (bf16[320,1024]{1,0:T(8,128)(2,1)}, bf16[320,1024]{1,0:T(8,128)(2,1)S(1)}, u32[]{:S(2)}, u32[]{:S(2)}) collective-permute-start(bf16[320,1024]{1,0:T(8,128)(2,1)} %collective-permute-done.16), channel_id=1, source_target_pairs={{0,2},{1,3},{2,0},{3,1},{4,6},{5,7},{6,4},{7,5},{8,10},{9,11},{10,... | collective-permute-start | bytes 1966088 | tf_op jit(solution)/shard_map/ppermute | solution.py:56
  75.2 24.6 %collective-permute-start.18 = (bf16[320,1024]{1,0:T(8,128)(2,1)}, bf16[320,1024]{1,0:T(8,128)(2,1)S(1)}, u32[]{:S(2)}, u32[]{:S(2)}) collective-permute-start(bf16[320,1024]{1,0:T(8,128)(2,1)} %get-tuple-element.86), channel_id=1, source_target_pairs={{0,8},{4,12},{8,0},{12,4},{16,24},{20,28},{24,16},{28,20},{1,9},{5... | collective-permute-start | bytes 1966088 | tf_op jit(solution)/shard_map/ppermute | solution.py:56
  87.0 14.9 %collective-permute-start.2 = (bf16[256,1280]{1,0:T(8,128)(2,1)}, bf16[256,1280]{1,0:T(8,128)(2,1)}, u32[]{:S(2)}, u32[]{:S(2)}) collective-permute-start(bf16[256,1280]{1,0:T(8,128)(2,1)} %collective-permute-done.refs_2_), channel_id=1, source_target_pairs={{0,1},{1,0},{2,3},{3,2},{4,5},{5,4},{6,7},{7,6},{8,9},{9,8},{10,11... | collective-permute-start | bytes 1966088 | tf_op jit(solution)/shard_map/ppermute | solution.py:56
  87.1 17.5 %collective-permute-start.8 = (bf16[2,160,1024]{2,1,0:T(8,128)(2,1)}, bf16[2,160,1024]{2,1,0:T(8,128)(2,1)}, u32[]{:S(2)}, u32[]{:S(2)}) collective-permute-start(bf16[2,160,1024]{2,1,0:T(8,128)(2,1)} %collective-permute-done.5.refs_8_), channel_id=1, source_target_pairs={{0,4},{4,0},{8,12},{12,8},{16,20},{20,16},{24,28},{28,24},{1,5},{5... | collective-permute-start | bytes 1966088 | tf_op jit(solution)/shard_map/ppermute | solution.py:56
  87.7 16.8 %collective-permute-start.3 = (bf16[256,1280]{1,0:T(8,128)(2,1)}, bf16[256,1280]{1,0:T(8,128)(2,1)}, u32[]{:S(2)}, u32[]{:S(2)}) collective-permute-start(bf16[256,1280]{1,0:T(8,128)(2,1)} %copy-done.53), channel_id=1, source_target_pairs={{0,1},{1,0},{2,3},{3,2},{4,5},{5,4},{6,7},{7,6},{8,9},{9,8},{10,11... | collective-permute-start | bytes 1966088 | tf_op jit(solution)/shard_map/ppermute | solution.py:56
  90.4 35.1 %collective-permute-start.20 = (bf16[160,1024]{1,0:T(8,128)(2,1)}, bf16[160,1024]{1,0:T(8,128)(2,1)S(1)}, u32[]{:S(2)}, u32[]{:S(2)}) collective-permute-start(bf16[160,1024]{1,0:T(8,128)(2,1)} %copy-done.40), channel_id=1, source_target_pairs={{0,2},{1,3},{2,0},{3,1},{4,6},{5,7},{6,4},{7,5},{8,10},{9,11},{10,... | collective-permute-start | bytes 983048 | tf_op jit(solution)/shard_map/ppermute | solution.py:56
  99.7 28.7 %collective-permute-start.22 = (bf16[320,1024]{1,0:T(8,128)(2,1)S(1)}, bf16[320,1024]{1,0:T(8,128)(2,1)S(1)}, u32[]{:S(2)}, u32[]{:S(2)}) collective-permute-start(bf16[320,1024]{1,0:T(8,128)(2,1)S(1)} %collective-permute-done.18), channel_id=1, source_target_pairs={{0,2},{1,3},{2,0},{3,1},{4,6},{5,7},{6,4},{7,5},{8,10},{9,11},{10,... | collective-permute-start | bytes 1966088 | tf_op jit(solution)/shard_map/ppermute | solution.py:56
  101.9 35.9 %collective-permute-start.19 = (bf16[4,320,1024]{2,1,0:T(8,128)(2,1)S(1)}, bf16[4,320,1024]{2,1,0:T(8,128)(2,1)}, u32[]{:S(2)}, u32[]{:S(2)}) collective-permute-start(bf16[4,320,1024]{2,1,0:T(8,128)(2,1)S(1)} %pad_maximum_fusion.refs_4_), channel_id=1, source_target_pairs={{0,1},{1,0},{2,3},{3,2},{4,5},{5,4},{6,7},{7,6},{8,9},{9,8},{10,11... | collective-permute-start | bytes 7864328 | tf_op jit(solution)/shard_map/ppermute | solution.py:56
  124.4 8.1 %collective-permute-start.10 = (bf16[256,320]{1,0:T(8,128)(2,1)}, bf16[256,320]{1,0:T(8,128)(2,1)S(1)}, u32[]{:S(2)}, u32[]{:S(2)}) collective-permute-start(bf16[256,320]{1,0:T(8,128)(2,1)} %get-tuple-element.79), channel_id=1, source_target_pairs={{0,2},{1,3},{2,0},{3,1},{4,6},{5,7},{6,4},{7,5},{8,10},{9,11},{10,... | collective-permute-start | bytes 491528 | tf_op jit(solution)/shard_map/ppermute | solution.py:56
  125.0 9.0 %collective-permute-start.11 = (bf16[256,320]{1,0:T(8,128)(2,1)}, bf16[256,320]{1,0:T(8,128)(2,1)S(1)}, u32[]{:S(2)}, u32[]{:S(2)}) collective-permute-start(bf16[256,320]{1,0:T(8,128)(2,1)} %get-tuple-element.80), channel_id=1, source_target_pairs={{0,3},{1,2},{2,1},{3,0},{4,7},{5,6},{6,5},{7,4},{8,11},{9,10},{10,... | collective-permute-start | bytes 491528 | tf_op jit(solution)/shard_map/ppermute | solution.py:56
  126.2 9.0 %collective-permute-start.9 = (bf16[256,320]{1,0:T(8,128)(2,1)}, bf16[256,320]{1,0:T(8,128)(2,1)S(1)}, u32[]{:S(2)}, u32[]{:S(2)}) collective-permute-start(bf16[256,320]{1,0:T(8,128)(2,1)} %get-tuple-element.78), channel_id=1, source_target_pairs={{0,1},{1,0},{2,3},{3,2},{4,5},{5,4},{6,7},{7,6},{8,9},{9,8},{10,11... | collective-permute-start | bytes 491528 | tf_op jit(solution)/shard_map/ppermute | solution.py:56
  128.5 6.7 %collective-permute-start.24 = (bf16[1,320,1024]{2,1,0:T(8,128)(2,1)S(1)}, bf16[1,320,1024]{2,1,0:T(8,128)(2,1)S(1)}, u32[]{:S(2)}, u32[]{:S(2)}) collective-permute-start(bf16[1,320,1024]{2,1,0:T(8,128)(2,1)S(1)} %bitcast.84), channel_id=1, source_target_pairs={{0,1},{1,0},{2,3},{3,2},{4,5},{5,4},{6,7},{7,6},{8,9},{9,8},{10,11... | collective-permute-start | bytes 1966088 | tf_op jit(solution)/shard_map/ppermute | solution.py:56
  152.0 7.2 %collective-permute-start.31 = (bf16[2,256,1280]{2,1,0:T(8,128)(2,1)}, bf16[2,256,1280]{2,1,0:T(8,128)(2,1)}, u32[]{:S(2)}, u32[]{:S(2)}) collective-permute-start(bf16[2,256,1280]{2,1,0:T(8,128)(2,1)} %get-tuple-element.103.refs_3_), channel_id=1, source_target_pairs={{0,1},{1,0},{2,3},{3,2},{4,5},{5,4},{6,7},{7,6},{8,9},{9,8},{10,11... | collective-permute-start | bytes 3932168 | tf_op jit(solution)/shard_map/ppermute | solution.py:56
  152.5 5.9 %collective-permute-start.32 = (bf16[2,256,640]{2,1,0:T(8,128)(2,1)}, bf16[2,256,640]{2,1,0:T(8,128)(2,1)S(1)}, u32[]{:S(2)}, u32[]{:S(2)}) collective-permute-start(bf16[2,256,640]{2,1,0:T(8,128)(2,1)} %get-tuple-element.105), channel_id=1, source_target_pairs={{0,1},{1,0},{2,3},{3,2},{4,5},{5,4},{6,7},{7,6},{8,9},{9,8},{10,11... | collective-permute-start | bytes 1966088 | tf_op jit(solution)/shard_map/ppermute | solution.py:56
  155.1 16.8 %collective-permute-start.27 = (bf16[256,320]{1,0:T(8,128)(2,1)}, bf16[256,320]{1,0:T(8,128)(2,1)}, u32[]{:S(2)}, u32[]{:S(2)}) collective-permute-start(bf16[256,320]{1,0:T(8,128)(2,1)} %get-tuple-element.97), channel_id=1, source_target_pairs={{0,1},{1,0},{2,3},{3,2},{4,5},{5,4},{6,7},{7,6},{8,9},{9,8},{10,11... | collective-permute-start | bytes 491528 | tf_op jit(solution)/shard_map/ppermute | solution.py:56
  156.9 15.0 %collective-permute-start.28 = (bf16[256,320]{1,0:T(8,128)(2,1)}, bf16[256,320]{1,0:T(8,128)(2,1)}, u32[]{:S(2)}, u32[]{:S(2)}) collective-permute-start(bf16[256,320]{1,0:T(8,128)(2,1)} %get-tuple-element.98), channel_id=1, source_target_pairs={{0,2},{1,3},{2,0},{3,1},{4,6},{5,7},{6,4},{7,5},{8,10},{9,11},{10,... | collective-permute-start | bytes 491528 | tf_op jit(solution)/shard_map/ppermute | solution.py:56
  157.6 14.3 %collective-permute-start.29 = (bf16[256,320]{1,0:T(8,128)(2,1)}, bf16[256,320]{1,0:T(8,128)(2,1)S(1)}, u32[]{:S(2)}, u32[]{:S(2)}) collective-permute-start(bf16[256,320]{1,0:T(8,128)(2,1)} %get-tuple-element.99), channel_id=1, source_target_pairs={{0,3},{1,2},{2,1},{3,0},{4,7},{5,6},{6,5},{7,4},{8,11},{9,10},{10,... | collective-permute-start | bytes 491528 | tf_op jit(solution)/shard_map/ppermute | solution.py:56
  169.8 33.1 %collective-permute-start.35 = (bf16[1280,512]{1,0:T(8,128)(2,1)S(1)}, bf16[1280,512]{1,0:T(8,128)(2,1)}, u32[]{:S(2)}, u32[]{:S(2)}) collective-permute-start(bf16[1280,512]{1,0:T(8,128)(2,1)S(1)} %get-tuple-element.107), channel_id=1, source_target_pairs={{0,2},{1,3},{2,0},{3,1},{4,6},{5,7},{6,4},{7,5},{8,10},{9,11},{10,... | collective-permute-start | bytes 3932168 | tf_op jit(solution)/shard_map/ppermute | solution.py:56
  171.1 34.6 %collective-permute-start.37 = (bf16[2,2,320,512]{3,2,1,0:T(8,128)(2,1)S(1)}, bf16[2,2,320,512]{3,2,1,0:T(8,128)(2,1)}, u32[]{:S(2)}, u32[]{:S(2)}) collective-permute-start(bf16[2,2,320,512]{3,2,1,0:T(8,128)(2,1)S(1)} %get-tuple-element.108), channel_id=1, source_target_pairs={{0,8},{4,12},{8,0},{12,4},{16,24},{20,28},{24,16},{28,20},{1,9},{5... | collective-permute-start | bytes 3932168 | tf_op jit(solution)/shard_map/ppermute | solution.py:56
  201.9 31.0 %collective-permute-start.34 = (bf16[4,160,1024]{2,1,0:T(8,128)(2,1)}, bf16[4,160,1024]{2,1,0:T(8,128)(2,1)}, u32[]{:S(2)}, u32[]{:S(2)}) collective-permute-start(bf16[4,160,1024]{2,1,0:T(8,128)(2,1)} %get-tuple-element.116), channel_id=1, source_target_pairs={{0,4},{4,0},{8,12},{12,8},{16,20},{20,16},{24,28},{28,24},{1,5},{5... | collective-permute-start | bytes 3932168 | tf_op jit(solution)/shard_map/ppermute | solution.py:56
  204.7 28.2 %collective-permute-start.36 = (bf16[2,2,160,512]{3,2,0,1:T(8,128)(2,1)S(1)}, bf16[2,2,160,512]{3,2,0,1:T(8,128)(2,1)S(1)}, u32[]{:S(2)}, u32[]{:S(2)}) collective-permute-start(bf16[2,2,160,512]{3,2,0,1:T(8,128)(2,1)S(1)} %fusion.13), channel_id=1, source_target_pairs={{0,8},{4,12},{8,0},{12,4},{16,24},{20,28},{24,16},{28,20},{1,9},{5... | collective-permute-start | bytes 1966088 | tf_op jit(solution)/shard_map/ppermute | solution.py:56
  208.1 24.9 %collective-permute-start.38 = (bf16[2,320,512]{2,1,0:T(8,128)(2,1)S(1)}, bf16[2,320,512]{2,1,0:T(8,128)(2,1)S(1)}, u32[]{:S(2)}, u32[]{:S(2)}) collective-permute-start(bf16[2,320,512]{2,1,0:T(8,128)(2,1)S(1)} %fusion.15), channel_id=1, source_target_pairs={{0,2},{1,3},{2,0},{3,1},{4,6},{5,7},{6,4},{7,5},{8,10},{9,11},{10,... | collective-permute-start | bytes 1966088 | tf_op jit(solution)/shard_map/ppermute | solution.py:56
  234.6 29.4 %collective-permute-start.39 = (bf16[2,256,2560]{2,1,0:T(8,128)(2,1)}, bf16[2,256,2560]{2,1,0:T(8,128)(2,1)}, u32[]{:S(2)}, u32[]{:S(2)}) collective-permute-start(bf16[2,256,2560]{2,1,0:T(8,128)(2,1)} %get-tuple-element.118), channel_id=1, source_target_pairs={{0,1},{1,0},{2,3},{3,2},{4,5},{5,4},{6,7},{7,6},{8,9},{9,8},{10,11... | collective-permute-start | bytes 7864328 | tf_op jit(solution)/shard_map/ppermute | solution.py:56
  237.5 24.2 %collective-permute-start.44 = (bf16[2,160,1024]{2,1,0:T(8,128)(2,1)S(1)}, bf16[2,160,1024]{2,1,0:T(8,128)(2,1)S(1)}, u32[]{:S(2)}, u32[]{:S(2)}) collective-permute-start(bf16[2,160,1024]{2,1,0:T(8,128)(2,1)S(1)} %fusion.14), channel_id=1, source_target_pairs={{0,8},{4,12},{8,0},{12,4},{16,24},{20,28},{24,16},{28,20},{1,9},{5... | collective-permute-start | bytes 1966088 | tf_op jit(solution)/shard_map/ppermute | solution.py:56
  238.7 25.2 %collective-permute-start.46 = (bf16[2,160,512]{2,1,0:T(8,128)(2,1)S(1)}, bf16[2,160,512]{2,1,0:T(8,128)(2,1)S(1)}, u32[]{:S(2)}, u32[]{:S(2)}) collective-permute-start(bf16[2,160,512]{2,1,0:T(8,128)(2,1)S(1)} %fusion.17), channel_id=1, source_target_pairs={{0,4},{4,0},{8,12},{12,8},{16,20},{20,16},{24,28},{28,24},{1,5},{5... | collective-permute-start | bytes 983048 | tf_op jit(solution)/shard_map/ppermute | solution.py:56
  240.0 28.5 %collective-permute-start.47 = (bf16[2,160,512]{2,1,0:T(8,128)(2,1)S(1)}, bf16[2,160,512]{2,1,0:T(8,128)(2,1)S(1)}, u32[]{:S(2)}, u32[]{:S(2)}) collective-permute-start(bf16[2,160,512]{2,1,0:T(8,128)(2,1)S(1)} %fusion.18), channel_id=1, source_target_pairs={{0,16},{4,20},{8,24},{12,28},{16,0},{20,4},{24,8},{28,12},{1,17},{... | collective-permute-start | bytes 983048 | tf_op jit(solution)/shard_map/ppermute | solution.py:56
  262.0 25.9 %collective-permute-start.45 = (bf16[160,1024]{1,0:T(8,128)(2,1)S(1)}, bf16[160,1024]{1,0:T(8,128)(2,1)S(1)}, u32[]{:S(2)}, u32[]{:S(2)}) collective-permute-start(bf16[160,1024]{1,0:T(8,128)(2,1)S(1)} %fusion.16), channel_id=1, source_target_pairs={{0,16},{4,20},{8,24},{12,28},{16,0},{20,4},{24,8},{28,12},{1,17},{... | collective-permute-start | bytes 983048 | tf_op jit(solution)/shard_map/ppermute | solution.py:56
  266.4 16.1 %collective-permute-start.40 = (bf16[256,1280]{1,0:T(8,128)(2,1)S(1)}, bf16[256,1280]{1,0:T(8,128)(2,1)S(1)}, u32[]{:S(2)}, u32[]{:S(2)}) collective-permute-start(bf16[256,1280]{1,0:T(8,128)(2,1)S(1)} %get-tuple-element.151), channel_id=1, source_target_pairs={{0,2},{1,3},{2,0},{3,1},{4,6},{5,7},{6,4},{7,5},{8,10},{9,11},{10,... | collective-permute-start | bytes 1966088 | tf_op jit(solution)/shard_map/ppermute | solution.py:56
  267.8 18.6 %collective-permute-start.48 = (bf16[160,512]{1,0:T(8,128)(2,1)S(1)}, bf16[160,512]{1,0:T(8,128)(2,1)S(1)}, u32[]{:S(2)}, u32[]{:S(2)}) collective-permute-start(bf16[160,512]{1,0:T(8,128)(2,1)S(1)} %fusion.19), channel_id=1, source_target_pairs={{0,16},{4,20},{8,24},{12,28},{16,0},{20,4},{24,8},{28,12},{1,17},{... | collective-permute-start | bytes 491528 | tf_op jit(solution)/shard_map/ppermute | solution.py:56
  268.6 17.7 %collective-permute-start.49 = (bf16[160,512]{1,0:T(8,128)(2,1)S(1)}, bf16[160,512]{1,0:T(8,128)(2,1)S(1)}, u32[]{:S(2)}, u32[]{:S(2)}) collective-permute-start(bf16[160,512]{1,0:T(8,128)(2,1)S(1)} %fusion.20), channel_id=1, source_target_pairs={{0,4},{4,0},{8,12},{12,8},{16,20},{20,16},{24,28},{28,24},{1,5},{5... | collective-permute-start | bytes 491528 | tf_op jit(solution)/shard_map/ppermute | solution.py:56
  282.6 15.2 %collective-permute-start.41 = (bf16[256,1280]{1,0:T(8,128)(2,1)S(1)}, bf16[256,1280]{1,0:T(8,128)(2,1)S(1)}, u32[]{:S(2)}, u32[]{:S(2)}) collective-permute-start(bf16[256,1280]{1,0:T(8,128)(2,1)S(1)} %get-tuple-element.120), channel_id=1, source_target_pairs={{0,2},{1,3},{2,0},{3,1},{4,6},{5,7},{6,4},{7,5},{8,10},{9,11},{10,... | collective-permute-start | bytes 1966088 | tf_op jit(solution)/shard_map/ppermute | solution.py:56
  284.0 7.8 %collective-permute-start.42 = (bf16[256,256]{1,0:T(8,128)(2,1)S(1)}, bf16[256,256]{1,0:T(8,128)(2,1)S(1)}, u32[]{:S(2)}, u32[]{:S(2)}) collective-permute-start(bf16[256,256]{1,0:T(8,128)(2,1)S(1)} %slice.116), channel_id=1, source_target_pairs={{4,0},{8,4},{12,8},{16,12},{20,16},{24,20},{28,24},{5,1},{9,5},{13... | collective-permute-start | bytes 393224 | tf_op jit(solution)/shard_map/ppermute | solution.py:770
  286.5 15.6 %collective-permute-start.43 = (bf16[256,1024]{1,0:T(8,128)(2,1)S(1)}, bf16[256,1024]{1,0:T(8,128)(2,1)S(1)}, u32[]{:S(2)}, u32[]{:S(2)}) collective-permute-start(bf16[256,1024]{1,0:T(8,128)(2,1)S(1)} %slice.117), channel_id=1, source_target_pairs={{4,0},{8,4},{12,8},{16,12},{20,16},{24,20},{28,24},{5,1},{9,5},{13... | collective-permute-start | bytes 1572872 | tf_op jit(solution)/shard_map/ppermute | solution.py:770
  299.1 6.2 %collective-permute-start.53 = (f32[8,160]{1,0:T(8,128)S(1)}, f32[8,160]{1,0:T(8,128)S(1)}, u32[]{:S(2)}, u32[]{:S(2)}) collective-permute-start(f32[8,160]{1,0:T(8,128)S(1)} %get-tuple-element.130), channel_id=1, source_target_pairs={{0,1},{1,0},{2,3},{3,2},{4,5},{5,4},{6,7},{7,6},{8,9},{9,8},{10,11... | collective-permute-start | bytes 15368 | tf_op jit(solution)/shard_map/ppermute | solution.py:56
  306.9 4.6 %collective-permute-start.52 = (f32[8,320]{1,0:T(8,128)S(1)}, f32[8,320]{1,0:T(8,128)S(1)}, u32[]{:S(2)}, u32[]{:S(2)}) collective-permute-start(f32[8,320]{1,0:T(8,128)S(1)} %add.205), channel_id=1, source_target_pairs={{0,16},{4,20},{8,24},{12,28},{16,0},{20,4},{24,8},{28,12},{1,17},{... | collective-permute-start | bytes 30728 | tf_op jit(solution)/shard_map/ppermute | solution.py:56
  313.5 12.2 %all-to-all-start = ((f32[32,8,128]{2,1,0:T(8,128)}), f32[32,8,128]{2,1,0:T(8,128)}, u32[]{:S(2)}, u32[]{:S(2)}) async-start(f32[32,8,128]{2,1,0:T(8,128)} %bitcast.51), calls=%async_computation | async-start | bytes 262144 | tf_op jit(solution)/shard_map/all_to_all | solution.py:829
  (65 other events, 518.0 us)
